TPU v7x, 128 devices: a whole 4x4x4 slice. The times are simulated.
128 devices in a mesh: row: 32 (over x, z, core), col: 4 (over y).
Axes of the slice: x: 4, y: 4, z: 4, core: 2. Of those that a mesh axis runs over, the one named last changes fastest.
Arguments:
- base_weight: bfloat16 [28672, 8192], P('row', 'col'), may hold values from -6 to 6
- stacked_down_matrices: bfloat16 [4096, 8192], P('row', 'col'), may hold values from -6 to 6
- stacked_up_matrices: bfloat16 [28672, 4096], P('row', 'col'), may hold values from -6 to 6
- ranks: int32 [64], replicated, may hold values from 1 to 64, 2304 in all
- samples: int32 [64], replicated, may hold values from 256 to 1023
Outputs:
- merged: bfloat16 [28672, 8192], P(('row', 'col'))
Inputs may be any that keep to these rules, and one draw needn't show every extreme that they name: The ranks sum to 2304; the largest is exactly 64.
All inputs are finite; a program needn't handle non-finite values.
Results may differ from a plain program's by a relative error of at most 0.0038.
Values may be sent and summed in bfloat16 or wider, within the bound.
No kernel may reach another device: no remote copies, remote signals or barrier semaphores. Data moves between devices by JAX's collectives and lax.ppermute only.
A program may use at most 128 MiB of HBM per device.

v0:
```python
import jax
import jax.numpy as jnp
from jax import lax
from jax.sharding import PartitionSpec as P

RMAX = 64


adapter_alpha_value = 8.0


def slot_scale(ranks, samples):
    counts = samples.astype(jnp.float32)
    client_weight_fraction = counts / jnp.sum(counts)
    client_scale_factor = (
        client_weight_fraction * adapter_alpha_value / jnp.sqrt(ranks.astype(jnp.float32))
    )
    is_live = jnp.arange(RMAX, dtype=jnp.int32)[None, :] < ranks[:, None]
    return jnp.where(is_live, client_scale_factor[:, None], jnp.float32(0.0)).reshape(-1)


def shards(base_weight, stacked_down_matrices, stacked_up_matrices, ranks, samples):
    coefficient = slot_scale(ranks, samples)
    gathered_up = lax.all_gather(stacked_up_matrices, "col", axis=1, tiled=True)
    scaled_up = (gathered_up.astype(jnp.float32) * coefficient[None, :]).astype(jnp.bfloat16)
    update = jnp.dot(
        scaled_up,
        lax.all_gather(stacked_down_matrices, "row", axis=0, tiled=True),
        preferred_element_type=jnp.float32,
    )
    merged = (base_weight.astype(jnp.float32) + update).astype(jnp.bfloat16)
    return lax.all_to_all(merged, "col", split_axis=0, concat_axis=1, tiled=True)


def solution(mesh):
    placed = (P("row", "col"), P("row", "col"), P("row", "col"), P(), P())
    return jax.shard_map(
        shards, mesh=mesh, in_specs=placed, out_specs=P(("row", "col"), None), check_vma=False
    )
```

profile of v0, /device:TPU:24, one launch (start us, length us, event | category | flops | bytes accessed | tf_op | source)
XLA Modules:
  0.0 237.0 jit_solution(10065302188238054074)
XLA Ops:
  6.5 0.0 all-gather.3.cloned.1.call-start
  6.5 0.7 all-gather.3.cloned.1.call-update
  7.3 0.0 all-gather.5.cloned.1.call-start
  7.3 0.7 all-gather.5.cloned.1.call-update
  8.0 1.3 convert_reduce_fusion
  9.3 1.3 rsqrt_multiply_fusion
  10.6 0.7 fusion.2
  11.3 0.1 select_n.12
  11.4 72.8 %all-gather.3.cloned.1.call-done = bf16[896,4096]{1,0:T(8,128)(2,1)} async-done(((bf16[896,1024]{1,0:T(8,128)(2,1)}), bf16[896,4096]{1,0:T(8,128)(2,1)}) %all-gather.3.cloned.1.call-update) | async-done | bytes 7340048 | tf_op jit(solution)/shard_map/all_gather | solution.py:24
  84.2 77.1 %all-gather.5.cloned.1.call-done = bf16[4096,2048]{1,0:T(8,128)(2,1)} async-done(((bf16[128,2048]{1,0:T(8,128)(2,1)}), bf16[4096,2048]{1,0:T(8,128)(2,1)}) %all-gather.5.cloned.1.call-update) | async-done | bytes 16777232 | tf_op jit(solution)/shard_map/all_gather | solution.py:28
  161.3 20.5 %add_convert_fusion = bf16[896,2048]{1,0:T(8,128)(2,1)S(1)} fusion(bf16[896,2048]{1,0:T(8,128)(2,1)} %param.5, bf16[4096,2048]{1,0:T(8,128)(2,1)} %all-gather.5.cloned.1.call-done, bf16[896,4096]{1,0:T(8,128)(2,1)} %all-gather.3.cloned.1.call-done, f32[4096]{0:T(1024)S(1)} %select_n.12), kind=kOutput, calls=%fused_computation.2 | convolution fusion | flops 15048900608 | bytes 31473664 | tf_op jit(solution)/shard_map/dot_general | solution.py:26
  181.8 46.1 %all_to_all.19 = bf16[4,224,2048]{2,1,0:T(8,128)(2,1)S(1)} all-to-all(bf16[4,224,2048]{2,1,0:T(8,128)(2,1)S(1)} %bitcast.6), channel_id=1, replica_groups=mesh['row'=32,'col'=4] {'col'}, dimensions={0} | all-to-all | bytes 7340032 | tf_op jit(solution)/shard_map/all_to_all | solution.py:32
  227.9 2.3 copy.7
Async XLA Ops:
  6.5 77.6 %all-gather.3.cloned.1.call-start = ((), (), s32[]{:S(2)}) async-start(), calls=%async_computation.1 | async-start | bytes 9175040 | tf_op jit(solution)/shard_map/all_gather | solution.py:24
  7.3 154.0 %all-gather.5.cloned.1.call-start = ((), (), s32[]{:S(2)}) async-start(), calls=%async_computation.2 | async-start | bytes 17301504 | tf_op jit(solution)/shard_map/all_gather | solution.py:28
Sparse Core Ops, SparseCore 0:
  9.0 75.1 all-gather.2
  86.4 74.7 all-gather.4
where the time goes:
time: 239 us; the launch traced here: 237 us
  waiting for transfers between devices  151 us (63%)
  blocking collectives  46.1 us (19%)
  matrix products  20.5 us (9%)
  between operations  13.4 us (6%)
  other arithmetic  3.32 us (1%)
    all_gather x1, waiting for transfers between devices, shards(): lax.all_gather(stacked_down_matrices, 'row', axis=0, tiled=True)  77.1 us
    all_gather x1, waiting for transfers between devices, shards(): gathered_up = lax.all_gather(stacked_up_matrices, 'col', axis=1, tiled=True)  72.8 us
    all_to_all x1, blocking collectives, shards(): lax.all_to_all(merged, 'col', split_axis=0, concat_axis=1, tiled=True)  46.1 us
    dot_general x1, matrix products, shards(): jnp.dot(scaled_up, lax.all_gather(stacked_down_matrices, 'row', axis=0, t...  20.5 us
  transfers between devices with their start and end apart: 2, of which 2 were waited for; matrix products, arithmetic and copies ran while one was open for 1% of the time, Pallas kernels for 0%

commit v1 on v0

v1 whole, which is shorter than its diff:
```python
import jax
import jax.numpy as jnp
from jax import lax
from jax.experimental import pallas as pl
from jax.experimental.pallas import tpu as pltpu
from jax.sharding import PartitionSpec as P

RMAX = 64
ALPHA = 8.0
WIDTH = 768
CHUNKS = (((0, 512), (512, 512)), ((0, 512), (512, 512)))
VMEM_LIMIT = 12 * 2**20
EARLY = 224
UNPACK_FLOPS = 30 * 10**9
MERGE_LIMIT = 22 * 2**20


def slot_scale(ranks, samples):
    counts = samples.astype(jnp.float32)
    fraction = counts / jnp.sum(counts)
    scale = fraction * ALPHA / jnp.sqrt(ranks.astype(jnp.float32))
    is_live = jnp.arange(RMAX, dtype=jnp.int32)[None, :] < ranks[:, None]
    return jnp.where(is_live, scale[:, None], jnp.float32(0.0)).reshape(-1)


def torus_place():
    row = lax.axis_index("row")
    return row // 8, (row // 2) % 4, row % 2


def near(at, i):
    return (at + (0, 3, 1, 2)[i]) % 4


def one_hot(ranks, group, slots, first, width):
    clients = slots // RMAX
    slot = lax.broadcasted_iota(jnp.int32, (1, slots), 1)
    client, m = slot // RMAX, slot % RMAX
    place = jnp.full((1, slots), -1, jnp.int32)
    start = jnp.int32(-first)
    for k in range(clients):
        rank = ranks[group * clients + k]
        place = jnp.where((client == k) & (m < rank), start + m, place)
        start = start + rank
    row = lax.broadcasted_iota(jnp.int32, (width, slots), 0)
    return jnp.where(row == place, jnp.float32(1.0), jnp.float32(0.0)).astype(jnp.bfloat16)


def pack(up, ranks, first, width):
    rows, slots = up.shape
    half = rows // 2
    clients = slots // RMAX

    def kernel(ranks_ref, up_ref, top_ref, bottom_ref, up_v, hot, sem):
        copies = []
        for j in range(2):
            span = pl.ds(j * half, half)
            copies.append(pltpu.make_async_copy(up_ref.at[span], up_v.at[span], sem.at[j]))
            copies[-1].start()
        group = lax.axis_index("col")
        m = lax.broadcasted_iota(jnp.int32, (RMAX, width), 0)
        ahead = lax.broadcasted_iota(jnp.int32, (RMAX, width), 1) - m
        start = jnp.int32(-first)
        for k in range(clients):
            rank = ranks_ref[group * clients + k]
            here = (ahead == start) & (m < rank)
            hot[k * RMAX : (k + 1) * RMAX] = jnp.where(here, jnp.float32(1.0), jnp.float32(0.0)).astype(jnp.bfloat16)
            start = start + rank
        for j, out_ref in enumerate((top_ref, bottom_ref)):
            copies[j].wait()
            out_ref[...] = jnp.dot(
                up_v[j * half : (j + 1) * half], hot[...], preferred_element_type=jnp.float32
            ).astype(jnp.bfloat16)

    return pl.pallas_call(
        kernel,
        grid_spec=pltpu.PrefetchScalarGridSpec(
            num_scalar_prefetch=1,
            grid=(1,),
            in_specs=[pl.BlockSpec(memory_space=pl.ANY)],
            out_specs=[pl.BlockSpec((half, width), lambda i, *_: (0, 0))] * 2,
            scratch_shapes=[
                pltpu.VMEM((rows, slots), jnp.bfloat16),
                pltpu.VMEM((slots, width), jnp.bfloat16),
                pltpu.SemaphoreType.DMA((2,)),
            ],
        ),
        out_shape=[jax.ShapeDtypeStruct((half, width), jnp.bfloat16)] * 2,
        compiler_params=pltpu.CompilerParams(vmem_limit_bytes=VMEM_LIMIT),
        cost_estimate=pl.CostEstimate(flops=2 * rows * slots * width, bytes_accessed=4 * rows * slots, transcendentals=0),
        name="pack",
    )(ranks, up)


def unpack(ups, items, rest, most, ranks, scale):
    groups, _, slots = scale.shape
    inner = slots // groups
    arrays = []
    for item in items:
        if not any(item[0] is a for a in arrays):
            arrays.append(item[0])
    index = [next(j for j, a in enumerate(arrays) if a is item[0]) for item in items]
    rows = items[0][0].shape[0] if ups is None else ups.shape[1]
    spill = slots - WIDTH
    n = len(arrays)

    def kernel(ranks_ref, most_ref, *refs):
        part_refs, scale_ref, rest_ref = refs[:n], refs[n], refs[n + 1]
        out_ref, rest_v, sem = refs[-3:]

        def put(group, at, value, add):
            for z in range(groups):
                cols = slice(z * inner, (z + 1) * inner)
                target = pl.ds(pl.multiple_of(group * inner, inner), inner)
                piece = value[:, cols]
                span = slice(at, at + value.shape[0])
                if add:
                    piece = piece + out_ref[group, span, cols]
                out_ref[group, span, cols] = piece
                out_ref[groups + z, span, target] = piece

        for which in range(groups):
            mine = [(j, item) for j, item in zip(index, items) if item[2] == which]
            if not mine:
                continue
            group = near(lax.axis_index("col"), which)
            factor = scale_ref[group]
            if which > 0:
                hot = one_hot(ranks_ref, group, slots, 0, WIDTH)
            for j, (_, first, _, at, count) in mine:
                part = part_refs[j][first : first + count]
                if which > 0:
                    whole = jnp.dot(part, hot, preferred_element_type=jnp.float32)
                else:
                    whole = part.astype(jnp.float32)
                put(group, at, (whole * factor).astype(jnp.bfloat16), False)
            if which > 0:

                @pl.when(most_ref[0] > WIDTH)
                def _(mine=mine, which=which, group=group, factor=factor):
                    copy = pltpu.make_async_copy(rest_ref.at[:, (which - 1) * spill : which * spill], rest_v, sem)
                    copy.start()
                    copy.wait()
                    hot = one_hot(ranks_ref, group, slots, WIDTH, spill)
                    for _, (_, _, _, at, count) in mine:
                        whole = jnp.dot(rest_v[at : at + count], hot, preferred_element_type=jnp.float32)
                        put(group, at, (whole * factor).astype(jnp.bfloat16), True)

    whole = pl.BlockSpec(memory_space=pltpu.VMEM)
    vmem = lambda a: pltpu.with_memory_space_constraint(a, pltpu.VMEM)
    extra = [] if ups is None else [vmem(ups)]
    return pl.pallas_call(
        kernel,
        grid_spec=pltpu.PrefetchScalarGridSpec(
            num_scalar_prefetch=2,
            grid=(1,),
            in_specs=[whole] * (n + 1) + [pl.BlockSpec(memory_space=pl.ANY)] + [whole] * len(extra),
            out_specs=whole,
            scratch_shapes=[pltpu.VMEM((rows, spill), jnp.bfloat16), pltpu.SemaphoreType.DMA],
        ),
        out_shape=pltpu.VMEM((2 * groups, rows, slots), jnp.bfloat16),
        input_output_aliases={n + 4: 0} if extra else {},
        compiler_params=pltpu.CompilerParams(vmem_limit_bytes=VMEM_LIMIT),
        cost_estimate=pl.CostEstimate(flops=UNPACK_FLOPS, bytes_accessed=6 * rows * slots, transcendentals=0),
        name="unpack",
    )(ranks, most, *[vmem(a) for a in arrays], scale, rest, *extra)


def pick(mine, other):
    rows, columns = mine.shape

    def kernel(mine_ref, other_ref, out_ref):
        core = lax.axis_index("row") % 2
        out_ref[pl.ds(pl.multiple_of(core * rows, rows), rows)] = mine_ref[...]
        out_ref[pl.ds(pl.multiple_of((1 - core) * rows, rows), rows)] = other_ref[...]

    return pl.pallas_call(
        kernel,
        grid=(1,),
        in_specs=[pl.BlockSpec((rows, columns // 2), lambda i: (0, lax.axis_index("row") % 2))] * 2,
        out_specs=pl.BlockSpec((2 * rows, columns // 2), lambda i: (0, 0)),
        out_shape=jax.ShapeDtypeStruct((2 * rows, columns // 2), mine.dtype),
        compiler_params=pltpu.CompilerParams(vmem_limit_bytes=VMEM_LIMIT),
        cost_estimate=pl.CostEstimate(flops=0, bytes_accessed=4 * rows * columns, transcendentals=0),
        name="pick",
    )(mine, other)


def halves(upper_of, lower_of):
    rows, columns = upper_of.shape
    half = rows // 2

    def kernel(a_ref, b_ref, upper_ref, lower_ref, sem):
        copies = [
            pltpu.make_async_copy(a_ref.at[pl.ds(0, half)], upper_ref, sem.at[0]),
            pltpu.make_async_copy(b_ref.at[pl.ds(half, half)], lower_ref, sem.at[1]),
        ]
        for copy in copies:
            copy.start()
        for copy in copies:
            copy.wait()

    return pl.pallas_call(
        kernel,
        in_specs=[pl.BlockSpec(memory_space=pl.ANY)] * 2,
        out_specs=[pl.BlockSpec(memory_space=pl.ANY)] * 2,
        out_shape=[jax.ShapeDtypeStruct((half, columns), upper_of.dtype)] * 2,
        scratch_shapes=[pltpu.SemaphoreType.DMA((2,))],
        compiler_params=pltpu.CompilerParams(vmem_limit_bytes=VMEM_LIMIT),
        cost_estimate=pl.CostEstimate(flops=0, bytes_accessed=4 * rows * columns, transcendentals=0),
        name="halves",
    )(upper_of, lower_of)


def line_up(pieces):
    rows, columns = pieces[0].shape

    def kernel(*refs):
        x, z, core = torus_place()
        at = jnp.where(core == 0, x, z)
        for i in range(4):
            refs[4][pl.ds(pl.multiple_of(near(at, i) * rows, rows), rows)] = refs[i][...]

    return pl.pallas_call(
        kernel,
        out_shape=jax.ShapeDtypeStruct((4 * rows, columns), pieces[0].dtype),
        compiler_params=pltpu.CompilerParams(vmem_limit_bytes=VMEM_LIMIT),
        cost_estimate=pl.CostEstimate(flops=0, bytes_accessed=16 * rows * columns, transcendentals=0),
        name="line_up",
    )(*pieces)


def merge(ups, lines, base, theirs, at, width):
    _, rows, slots = ups.shape
    part = rows // 4
    features = base.shape[1]

    def half():
        core = lax.axis_index("row") % 2
        return 1 - core if theirs else core

    def kernel(ups_ref, l0, l1, l2, l3, l4, base_ref, o0, o1, o2, o3, d_v, base_v, total, d_sem, base_sem):
        x, z, _ = torus_place()
        core = half()
        along = jnp.where(core == 0, z, x)
        first = jnp.where(core == 0, 4, 0)
        where = ((l0, slots), (l1, slots), (l2, slots), (l3, slots // 2), (l4, slots // 2))
        copies = []
        row = 0
        for j, (line, count) in enumerate(where):
            copies.append(pltpu.make_async_copy(line.at[:, pl.ds(at, width)], d_v.at[pl.ds(row, count)], d_sem.at[j]))
            row += count
        base_at = pl.ds(pl.multiple_of(half() * (features // 2) + at, width), width)
        copies.append(pltpu.make_async_copy(base_ref.at[:, base_at], base_v, base_sem))
        for copy in copies:
            copy.start()
        for i in range(4):
            for copy in copies[i:] if i == 3 else copies[i : i + 1]:
                copy.wait()
            product = jnp.dot(
                ups_ref[first + near(along, i)], d_v[i * slots : (i + 1) * slots], preferred_element_type=jnp.float32
            )
            if i == 0:
                total[...] = product
            else:
                total[...] += product
        col = lax.axis_index("col")
        for i, out in enumerate((o0, o1, o2, o3)):
            r = pl.ds(pl.multiple_of(near(col, i) * part, 32), part)
            out[...] = (base_v[r, :].astype(jnp.float32) + total[r, :]).astype(jnp.bfloat16)

    hold = pl.BlockSpec(memory_space=pl.ANY)
    return pl.pallas_call(
        kernel,
        grid=(1,),
        in_specs=[pl.BlockSpec(memory_space=pltpu.VMEM)] + [hold] * 6,
        out_specs=[pl.BlockSpec((part, width), lambda i: (0, 0))] * 4,
        scratch_shapes=[
            pltpu.VMEM((4 * slots, width), jnp.bfloat16),
            pltpu.VMEM((rows, width), jnp.bfloat16),
            pltpu.VMEM((rows, width), jnp.float32),
            pltpu.SemaphoreType.DMA((5,)),
            pltpu.SemaphoreType.DMA,
        ],
        out_shape=[jax.ShapeDtypeStruct((part, width), jnp.bfloat16)] * 4,
        compiler_params=pltpu.CompilerParams(vmem_limit_bytes=MERGE_LIMIT),
        cost_estimate=pl.CostEstimate(flops=2 * rows * 4 * slots * width, bytes_accessed=4 * rows * width, transcendentals=0),
        name="merge",
    )(pltpu.with_memory_space_constraint(ups, pltpu.VMEM), *lines, base)


def place(pieces, features):
    part = pieces[0][0].shape[0]
    count = len(pieces[0])
    flat = [a for row in pieces for a in row]
    starts = [(theirs, at, width) for theirs in (False, True) for at, width in CHUNKS[theirs]]

    def kernel(*refs):
        core = lax.axis_index("row") % 2
        n = pl.program_id(0)
        for i in range(4):

            @pl.when(near(lax.axis_index("col"), i) == n)
            def _(i=i):
                for j, (theirs, at, width) in enumerate(starts):
                    half = 1 - core if theirs else core
                    cols = pl.ds(pl.multiple_of(half * (features // 8) + at, 128), width)
                    refs[-1][:, cols] = refs[i * count + j][...]

    return pl.pallas_call(
        kernel,
        grid=(4,),
        in_specs=[pl.BlockSpec(a.shape, lambda n: (0, 0)) for a in flat],
        out_specs=pl.BlockSpec((part, features // 4), lambda n: (0, n)),
        out_shape=jax.ShapeDtypeStruct((part, features), jnp.bfloat16),
        compiler_params=pltpu.CompilerParams(vmem_limit_bytes=VMEM_LIMIT),
        cost_estimate=pl.CostEstimate(flops=0, bytes_accessed=4 * part * features, transcendentals=0),
        name="place",
    )(*flat)


def ring(step):
    return [(i, (i + step) % 4) for i in range(4)]


def torus(step, first):
    pairs = []
    for x in range(4):
        for z in range(4):
            for core in range(2):
                along_x = (core == 0) == first
                to = ((x + step) % 4, z) if along_x else (x, (z + step) % 4)
                pairs.append(((x * 4 + z) * 2 + core, (to[0] * 4 + to[1]) * 2 + core))
    return pairs


SWAP = [(i, i ^ 1) for i in range(32)]


def after(value, *others):
    return lax.optimization_barrier((value, *others))[0]


def shards(base, down, up, ranks, samples):
    rows, slots = up.shape
    features = base.shape[1]

    half = rows // 2
    top, bottom = pack(up, ranks, 0, WIDTH)
    mine = pick(down, lax.ppermute(down, "row", SWAP))
    mine, top, bottom = lax.optimization_barrier((mine, top, bottom))

    left_top = lax.ppermute(top, "col", ring(1))
    right_bottom = lax.ppermute(bottom, "col", ring(3))
    piece_far = lax.ppermute(mine, "row", torus(2, True))
    piece_left = lax.ppermute(mine, "row", torus(1, True))
    piece_right = lax.ppermute(mine, "row", torus(3, True))

    most = jnp.max(jnp.sum(ranks.reshape(4, -1), axis=1))

    def send_rest(up, ranks):
        own = jnp.concatenate(pack(up, ranks, WIDTH, slots - WIDTH))
        return jnp.concatenate([lax.ppermute(own, "col", ring(k)) for k in (1, 3, 2)], axis=1)

    def no_rest(up, ranks):
        return jnp.zeros((rows, 3 * (slots - WIDTH)), jnp.bfloat16)

    rest = lax.cond(most > WIDTH, send_rest, no_rest, up, ranks)
    most = most.reshape(1)
    scale = slot_scale(ranks, samples).reshape(4, 1, slots)
    ups = unpack(None, [(up, 0, 0, 0, rows)], rest, most, ranks, scale)
    mine, piece_left, piece_right, piece_far, left_top, right_bottom, top, bottom, ups = lax.optimization_barrier(
        (mine, piece_left, piece_right, piece_far, left_top, right_bottom, top, bottom, ups)
    )

    line = line_up([mine, piece_left, piece_right, piece_far])
    line_left = lax.ppermute(line, "row", torus(1, False))
    line_right = lax.ppermute(line, "row", torus(3, False))
    from_left = lax.ppermute(jnp.concatenate([bottom, left_top[:EARLY]]), "col", ring(1))
    from_right = lax.ppermute(jnp.concatenate([top, right_bottom[:EARLY]]), "col", ring(3))
    line_there = lax.ppermute(line, "row", SWAP)
    ups = unpack(ups, [(left_top, 0, 1, 0, half), (right_bottom, 0, 2, half, half)], rest, most, ranks, scale)
    line, line_left, line_right, from_left, from_right, line_there, left_top, right_bottom, ups = (
        lax.optimization_barrier(
            (line, line_left, line_right, from_left, from_right, line_there, left_top, right_bottom, ups)
        )
    )

    upper, lower = halves(line_left, line_right)
    line_far = [lax.ppermute(upper, "row", torus(1, False)), lax.ppermute(lower, "row", torus(3, False))]
    late_left = lax.ppermute(left_top[EARLY:], "col", ring(1))
    late_right = lax.ppermute(right_bottom[EARLY:], "col", ring(3))
    left_there = lax.ppermute(line_left, "row", SWAP)
    ups = unpack(
        ups,
        [
            (from_left, 0, 1, half, half),
            (from_right, 0, 2, 0, half),
            (from_left, half, 3, 0, EARLY),
            (from_right, half, 3, half, EARLY),
        ],
        rest, most, ranks, scale,
    )
    *line_far, late_left, late_right, left_there, ups = lax.optimization_barrier(
        (*line_far, late_left, late_right, left_there, ups)
    )
    ups = unpack(
        ups,
        [(late_left, 0, 3, EARLY, half - EARLY), (late_right, 0, 3, half + EARLY, half - EARLY)],
        rest, most, ranks, scale,
    )
    lines = [line, line_left, line_right, *line_far]
    other_lines = [line_there, left_there] + [lax.ppermute(a, "row", SWAP) for a in lines[2:]]

    pieces = [[], [], [], []]
    for theirs, from_lines in ((False, lines), (True, other_lines)):
        for at, width in CHUNKS[theirs]:
            if len(pieces[0]) == 1:
                ups, *other_lines[2:] = lax.optimization_barrier((ups, *other_lines[2:]))
            own, to_left, to_right, to_far = merge(ups, from_lines, base, theirs, at, width)
            from_far = lax.ppermute(to_far, "col", ring(2))
            from_left = lax.ppermute(to_right, "col", ring(1))
            from_right = lax.ppermute(to_left, "col", ring(3))
            for row, piece in zip(pieces, (own, from_left, from_right, from_far)):
                row.append(piece)
    return place(pieces, 4 * features)


def solution(mesh):
    placed = (P("row", "col"), P("row", "col"), P("row", "col"), P(), P())
    return jax.shard_map(
        shards, mesh=mesh, in_specs=placed, out_specs=P(("row", "col"), None), check_vma=False
    )
```

time: 239 us -> 139 us (0.58)
  waiting for transfers between devices: 151 us -> 53.9 us
  blocking collectives: 46.1 us -> 0 us
  Pallas kernels: 0 us -> 39.8 us
  starting transfers between devices: 0.04 us -> 39.5 us
  matrix products: 20.5 us -> 0 us
  between operations: 13.4 us -> 0.96 us
    all_gather x2 -> x0, waiting for transfers between devices: 150 us -> none  [the longest x1 77.1 us: shards(): lax.all_gather(stacked_down_matrices, 'row', axis=0, tiled=True)]
    ppermute x0 -> x31, waiting for transfers between devices: none -> 53.9 us  [the longest x1 18.2 us: shards(): lax.ppermute(jnp.concatenate([top, right_bottom[:EARLY]]), 'col', ring(3))]
    all_to_all x1 -> x0, blocking collectives: 46.1 us -> none  [shards(): lax.all_to_all(merged, 'col', split_axis=0, concat_axis=1, tiled=True)]
    pallas_call x0 -> x13, Pallas kernels: none -> 39.8 us  [the longest x4 20.4 us: merge(): pl.pallas_call(kernel, grid=(1,), in_specs=[pl.BlockSpec(memory_space=plt...]
    ppermute x0 -> x31, starting transfers between devices: none -> 39.5 us  [the longest x4 8 us: shards(): from_left = lax.ppermute(to_right, 'col', ring(1))]
    dot_general x1 -> x0, matrix products: 20.5 us -> none  [shards(): jnp.dot(scaled_up, lax.all_gather(stacked_down_matrices, 'row', axis=0, t...]
  transfers between devices with their start and end apart: 2 -> 31, of which waited for: 2 -> 11; matrix products, arithmetic and copies ran while one was open for 1% -> 4% of each run, Pallas kernels for 0% -> 27%
where the time goes in v1:
time: 139 us
  waiting for transfers between devices  53.9 us (39%)
  Pallas kernels  39.8 us (29%)
  starting transfers between devices  39.5 us (28%)
  other arithmetic  3.49 us (3%)
  local copies, waits for them, and re-layouts  1.43 us (1%)
    pallas_call x4, Pallas kernels, merge(): pl.pallas_call(kernel, grid=(1,), in_specs=[pl.BlockSpec(memory_space=plt...  20.4 us
    ppermute x1, waiting for transfers between devices, shards(): lax.ppermute(jnp.concatenate([top, right_bottom[:EARLY]]), 'col', ring(3))  18.2 us
    ppermute x4, waiting for transfers between devices, shards(): from_right = lax.ppermute(to_left, 'col', ring(3))  13.9 us
    pallas_call x4, Pallas kernels, unpack(): pl.pallas_call(kernel, grid_spec=pltpu.PrefetchScalarGridSpec(num_scalar_...  12.4 us
    ppermute x4, starting transfers between devices, shards(): from_left = lax.ppermute(to_right, 'col', ring(1))  8 us
    ppermute x4, starting transfers between devices, shards(): from_far = lax.ppermute(to_far, 'col', ring(2))  7.82 us
    ppermute x1, waiting for transfers between devices, shards(): left_top = lax.ppermute(top, 'col', ring(1))  5.92 us
    ppermute x1, waiting for transfers between devices, shards(): piece_right = lax.ppermute(mine, 'row', torus(3, True))  5.2 us
  transfers between devices with their start and end apart: 31, of which 11 were waited for; matrix products, arithmetic and copies ran while one was open for 4% of the time, Pallas kernels for 27%

profile of v1, /device:TPU:24, one launch (start us, length us, event | category | flops | bytes accessed | tf_op | source)
XLA Modules:
  0.0 139.1 jit_solution(402687268521327626)
XLA Ops:
  0.0 0.7 reshape.64
  0.7 0.1 reduce_sum.18
  0.9 0.6 reduce_max.9
  2.2 0.1 lt.29
  2.2 0.1 lt.30
  2.3 1.3 convert_reduce_fusion
  3.6 1.3 rsqrt_multiply_fusion
  4.9 0.1 broadcast_in_dim.19
  5.0 0.1 broadcast_in_dim.20
  5.1 0.1 broadcast_in_dim.21
  5.2 0.1 conditional.1
  5.2 0.1 broadcast.31
  5.4 4.2 %pack.3 = (bf16[448,768]{1,0:T(8,128)(2,1)S(1)}, bf16[448,768]{1,0:T(8,128)(2,1)S(1)}) custom-call(s32[64]{0:T(128)} %ranks_ref.9, bf16[896,1024]{1,0:T(8,128)(2,1)} %refs_0_.1), custom_call_target="tpu_custom_call" | custom-call | flops 1409286144 | bytes 3670016 | tf_op jit(solution)/shard_map/pack/pallas_call | solution.py:75
  9.7 1.6 %collective-permute-start.4 = (bf16[256,1024]{1,0:T(8,128)(2,1)S(1)}, bf16[256,1024]{1,0:T(8,128)(2,1)S(1)}, u32[]{:S(2)}, u32[]{:S(2)}) collective-permute-start(bf16[256,1024]{1,0:T(8,128)(2,1)S(1)} %pick.1.refs_0_), channel_id=1, source_target_pairs={{0,32},{4,12},{8,40},{12,20},{16,48},{20,28},{24,56},{28,4},{32,64... | collective-permute-start | bytes 1572872 | tf_op jit(solution)/shard_map/ppermute | solution.py:356
  11.2 1.8 %collective-permute-start.5 = (bf16[256,1024]{1,0:T(8,128)(2,1)S(1)}, bf16[256,1024]{1,0:T(8,128)(2,1)S(1)}, u32[]{:S(2)}, u32[]{:S(2)}) collective-permute-start(bf16[256,1024]{1,0:T(8,128)(2,1)S(1)} %pick.1.refs_0_), channel_id=1, source_target_pairs={{0,96},{4,28},{8,104},{12,4},{16,112},{20,12},{24,120},{28,20},{32... | collective-permute-start | bytes 1572872 | tf_op jit(solution)/shard_map/ppermute | solution.py:357
  13.0 1.8 %collective-permute-start.6 = (bf16[256,1024]{1,0:T(8,128)(2,1)S(1)}, bf16[256,1024]{1,0:T(8,128)(2,1)S(1)}, u32[]{:S(2)}, u32[]{:S(2)}) collective-permute-start(bf16[256,1024]{1,0:T(8,128)(2,1)S(1)} %pick.1.refs_0_), channel_id=1, source_target_pairs={{0,64},{4,20},{8,72},{12,28},{16,80},{20,4},{24,88},{28,12},{32,96... | collective-permute-start | bytes 1572872 | tf_op jit(solution)/shard_map/ppermute | solution.py:355
  14.8 0.2 collective-permute-start.7
  15.0 1.8 %collective-permute-start.8 = (bf16[448,768]{1,0:T(8,128)(2,1)S(1)}, bf16[448,768]{1,0:T(8,128)(2,1)S(1)}, u32[]{:S(2)}, u32[]{:S(2)}) collective-permute-start(bf16[448,768]{1,0:T(8,128)(2,1)S(1)} %get-tuple-element.76), channel_id=1, source_target_pairs={{0,3},{1,0},{2,1},{3,2},{4,7},{5,4},{6,5},{7,6},{8,11},{9,8},{10,9... | collective-permute-start | bytes 2064392 | tf_op jit(solution)/shard_map/ppermute | solution.py:354
  16.8 1.8 %unpack.4.refs_4_ = bf16[8,896,1024]{2,1,0:T(8,128)(2,1)S(1)} custom-call(s32[64]{0:T(128)S(1)} %copy-done.3, s32[1]{0:T(128)} %bitcast.most_ref, bf16[896,1024]{1,0:T(8,128)(2,1)S(1)} %copy-done.1, f32[4,1,1024]{2,1,0:T(1,128)S(1)} %compare_select_fusion.refs_1_.refs_2_, bf16[896,768]{1,0:T(8,128)(2,1)S(1)} %get-tuple-element.118.refs_2_.refs_3_), custom_call_target="tpu_custom_call" | custom-call | flops 30000001024 | bytes 5505024 | tf_op jit(solution)/shard_map/unpack/pallas_call | solution.py:152
  18.7 1.5 %collective-permute-done.4.refs_1_ = bf16[256,1024]{1,0:T(8,128)(2,1)S(1)} collective-permute-done((bf16[256,1024]{1,0:T(8,128)(2,1)S(1)}, bf16[256,1024]{1,0:T(8,128)(2,1)S(1)}, u32[]{:S(2)}, u32[]{:S(2)}) %collective-permute-start.4) | collective-permute-done | bytes 524320 | tf_op jit(solution)/shard_map/ppermute | solution.py:356
  20.2 5.2 %collective-permute-done.5.refs_2_ = bf16[256,1024]{1,0:T(8,128)(2,1)S(1)} collective-permute-done((bf16[256,1024]{1,0:T(8,128)(2,1)S(1)}, bf16[256,1024]{1,0:T(8,128)(2,1)S(1)}, u32[]{:S(2)}, u32[]{:S(2)}) %collective-permute-start.5) | collective-permute-done | bytes 524320 | tf_op jit(solution)/shard_map/ppermute | solution.py:357
  25.3 1.4 %collective-permute-done.6.refs_3_ = bf16[256,1024]{1,0:T(8,128)(2,1)S(1)} collective-permute-done((bf16[256,1024]{1,0:T(8,128)(2,1)S(1)}, bf16[256,1024]{1,0:T(8,128)(2,1)S(1)}, u32[]{:S(2)}, u32[]{:S(2)}) %collective-permute-start.6) | collective-permute-done | bytes 524320 | tf_op jit(solution)/shard_map/ppermute | solution.py:355
  26.8 5.9 %collective-permute-done.7.refs_0_ = bf16[448,768]{1,0:T(8,128)(2,1)S(1)} collective-permute-done((bf16[448,768]{1,0:T(8,128)(2,1)S(1)}, bf16[448,768]{1,0:T(8,128)(2,1)S(1)}, u32[]{:S(2)}, u32[]{:S(2)}) %collective-permute-start.7) | collective-permute-done | bytes 688160 | tf_op jit(solution)/shard_map/ppermute | solution.py:353
  32.7 1.2 collective-permute-done.8.refs_1_
  33.9 0.2 line_up.1.l0
  34.1 1.0 collective-permute-start.10
  35.0 0.5 collective-permute-start.13
  35.5 2.2 %collective-permute-start.9 = (bf16[1024,1024]{1,0:T(8,128)(2,1)S(1)}, bf16[1024,1024]{1,0:T(8,128)(2,1)S(1)}, u32[]{:S(2)}, u32[]{:S(2)}) collective-permute-start(bf16[1024,1024]{1,0:T(8,128)(2,1)S(1)} %line_up.1.l0), channel_id=1, source_target_pairs={{0,8},{4,36},{8,16},{12,44},{16,24},{20,52},{24,0},{28,60},{32,40}... | collective-permute-start | bytes 6291464 | tf_op jit(solution)/shard_map/ppermute | solution.py:377
  37.7 0.7 collective-permute-start.12
  38.5 2.7 %collective-permute-start.11 = (bf16[672,768]{1,0:T(8,128)(2,1)S(1)}, bf16[672,768]{1,0:T(8,128)(2,1)S(1)}, u32[]{:S(2)}, u32[]{:S(2)}) collective-permute-start(bf16[672,768]{1,0:T(8,128)(2,1)S(1)} %pad_maximum_fusion.1), channel_id=1, source_target_pairs={{0,1},{1,2},{2,3},{3,0},{4,5},{5,6},{6,7},{7,4},{8,9},{9,10},{10,1... | collective-permute-start | bytes 3096584 | tf_op jit(solution)/shard_map/ppermute | solution.py:379
  41.2 3.4 %unpack.5.refs_4_ = bf16[8,896,1024]{2,1,0:T(8,128)(2,1)S(1)} custom-call(s32[64]{0:T(128)S(1)} %copy-done.3, s32[1]{0:T(128)} %bitcast.most_ref, bf16[448,768]{1,0:T(8,128)(2,1)S(1)} %collective-permute-done.7.refs_0_, bf16[448,768]{1,0:T(8,128)(2,1)S(1)} %collective-permute-done.8.refs_1_, ...), custom_call_target="tpu_custom_call", output_to_operand_aliasing={{}: (6, {})} | custom-call | flops 30000001024 | bytes 5505024 | tf_op jit(solution)/shard_map/unpack/pallas_call | solution.py:152
  44.6 18.2 %collective-permute-done.12.refs_1_ = bf16[672,768]{1,0:T(8,128)(2,1)S(1)} collective-permute-done((bf16[672,768]{1,0:T(8,128)(2,1)S(1)}, bf16[672,768]{1,0:T(8,128)(2,1)S(1)}, u32[]{:S(2)}, u32[]{:S(2)}) %collective-permute-start.12) | collective-permute-done | bytes 1032224 | tf_op jit(solution)/shard_map/ppermute | solution.py:380
  62.9 0.3 collective-permute-start.18
  63.1 0.2 halves.1
  63.3 1.0 collective-permute-start.14
  64.3 2.3 %collective-permute-start.15 = (bf16[512,1024]{1,0:T(8,128)(2,1)S(1)}, bf16[512,1024]{1,0:T(8,128)(2,1)S(1)}, u32[]{:S(2)}, u32[]{:S(2)}) collective-permute-start(bf16[512,1024]{1,0:T(8,128)(2,1)S(1)} %get-tuple-element.84), channel_id=1, source_target_pairs={{0,24},{4,100},{8,0},{12,108},{16,8},{20,116},{24,16},{28,124},{32... | collective-permute-start | bytes 3145736 | tf_op jit(solution)/shard_map/ppermute | solution.py:390
  66.6 3.2 %collective-permute-start.16 = (bf16[224,768]{1,0:T(8,128)(2,1)S(1)}, bf16[224,768]{1,0:T(8,128)(2,1)S(1)}, u32[]{:S(2)}, u32[]{:S(2)}) collective-permute-start(bf16[224,768]{1,0:T(8,128)(2,1)S(1)} %slice.14), channel_id=1, source_target_pairs={{0,1},{1,2},{2,3},{3,0},{4,5},{5,6},{6,7},{7,4},{8,9},{9,10},{10,1... | collective-permute-start | bytes 1032200 | tf_op jit(solution)/shard_map/ppermute | solution.py:391
  69.9 0.1 collective-permute-start.17
  69.9 4.6 %unpack.6.refs_4_ = bf16[8,896,1024]{2,1,0:T(8,128)(2,1)S(1)} custom-call(s32[64]{0:T(128)S(1)} %copy-done.3, s32[1]{0:T(128)} %bitcast.most_ref, bf16[672,768]{1,0:T(8,128)(2,1)S(1)} %collective-permute-done.11.refs_0_, bf16[672,768]{1,0:T(8,128)(2,1)S(1)} %collective-permute-done.12.refs_1_, ...), custom_call_target="tpu_custom_call", output_to_operand_aliasing={{}: (6, {})} | custom-call | flops 30000001024 | bytes 5505024 | tf_op jit(solution)/shard_map/unpack/pallas_call | solution.py:152
  74.6 2.7 %collective-permute-done.16.refs_0_ = bf16[224,768]{1,0:T(8,128)(2,1)S(1)} collective-permute-done((bf16[224,768]{1,0:T(8,128)(2,1)S(1)}, bf16[224,768]{1,0:T(8,128)(2,1)S(1)}, u32[]{:S(2)}, u32[]{:S(2)}) %collective-permute-start.16) | collective-permute-done | bytes 344096 | tf_op jit(solution)/shard_map/ppermute | solution.py:391
  77.3 3.5 %collective-permute-done.17.refs_1_ = bf16[224,768]{1,0:T(8,128)(2,1)S(1)} collective-permute-done((bf16[224,768]{1,0:T(8,128)(2,1)S(1)}, bf16[224,768]{1,0:T(8,128)(2,1)S(1)}, u32[]{:S(2)}, u32[]{:S(2)}) %collective-permute-start.17) | collective-permute-done | bytes 344096 | tf_op jit(solution)/shard_map/ppermute | solution.py:392
  80.8 0.1 collective-permute-start.20
  80.9 0.5 collective-permute-start.21
  81.4 2.6 %unpack.7.ups_ref = bf16[8,896,1024]{2,1,0:T(8,128)(2,1)S(1)} custom-call(s32[64]{0:T(128)S(1)} %copy-done.3, s32[1]{0:T(128)} %bitcast.most_ref, bf16[224,768]{1,0:T(8,128)(2,1)S(1)} %collective-permute-done.16.refs_0_, bf16[224,768]{1,0:T(8,128)(2,1)S(1)} %collective-permute-done.17.refs_1_, ...), custom_call_target="tpu_custom_call", output_to_operand_aliasing={{}: (6, {})} | custom-call | flops 30000001024 | bytes 5505024 | tf_op jit(solution)/shard_map/unpack/pallas_call | solution.py:152
  84.0 5.1 %merge.4 = (bf16[224,512]{1,0:T(8,128)(2,1)S(1)}, bf16[224,512]{1,0:T(8,128)(2,1)S(1)}, bf16[224,512]{1,0:T(8,128)(2,1)S(1)}, bf16[224,512]{1,0:T(8,128)(2,1)S(1)}) custom-call(bf16[8,896,1024]{2,1,0:T(8,128)(2,1)S(1)} %unpack.7.ups_ref, bf16[1024,1024]{1,0:T(8,128)(2,1)S(1)} %line_up.1.l0, bf16[1024,1024]{1,0:T(8,128)(2,1)S(1)} %collective-permute-done.9.a_ref.l1, ...), custom_call_target="tpu_custom_call" | custom-call | flops 3758096384 | bytes 1835008 | tf_op jit(solution)/shard_map/merge/pallas_call | solution.py:273
  89.1 1.7 %collective-permute-start.22 = (bf16[224,512]{1,0:T(8,128)(2,1)S(1)}, bf16[224,512]{1,0:T(8,128)(2,1)S(1)}, u32[]{:S(2)}, u32[]{:S(2)}) collective-permute-start(bf16[224,512]{1,0:T(8,128)(2,1)S(1)} %get-tuple-element.106), channel_id=1, source_target_pairs={{0,1},{1,2},{2,3},{3,0},{4,5},{5,6},{6,7},{7,4},{8,9},{9,10},{10,1... | collective-permute-start | bytes 688136 | tf_op jit(solution)/shard_map/ppermute | solution.py:422
  90.8 0.4 collective-permute-start.26
  91.2 1.2 collective-permute-start.30
  92.4 5.1 %merge.7 = (bf16[224,512]{1,0:T(8,128)(2,1)S(1)}, bf16[224,512]{1,0:T(8,128)(2,1)S(1)}, bf16[224,512]{1,0:T(8,128)(2,1)S(1)}, bf16[224,512]{1,0:T(8,128)(2,1)S(1)}) custom-call(bf16[8,896,1024]{2,1,0:T(8,128)(2,1)S(1)} %unpack.7.ups_ref, bf16[1024,1024]{1,0:T(8,128)(2,1)S(1)} %collective-permute-done.13.l0, ...), custom_call_target="tpu_custom_call" | custom-call | flops 3758096384 | bytes 1835008 | tf_op jit(solution)/shard_map/merge/pallas_call | solution.py:273
  97.5 1.8 %collective-permute-start.25 = (bf16[224,512]{1,0:T(8,128)(2,1)S(1)}, bf16[224,512]{1,0:T(8,128)(2,1)S(1)}, u32[]{:S(2)}, u32[]{:S(2)}) collective-permute-start(bf16[224,512]{1,0:T(8,128)(2,1)S(1)} %get-tuple-element.109), channel_id=1, source_target_pairs={{0,1},{1,2},{2,3},{3,0},{4,5},{5,6},{6,7},{7,4},{8,9},{9,10},{10,1... | collective-permute-start | bytes 688136 | tf_op jit(solution)/shard_map/ppermute | solution.py:422
  99.3 0.9 collective-permute-start.29
  100.2 5.1 %merge.6 = (bf16[224,512]{1,0:T(8,128)(2,1)S(1)}, bf16[224,512]{1,0:T(8,128)(2,1)S(1)}, bf16[224,512]{1,0:T(8,128)(2,1)S(1)}, bf16[224,512]{1,0:T(8,128)(2,1)S(1)}) custom-call(bf16[8,896,1024]{2,1,0:T(8,128)(2,1)S(1)} %unpack.7.ups_ref, bf16[1024,1024]{1,0:T(8,128)(2,1)S(1)} %collective-permute-done.13.l0, ...), custom_call_target="tpu_custom_call" | custom-call | flops 3758096384 | bytes 1835008 | tf_op jit(solution)/shard_map/merge/pallas_call | solution.py:273
  105.3 2.1 %collective-permute-start.33 = (bf16[224,512]{1,0:T(8,128)(2,1)S(1)}, bf16[224,512]{1,0:T(8,128)(2,1)S(1)}, u32[]{:S(2)}, u32[]{:S(2)}) collective-permute-start(bf16[224,512]{1,0:T(8,128)(2,1)S(1)} %get-tuple-element.117), channel_id=1, source_target_pairs={{0,2},{1,3},{2,0},{3,1},{4,6},{5,7},{6,4},{7,5},{8,10},{9,11},{10,... | collective-permute-start | bytes 688136 | tf_op jit(solution)/shard_map/ppermute | solution.py:421
  107.4 2.6 %collective-permute-start.24 = (bf16[224,512]{1,0:T(8,128)(2,1)S(1)}, bf16[224,512]{1,0:T(8,128)(2,1)S(1)}, u32[]{:S(2)}, u32[]{:S(2)}) collective-permute-start(bf16[224,512]{1,0:T(8,128)(2,1)S(1)} %get-tuple-element.108), channel_id=1, source_target_pairs={{0,1},{1,2},{2,3},{3,0},{4,5},{5,6},{6,7},{7,4},{8,9},{9,10},{10,1... | collective-permute-start | bytes 688136 | tf_op jit(solution)/shard_map/ppermute | solution.py:422
  110.0 5.1 %merge.5 = (bf16[224,512]{1,0:T(8,128)(2,1)S(1)}, bf16[224,512]{1,0:T(8,128)(2,1)S(1)}, bf16[224,512]{1,0:T(8,128)(2,1)S(1)}, bf16[224,512]{1,0:T(8,128)(2,1)S(1)}) custom-call(bf16[8,896,1024]{2,1,0:T(8,128)(2,1)S(1)} %unpack.7.ups_ref, bf16[1024,1024]{1,0:T(8,128)(2,1)S(1)} %line_up.1.l0, bf16[1024,1024]{1,0:T(8,128)(2,1)S(1)} %collective-permute-done.9.a_ref.l1, ...), custom_call_target="tpu_custom_call" | custom-call | flops 3758096384 | bytes 1835008 | tf_op jit(solution)/shard_map/merge/pallas_call | solution.py:273
  115.1 0.1 collective-permute-start.28
  115.2 1.4 %collective-permute-start.32 = (bf16[224,512]{1,0:T(8,128)(2,1)S(1)}, bf16[224,512]{1,0:T(8,128)(2,1)S(1)}, u32[]{:S(2)}, u32[]{:S(2)}) collective-permute-start(bf16[224,512]{1,0:T(8,128)(2,1)S(1)} %get-tuple-element.116), channel_id=1, source_target_pairs={{0,2},{1,3},{2,0},{3,1},{4,6},{5,7},{6,4},{7,5},{8,10},{9,11},{10,... | collective-permute-start | bytes 688136 | tf_op jit(solution)/shard_map/ppermute | solution.py:421
  116.7 1.8 %collective-permute-start.23 = (bf16[224,512]{1,0:T(8,128)(2,1)S(1)}, bf16[224,512]{1,0:T(8,128)(2,1)S(1)}, u32[]{:S(2)}, u32[]{:S(2)}) collective-permute-start(bf16[224,512]{1,0:T(8,128)(2,1)S(1)} %get-tuple-element.107), channel_id=1, source_target_pairs={{0,1},{1,2},{2,3},{3,0},{4,5},{5,6},{6,7},{7,4},{8,9},{9,10},{10,1... | collective-permute-start | bytes 688136 | tf_op jit(solution)/shard_map/ppermute | solution.py:422
  118.5 0.9 collective-permute-start.27
  119.4 3.1 %collective-permute-start.31 = (bf16[224,512]{1,0:T(8,128)(2,1)S(1)}, bf16[224,512]{1,0:T(8,128)(2,1)S(1)}, u32[]{:S(2)}, u32[]{:S(2)}) collective-permute-start(bf16[224,512]{1,0:T(8,128)(2,1)S(1)} %get-tuple-element.115), channel_id=1, source_target_pairs={{0,2},{1,3},{2,0},{3,1},{4,6},{5,7},{6,4},{7,5},{8,10},{9,11},{10,... | collective-permute-start | bytes 688136 | tf_op jit(solution)/shard_map/ppermute | solution.py:421
  122.5 7.4 %collective-permute-done.28.refs_10_ = bf16[224,512]{1,0:T(8,128)(2,1)S(1)} collective-permute-done((bf16[224,512]{1,0:T(8,128)(2,1)S(1)}, bf16[224,512]{1,0:T(8,128)(2,1)S(1)}, u32[]{:S(2)}, u32[]{:S(2)}) %collective-permute-start.28) | collective-permute-done | bytes 229408 | tf_op jit(solution)/shard_map/ppermute | solution.py:423
  129.9 0.4 collective-permute-done.23.refs_5_
  130.3 6.5 %collective-permute-done.27.refs_9_ = bf16[224,512]{1,0:T(8,128)(2,1)S(1)} collective-permute-done((bf16[224,512]{1,0:T(8,128)(2,1)S(1)}, bf16[224,512]{1,0:T(8,128)(2,1)S(1)}, u32[]{:S(2)}, u32[]{:S(2)}) %collective-permute-start.27) | collective-permute-done | bytes 229408 | tf_op jit(solution)/shard_map/ppermute | solution.py:423
  136.8 2.3 %place.1 = bf16[224,8192]{1,0:T(8,128)(2,1)} custom-call(bf16[224,512]{1,0:T(8,128)(2,1)S(1)} %get-tuple-element.96.refs_0_, bf16[224,512]{1,0:T(8,128)(2,1)S(1)} %get-tuple-element.98.refs_1_, bf16[224,512]{1,0:T(8,128)(2,1)S(1)} %get-tuple-element.104.refs_2_, bf16[224,512]{1,0:T(8,128)(2,1)S(1)} %get-tuple-element.105.refs_3_, ...), custom_call_target="tpu_custom_call" | custom-call | bytes 7340032 | tf_op jit(solution)/shard_map/place/pallas_call | solution.py:310
  (40 shorter events, 0.5 us)
Async XLA Ops:
  0.0 9.6 %collective-permute-start.3 = (bf16[128,2048]{1,0:T(8,128)(2,1)}, bf16[128,2048]{1,0:T(8,128)(2,1)S(1)}, u32[]{:S(2)}, u32[]{:S(2)}) collective-permute-start(bf16[128,2048]{1,0:T(8,128)(2,1)} %mine_ref.1), channel_id=1, source_target_pairs={{0,4},{4,0},{8,12},{12,8},{16,20},{20,16},{24,28},{28,24},{32,36},... | collective-permute-start | bytes 1572872 | tf_op jit(solution)/shard_map/ppermute | solution.py:350
  5.3 4.3 %copy-start.2 = (bf16[128,2048]{1,0:T(8,128)(2,1)S(1)}, bf16[128,2048]{1,0:T(8,128)(2,1)}, u32[]{:S(2)}) copy-start(bf16[128,2048]{1,0:T(8,128)(2,1)} %mine_ref.1) | copy-start | bytes 1572868
  5.3 11.5 %copy-start.1 = (bf16[896,1024]{1,0:T(8,128)(2,1)S(1)}, bf16[896,1024]{1,0:T(8,128)(2,1)}, u32[]{:S(2)}) copy-start(bf16[896,1024]{1,0:T(8,128)(2,1)} %refs_0_.1) | copy-start | bytes 5505028
  5.4 11.5 %copy-start.3 = (s32[64]{0:T(128)S(1)}, s32[64]{0:T(128)}, u32[]{:S(2)}) copy-start(s32[64]{0:T(128)} %ranks_ref.9) | copy-start | bytes 772
  9.7 10.5 %collective-permute-start.4 = (bf16[256,1024]{1,0:T(8,128)(2,1)S(1)}, bf16[256,1024]{1,0:T(8,128)(2,1)S(1)}, u32[]{:S(2)}, u32[]{:S(2)}) collective-permute-start(bf16[256,1024]{1,0:T(8,128)(2,1)S(1)} %pick.1.refs_0_), channel_id=1, source_target_pairs={{0,32},{4,12},{8,40},{12,20},{16,48},{20,28},{24,56},{28,4},{32,64... | collective-permute-start | bytes 1572872 | tf_op jit(solution)/shard_map/ppermute | solution.py:356
  11.2 14.1 %collective-permute-start.5 = (bf16[256,1024]{1,0:T(8,128)(2,1)S(1)}, bf16[256,1024]{1,0:T(8,128)(2,1)S(1)}, u32[]{:S(2)}, u32[]{:S(2)}) collective-permute-start(bf16[256,1024]{1,0:T(8,128)(2,1)S(1)} %pick.1.refs_0_), channel_id=1, source_target_pairs={{0,96},{4,28},{8,104},{12,4},{16,112},{20,12},{24,120},{28,20},{32... | collective-permute-start | bytes 1572872 | tf_op jit(solution)/shard_map/ppermute | solution.py:357
  13.0 13.8 %collective-permute-start.6 = (bf16[256,1024]{1,0:T(8,128)(2,1)S(1)}, bf16[256,1024]{1,0:T(8,128)(2,1)S(1)}, u32[]{:S(2)}, u32[]{:S(2)}) collective-permute-start(bf16[256,1024]{1,0:T(8,128)(2,1)S(1)} %pick.1.refs_0_), channel_id=1, source_target_pairs={{0,64},{4,20},{8,72},{12,28},{16,80},{20,4},{24,88},{28,12},{32,96... | collective-permute-start | bytes 1572872 | tf_op jit(solution)/shard_map/ppermute | solution.py:355
  14.8 17.9 %collective-permute-start.7 = (bf16[448,768]{1,0:T(8,128)(2,1)S(1)}, bf16[448,768]{1,0:T(8,128)(2,1)S(1)}, u32[]{:S(2)}, u32[]{:S(2)}) collective-permute-start(bf16[448,768]{1,0:T(8,128)(2,1)S(1)} %get-tuple-element.78), channel_id=1, source_target_pairs={{0,1},{1,2},{2,3},{3,0},{4,5},{5,6},{6,7},{7,4},{8,9},{9,10},{10,1... | collective-permute-start | bytes 2064392 | tf_op jit(solution)/shard_map/ppermute | solution.py:353
  15.0 18.9 %collective-permute-start.8 = (bf16[448,768]{1,0:T(8,128)(2,1)S(1)}, bf16[448,768]{1,0:T(8,128)(2,1)S(1)}, u32[]{:S(2)}, u32[]{:S(2)}) collective-permute-start(bf16[448,768]{1,0:T(8,128)(2,1)S(1)} %get-tuple-element.76), channel_id=1, source_target_pairs={{0,3},{1,0},{2,1},{3,2},{4,7},{5,4},{6,5},{7,6},{8,11},{9,8},{10,9... | collective-permute-start | bytes 2064392 | tf_op jit(solution)/shard_map/ppermute | solution.py:354
  34.1 28.8 %collective-permute-start.10 = (bf16[1024,1024]{1,0:T(8,128)(2,1)S(1)}, bf16[1024,1024]{1,0:T(8,128)(2,1)S(1)}, u32[]{:S(2)}, u32[]{:S(2)}) collective-permute-start(bf16[1024,1024]{1,0:T(8,128)(2,1)S(1)} %line_up.1.l0), channel_id=1, source_target_pairs={{0,24},{4,100},{8,0},{12,108},{16,8},{20,116},{24,16},{28,124},{32... | collective-permute-start | bytes 6291464 | tf_op jit(solution)/shard_map/ppermute | solution.py:378
  35.0 27.8 %collective-permute-start.13 = (bf16[1024,1024]{1,0:T(8,128)(2,1)S(1)}, bf16[1024,1024]{1,0:T(8,128)(2,1)S(1)}, u32[]{:S(2)}, u32[]{:S(2)}) collective-permute-start(bf16[1024,1024]{1,0:T(8,128)(2,1)S(1)} %line_up.1.l0), channel_id=1, source_target_pairs={{0,4},{4,0},{8,12},{12,8},{16,20},{20,16},{24,28},{28,24},{32,36},... | collective-permute-start | bytes 6291464 | tf_op jit(solution)/shard_map/ppermute | solution.py:381
  35.5 27.4 %collective-permute-start.9 = (bf16[1024,1024]{1,0:T(8,128)(2,1)S(1)}, bf16[1024,1024]{1,0:T(8,128)(2,1)S(1)}, u32[]{:S(2)}, u32[]{:S(2)}) collective-permute-start(bf16[1024,1024]{1,0:T(8,128)(2,1)S(1)} %line_up.1.l0), channel_id=1, source_target_pairs={{0,8},{4,36},{8,16},{12,44},{16,24},{20,52},{24,0},{28,60},{32,40}... | collective-permute-start | bytes 6291464 | tf_op jit(solution)/shard_map/ppermute | solution.py:377
  37.7 25.1 %collective-permute-start.12 = (bf16[672,768]{1,0:T(8,128)(2,1)S(1)}, bf16[672,768]{1,0:T(8,128)(2,1)S(1)}, u32[]{:S(2)}, u32[]{:S(2)}) collective-permute-start(bf16[672,768]{1,0:T(8,128)(2,1)S(1)} %pad_maximum_fusion.2), channel_id=1, source_target_pairs={{0,3},{1,0},{2,1},{3,2},{4,7},{5,4},{6,5},{7,6},{8,11},{9,8},{10,9... | collective-permute-start | bytes 3096584 | tf_op jit(solution)/shard_map/ppermute | solution.py:380
  38.5 24.3 %collective-permute-start.11 = (bf16[672,768]{1,0:T(8,128)(2,1)S(1)}, bf16[672,768]{1,0:T(8,128)(2,1)S(1)}, u32[]{:S(2)}, u32[]{:S(2)}) collective-permute-start(bf16[672,768]{1,0:T(8,128)(2,1)S(1)} %pad_maximum_fusion.1), channel_id=1, source_target_pairs={{0,1},{1,2},{2,3},{3,0},{4,5},{5,6},{6,7},{7,4},{8,9},{9,10},{10,1... | collective-permute-start | bytes 3096584 | tf_op jit(solution)/shard_map/ppermute | solution.py:379
  62.9 17.9 %collective-permute-start.18 = (bf16[1024,1024]{1,0:T(8,128)(2,1)S(1)}, bf16[1024,1024]{1,0:T(8,128)(2,1)S(1)}, u32[]{:S(2)}, u32[]{:S(2)}) collective-permute-start(bf16[1024,1024]{1,0:T(8,128)(2,1)S(1)} %collective-permute-done.9.a_ref.l1), channel_id=1, source_target_pairs={{0,4},{4,0},{8,12},{12,8},{16,20},{20,16},{24,28},{28,24},{32,36},... | collective-permute-start | bytes 6291464 | tf_op jit(solution)/shard_map/ppermute | solution.py:393
  63.3 17.5 %collective-permute-start.14 = (bf16[512,1024]{1,0:T(8,128)(2,1)S(1)}, bf16[512,1024]{1,0:T(8,128)(2,1)S(1)}, u32[]{:S(2)}, u32[]{:S(2)}) collective-permute-start(bf16[512,1024]{1,0:T(8,128)(2,1)S(1)} %get-tuple-element.83), channel_id=1, source_target_pairs={{0,8},{4,36},{8,16},{12,44},{16,24},{20,52},{24,0},{28,60},{32,40}... | collective-permute-start | bytes 3145736 | tf_op jit(solution)/shard_map/ppermute | solution.py:390
  64.3 16.5 %collective-permute-start.15 = (bf16[512,1024]{1,0:T(8,128)(2,1)S(1)}, bf16[512,1024]{1,0:T(8,128)(2,1)S(1)}, u32[]{:S(2)}, u32[]{:S(2)}) collective-permute-start(bf16[512,1024]{1,0:T(8,128)(2,1)S(1)} %get-tuple-element.84), channel_id=1, source_target_pairs={{0,24},{4,100},{8,0},{12,108},{16,8},{20,116},{24,16},{28,124},{32... | collective-permute-start | bytes 3145736 | tf_op jit(solution)/shard_map/ppermute | solution.py:390
  66.6 10.6 %collective-permute-start.16 = (bf16[224,768]{1,0:T(8,128)(2,1)S(1)}, bf16[224,768]{1,0:T(8,128)(2,1)S(1)}, u32[]{:S(2)}, u32[]{:S(2)}) collective-permute-start(bf16[224,768]{1,0:T(8,128)(2,1)S(1)} %slice.14), channel_id=1, source_target_pairs={{0,1},{1,2},{2,3},{3,0},{4,5},{5,6},{6,7},{7,4},{8,9},{9,10},{10,1... | collective-permute-start | bytes 1032200 | tf_op jit(solution)/shard_map/ppermute | solution.py:391
  69.9 10.9 %collective-permute-start.17 = (bf16[224,768]{1,0:T(8,128)(2,1)S(1)}, bf16[224,768]{1,0:T(8,128)(2,1)S(1)}, u32[]{:S(2)}, u32[]{:S(2)}) collective-permute-start(bf16[224,768]{1,0:T(8,128)(2,1)S(1)} %slice.15), channel_id=1, source_target_pairs={{0,3},{1,0},{2,1},{3,2},{4,7},{5,4},{6,5},{7,6},{8,11},{9,8},{10,9... | collective-permute-start | bytes 1032200 | tf_op jit(solution)/shard_map/ppermute | solution.py:392
  77.2 14.0 %collective-permute-start.19 = (bf16[1024,1024]{1,0:T(8,128)(2,1)S(1)}, bf16[1024,1024]{1,0:T(8,128)(2,1)S(1)}, u32[]{:S(2)}, u32[]{:S(2)}) collective-permute-start(bf16[1024,1024]{1,0:T(8,128)(2,1)S(1)} %collective-permute-done.10.b_ref.l2), channel_id=1, source_target_pairs={{0,4},{4,0},{8,12},{12,8},{16,20},{20,16},{24,28},{28,24},{32,36},... | collective-permute-start | bytes 6291464 | tf_op jit(solution)/shard_map/ppermute | solution.py:413
  80.8 11.6 %collective-permute-start.20 = (bf16[512,1024]{1,0:T(8,128)(2,1)S(1)}, bf16[512,1024]{1,0:T(8,128)(2,1)S(1)}, u32[]{:S(2)}, u32[]{:S(2)}) collective-permute-start(bf16[512,1024]{1,0:T(8,128)(2,1)S(1)} %collective-permute-done.14.l3), channel_id=1, source_target_pairs={{0,4},{4,0},{8,12},{12,8},{16,20},{20,16},{24,28},{28,24},{32,36},... | collective-permute-start | bytes 3145736 | tf_op jit(solution)/shard_map/ppermute | solution.py:413
  80.9 11.5 %collective-permute-start.21 = (bf16[512,1024]{1,0:T(8,128)(2,1)S(1)}, bf16[512,1024]{1,0:T(8,128)(2,1)S(1)}, u32[]{:S(2)}, u32[]{:S(2)}) collective-permute-start(bf16[512,1024]{1,0:T(8,128)(2,1)S(1)} %collective-permute-done.15.l4), channel_id=1, source_target_pairs={{0,4},{4,0},{8,12},{12,8},{16,20},{20,16},{24,28},{28,24},{32,36},... | collective-permute-start | bytes 3145736 | tf_op jit(solution)/shard_map/ppermute | solution.py:413
  81.4 2.6 %copy-start = (bf16[896,2048]{1,0:T(8,128)(2,1)S(1)}, bf16[896,2048]{1,0:T(8,128)(2,1)}, u32[]{:S(2)}) copy-start(bf16[896,2048]{1,0:T(8,128)(2,1)} %base_ref.7) | copy-start | bytes 11010052
  89.1 16.2 %collective-permute-start.22 = (bf16[224,512]{1,0:T(8,128)(2,1)S(1)}, bf16[224,512]{1,0:T(8,128)(2,1)S(1)}, u32[]{:S(2)}, u32[]{:S(2)}) collective-permute-start(bf16[224,512]{1,0:T(8,128)(2,1)S(1)} %get-tuple-element.106), channel_id=1, source_target_pairs={{0,1},{1,2},{2,3},{3,0},{4,5},{5,6},{6,7},{7,4},{8,9},{9,10},{10,1... | collective-permute-start | bytes 688136 | tf_op jit(solution)/shard_map/ppermute | solution.py:422
  90.8 16.6 %collective-permute-start.26 = (bf16[224,512]{1,0:T(8,128)(2,1)S(1)}, bf16[224,512]{1,0:T(8,128)(2,1)S(1)}, u32[]{:S(2)}, u32[]{:S(2)}) collective-permute-start(bf16[224,512]{1,0:T(8,128)(2,1)S(1)} %get-tuple-element.110), channel_id=1, source_target_pairs={{0,3},{1,0},{2,1},{3,2},{4,7},{5,4},{6,5},{7,6},{8,11},{9,8},{10,9... | collective-permute-start | bytes 688136 | tf_op jit(solution)/shard_map/ppermute | solution.py:423
  91.2 23.9 %collective-permute-start.30 = (bf16[224,512]{1,0:T(8,128)(2,1)S(1)}, bf16[224,512]{1,0:T(8,128)(2,1)S(1)}, u32[]{:S(2)}, u32[]{:S(2)}) collective-permute-start(bf16[224,512]{1,0:T(8,128)(2,1)S(1)} %get-tuple-element.114), channel_id=1, source_target_pairs={{0,2},{1,3},{2,0},{3,1},{4,6},{5,7},{6,4},{7,5},{8,10},{9,11},{10,... | collective-permute-start | bytes 688136 | tf_op jit(solution)/shard_map/ppermute | solution.py:421
  97.5 17.7 %collective-permute-start.25 = (bf16[224,512]{1,0:T(8,128)(2,1)S(1)}, bf16[224,512]{1,0:T(8,128)(2,1)S(1)}, u32[]{:S(2)}, u32[]{:S(2)}) collective-permute-start(bf16[224,512]{1,0:T(8,128)(2,1)S(1)} %get-tuple-element.109), channel_id=1, source_target_pairs={{0,1},{1,2},{2,3},{3,0},{4,5},{5,6},{6,7},{7,4},{8,9},{9,10},{10,1... | collective-permute-start | bytes 688136 | tf_op jit(solution)/shard_map/ppermute | solution.py:422
  99.3 17.4 %collective-permute-start.29 = (bf16[224,512]{1,0:T(8,128)(2,1)S(1)}, bf16[224,512]{1,0:T(8,128)(2,1)S(1)}, u32[]{:S(2)}, u32[]{:S(2)}) collective-permute-start(bf16[224,512]{1,0:T(8,128)(2,1)S(1)} %get-tuple-element.113), channel_id=1, source_target_pairs={{0,3},{1,0},{2,1},{3,2},{4,7},{5,4},{6,5},{7,6},{8,11},{9,8},{10,9... | collective-permute-start | bytes 688136 | tf_op jit(solution)/shard_map/ppermute | solution.py:423
  105.3 13.2 %collective-permute-start.33 = (bf16[224,512]{1,0:T(8,128)(2,1)S(1)}, bf16[224,512]{1,0:T(8,128)(2,1)S(1)}, u32[]{:S(2)}, u32[]{:S(2)}) collective-permute-start(bf16[224,512]{1,0:T(8,128)(2,1)S(1)} %get-tuple-element.117), channel_id=1, source_target_pairs={{0,2},{1,3},{2,0},{3,1},{4,6},{5,7},{6,4},{7,5},{8,10},{9,11},{10,... | collective-permute-start | bytes 688136 | tf_op jit(solution)/shard_map/ppermute | solution.py:421
  107.4 12.0 %collective-permute-start.24 = (bf16[224,512]{1,0:T(8,128)(2,1)S(1)}, bf16[224,512]{1,0:T(8,128)(2,1)S(1)}, u32[]{:S(2)}, u32[]{:S(2)}) collective-permute-start(bf16[224,512]{1,0:T(8,128)(2,1)S(1)} %get-tuple-element.108), channel_id=1, source_target_pairs={{0,1},{1,2},{2,3},{3,0},{4,5},{5,6},{6,7},{7,4},{8,9},{9,10},{10,1... | collective-permute-start | bytes 688136 | tf_op jit(solution)/shard_map/ppermute | solution.py:422
  115.1 14.8 %collective-permute-start.28 = (bf16[224,512]{1,0:T(8,128)(2,1)S(1)}, bf16[224,512]{1,0:T(8,128)(2,1)S(1)}, u32[]{:S(2)}, u32[]{:S(2)}) collective-permute-start(bf16[224,512]{1,0:T(8,128)(2,1)S(1)} %get-tuple-element.112), channel_id=1, source_target_pairs={{0,3},{1,0},{2,1},{3,2},{4,7},{5,4},{6,5},{7,6},{8,11},{9,8},{10,9... | collective-permute-start | bytes 688136 | tf_op jit(solution)/shard_map/ppermute | solution.py:423
  115.2 14.7 %collective-permute-start.32 = (bf16[224,512]{1,0:T(8,128)(2,1)S(1)}, bf16[224,512]{1,0:T(8,128)(2,1)S(1)}, u32[]{:S(2)}, u32[]{:S(2)}) collective-permute-start(bf16[224,512]{1,0:T(8,128)(2,1)S(1)} %get-tuple-element.116), channel_id=1, source_target_pairs={{0,2},{1,3},{2,0},{3,1},{4,6},{5,7},{6,4},{7,5},{8,10},{9,11},{10,... | collective-permute-start | bytes 688136 | tf_op jit(solution)/shard_map/ppermute | solution.py:421
  116.7 13.6 %collective-permute-start.23 = (bf16[224,512]{1,0:T(8,128)(2,1)S(1)}, bf16[224,512]{1,0:T(8,128)(2,1)S(1)}, u32[]{:S(2)}, u32[]{:S(2)}) collective-permute-start(bf16[224,512]{1,0:T(8,128)(2,1)S(1)} %get-tuple-element.107), channel_id=1, source_target_pairs={{0,1},{1,2},{2,3},{3,0},{4,5},{5,6},{6,7},{7,4},{8,9},{9,10},{10,1... | collective-permute-start | bytes 688136 | tf_op jit(solution)/shard_map/ppermute | solution.py:422
  118.5 18.3 %collective-permute-start.27 = (bf16[224,512]{1,0:T(8,128)(2,1)S(1)}, bf16[224,512]{1,0:T(8,128)(2,1)S(1)}, u32[]{:S(2)}, u32[]{:S(2)}) collective-permute-start(bf16[224,512]{1,0:T(8,128)(2,1)S(1)} %get-tuple-element.111), channel_id=1, source_target_pairs={{0,3},{1,0},{2,1},{3,2},{4,7},{5,4},{6,5},{7,6},{8,11},{9,8},{10,9... | collective-permute-start | bytes 688136 | tf_op jit(solution)/shard_map/ppermute | solution.py:423
  119.4 17.4 %collective-permute-start.31 = (bf16[224,512]{1,0:T(8,128)(2,1)S(1)}, bf16[224,512]{1,0:T(8,128)(2,1)S(1)}, u32[]{:S(2)}, u32[]{:S(2)}) collective-permute-start(bf16[224,512]{1,0:T(8,128)(2,1)S(1)} %get-tuple-element.115), channel_id=1, source_target_pairs={{0,2},{1,3},{2,0},{3,1},{4,6},{5,7},{6,4},{7,5},{8,10},{9,11},{10,... | collective-permute-start | bytes 688136 | tf_op jit(solution)/shard_map/ppermute | solution.py:421

commit v2 on v1

--- a/solution.py
+++ b/solution.py
@@ -8,19 +8,12 @@
 RMAX = 64
 ALPHA = 8.0
 WIDTH = 768
+CHUNK = 512
 CHUNKS = (((0, 512), (512, 512)), ((0, 512), (512, 512)))
 VMEM_LIMIT = 12 * 2**20
-EARLY = 224
+EARLY = 160
 UNPACK_FLOPS = 30 * 10**9
 MERGE_LIMIT = 22 * 2**20
-
-
-def slot_scale(ranks, samples):
-    counts = samples.astype(jnp.float32)
-    fraction = counts / jnp.sum(counts)
-    scale = fraction * ALPHA / jnp.sqrt(ranks.astype(jnp.float32))
-    is_live = jnp.arange(RMAX, dtype=jnp.int32)[None, :] < ranks[:, None]
-    return jnp.where(is_live, scale[:, None], jnp.float32(0.0)).reshape(-1)
 
 
 def torus_place():
@@ -30,6 +23,23 @@
 
 def near(at, i):
     return (at + (0, 3, 1, 2)[i]) % 4
+
+
+def slot_scale(ranks, samples, group, slots):
+    clients = slots // RMAX
+    total = jnp.int32(0)
+    for k in range(samples.shape[0]):
+        total = total + samples[k]
+    slot = lax.broadcasted_iota(jnp.int32, (1, slots), 1)
+    client, m = slot // RMAX, slot % RMAX
+    rank = jnp.ones((1, slots), jnp.int32)
+    count = jnp.ones((1, slots), jnp.int32)
+    for k in range(clients):
+        rank = jnp.where(client == k, ranks[group * clients + k], rank)
+        count = jnp.where(client == k, samples[group * clients + k], count)
+    fraction = count.astype(jnp.float32) / jnp.full((1, slots), total, jnp.int32).astype(jnp.float32)
+    scale = fraction * ALPHA / jnp.sqrt(rank.astype(jnp.float32))
+    return jnp.where(m < rank, scale, jnp.float32(0.0))
 
 
 def one_hot(ranks, group, slots, first, width):
@@ -37,13 +47,13 @@
     slot = lax.broadcasted_iota(jnp.int32, (1, slots), 1)
     client, m = slot // RMAX, slot % RMAX
     place = jnp.full((1, slots), -1, jnp.int32)
-    start = jnp.int32(-first)
+    start = jnp.int32(0)
     for k in range(clients):
         rank = ranks[group * clients + k]
         place = jnp.where((client == k) & (m < rank), start + m, place)
         start = start + rank
-    row = lax.broadcasted_iota(jnp.int32, (width, slots), 0)
-    return jnp.where(row == place, jnp.float32(1.0), jnp.float32(0.0)).astype(jnp.bfloat16)
+    row = lax.broadcasted_iota(jnp.int32, (width, slots), 0) + first
+    return jnp.where(row == place, jnp.float32(1.0), jnp.float32(0.0)).astype(jnp.bfloat16), start
 
 
 def pack(up, ranks, first, width):
@@ -92,8 +102,8 @@
     )(ranks, up)
 
 
-def unpack(ups, items, rest, most, ranks, scale):
-    groups, _, slots = scale.shape
+def unpack(ups, items, rest, ranks, samples, slots):
+    groups = 4
     inner = slots // groups
     arrays = []
     for item in items:
@@ -104,8 +114,8 @@
     spill = slots - WIDTH
     n = len(arrays)
 
-    def kernel(ranks_ref, most_ref, *refs):
-        part_refs, scale_ref, rest_ref = refs[:n], refs[n], refs[n + 1]
+    def kernel(ranks_ref, samples_ref, *refs):
+        part_refs, rest_ref = refs[:n], refs[n]
         out_ref, rest_v, sem = refs[-3:]
 
         def put(group, at, value, add):
@@ -124,9 +134,9 @@
             if not mine:
                 continue
             group = near(lax.axis_index("col"), which)
-            factor = scale_ref[group]
+            factor = slot_scale(ranks_ref, samples_ref, group, slots)
             if which > 0:
-                hot = one_hot(ranks_ref, group, slots, 0, WIDTH)
+                hot, live = one_hot(ranks_ref, group, slots, 0, WIDTH)
             for j, (_, first, _, at, count) in mine:
                 part = part_refs[j][first : first + count]
                 if which > 0:
@@ -136,12 +146,12 @@
                 put(group, at, (whole * factor).astype(jnp.bfloat16), False)
             if which > 0:
 
-                @pl.when(most_ref[0] > WIDTH)
+                @pl.when(live > WIDTH)
                 def _(mine=mine, which=which, group=group, factor=factor):
                     copy = pltpu.make_async_copy(rest_ref.at[:, (which - 1) * spill : which * spill], rest_v, sem)
                     copy.start()
                     copy.wait()
-                    hot = one_hot(ranks_ref, group, slots, WIDTH, spill)
+                    hot, _ = one_hot(ranks_ref, group, slots, WIDTH, spill)
                     for _, (_, _, _, at, count) in mine:
                         whole = jnp.dot(rest_v[at : at + count], hot, preferred_element_type=jnp.float32)
                         put(group, at, (whole * factor).astype(jnp.bfloat16), True)
@@ -154,16 +164,16 @@
         grid_spec=pltpu.PrefetchScalarGridSpec(
             num_scalar_prefetch=2,
             grid=(1,),
-            in_specs=[whole] * (n + 1) + [pl.BlockSpec(memory_space=pl.ANY)] + [whole] * len(extra),
+            in_specs=[whole] * n + [pl.BlockSpec(memory_space=pl.ANY)] + [whole] * len(extra),
             out_specs=whole,
             scratch_shapes=[pltpu.VMEM((rows, spill), jnp.bfloat16), pltpu.SemaphoreType.DMA],
         ),
         out_shape=pltpu.VMEM((2 * groups, rows, slots), jnp.bfloat16),
-        input_output_aliases={n + 4: 0} if extra else {},
+        input_output_aliases={n + 3: 0} if extra else {},
         compiler_params=pltpu.CompilerParams(vmem_limit_bytes=VMEM_LIMIT),
         cost_estimate=pl.CostEstimate(flops=UNPACK_FLOPS, bytes_accessed=6 * rows * slots, transcendentals=0),
         name="unpack",
-    )(ranks, most, *[vmem(a) for a in arrays], scale, rest, *extra)
+    )(ranks, samples, *[vmem(a) for a in arrays], rest, *extra)
 
 
 def pick(mine, other):
@@ -171,15 +181,17 @@
 
     def kernel(mine_ref, other_ref, out_ref):
         core = lax.axis_index("row") % 2
-        out_ref[pl.ds(pl.multiple_of(core * rows, rows), rows)] = mine_ref[...]
-        out_ref[pl.ds(pl.multiple_of((1 - core) * rows, rows), rows)] = other_ref[...]
+        for n in range(columns // 2 // CHUNK):
+            cols = slice(n * CHUNK, (n + 1) * CHUNK)
+            out_ref[n, pl.ds(pl.multiple_of(core * rows, rows), rows)] = mine_ref[:, cols]
+            out_ref[n, pl.ds(pl.multiple_of((1 - core) * rows, rows), rows)] = other_ref[:, cols]
 
     return pl.pallas_call(
         kernel,
         grid=(1,),
         in_specs=[pl.BlockSpec((rows, columns // 2), lambda i: (0, lax.axis_index("row") % 2))] * 2,
-        out_specs=pl.BlockSpec((2 * rows, columns // 2), lambda i: (0, 0)),
-        out_shape=jax.ShapeDtypeStruct((2 * rows, columns // 2), mine.dtype),
+        out_specs=pl.BlockSpec((columns // 2 // CHUNK, 2 * rows, CHUNK), lambda i: (0, 0, 0)),
+        out_shape=jax.ShapeDtypeStruct((columns // 2 // CHUNK, 2 * rows, CHUNK), mine.dtype),
         compiler_params=pltpu.CompilerParams(vmem_limit_bytes=VMEM_LIMIT),
         cost_estimate=pl.CostEstimate(flops=0, bytes_accessed=4 * rows * columns, transcendentals=0),
         name="pick",
@@ -187,13 +199,13 @@
 
 
 def halves(upper_of, lower_of):
-    rows, columns = upper_of.shape
+    chunks, rows, columns = upper_of.shape
     half = rows // 2
 
     def kernel(a_ref, b_ref, upper_ref, lower_ref, sem):
         copies = [
-            pltpu.make_async_copy(a_ref.at[pl.ds(0, half)], upper_ref, sem.at[0]),
-            pltpu.make_async_copy(b_ref.at[pl.ds(half, half)], lower_ref, sem.at[1]),
+            pltpu.make_async_copy(a_ref.at[:, pl.ds(0, half)], upper_ref, sem.at[0]),
+            pltpu.make_async_copy(b_ref.at[:, pl.ds(half, half)], lower_ref, sem.at[1]),
         ]
         for copy in copies:
             copy.start()
@@ -204,7 +216,7 @@
         kernel,
         in_specs=[pl.BlockSpec(memory_space=pl.ANY)] * 2,
         out_specs=[pl.BlockSpec(memory_space=pl.ANY)] * 2,
-        out_shape=[jax.ShapeDtypeStruct((half, columns), upper_of.dtype)] * 2,
+        out_shape=[jax.ShapeDtypeStruct((chunks, half, columns), upper_of.dtype)] * 2,
         scratch_shapes=[pltpu.SemaphoreType.DMA((2,))],
         compiler_params=pltpu.CompilerParams(vmem_limit_bytes=VMEM_LIMIT),
         cost_estimate=pl.CostEstimate(flops=0, bytes_accessed=4 * rows * columns, transcendentals=0),
@@ -213,19 +225,19 @@
 
 
 def line_up(pieces):
-    rows, columns = pieces[0].shape
+    chunks, rows, columns = pieces[0].shape
 
     def kernel(*refs):
         x, z, core = torus_place()
         at = jnp.where(core == 0, x, z)
         for i in range(4):
-            refs[4][pl.ds(pl.multiple_of(near(at, i) * rows, rows), rows)] = refs[i][...]
-
-    return pl.pallas_call(
-        kernel,
-        out_shape=jax.ShapeDtypeStruct((4 * rows, columns), pieces[0].dtype),
-        compiler_params=pltpu.CompilerParams(vmem_limit_bytes=VMEM_LIMIT),
-        cost_estimate=pl.CostEstimate(flops=0, bytes_accessed=16 * rows * columns, transcendentals=0),
+            refs[4][:, pl.ds(pl.multiple_of(near(at, (3, 1, 2, 0)[i]) * rows, rows), rows)] = refs[i][...]
+
+    return pl.pallas_call(
+        kernel,
+        out_shape=jax.ShapeDtypeStruct((chunks, 4 * rows, columns), pieces[0].dtype),
+        compiler_params=pltpu.CompilerParams(vmem_limit_bytes=VMEM_LIMIT),
+        cost_estimate=pl.CostEstimate(flops=0, bytes_accessed=16 * chunks * rows * columns, transcendentals=0),
         name="line_up",
     )(*pieces)
 
@@ -248,7 +260,7 @@
         copies = []
         row = 0
         for j, (line, count) in enumerate(where):
-            copies.append(pltpu.make_async_copy(line.at[:, pl.ds(at, width)], d_v.at[pl.ds(row, count)], d_sem.at[j]))
+            copies.append(pltpu.make_async_copy(line.at[at // width], d_v.at[pl.ds(row, count)], d_sem.at[j]))
             row += count
         base_at = pl.ds(pl.multiple_of(half() * (features // 2) + at, width), width)
         copies.append(pltpu.make_async_copy(base_ref.at[:, base_at], base_v, base_sem))
@@ -289,34 +301,34 @@
     )(pltpu.with_memory_space_constraint(ups, pltpu.VMEM), *lines, base)
 
 
-def place(pieces, features):
-    part = pieces[0][0].shape[0]
-    count = len(pieces[0])
-    flat = [a for row in pieces for a in row]
-    starts = [(theirs, at, width) for theirs in (False, True) for at, width in CHUNKS[theirs]]
+def place(out, pieces, chunk, features):
+    part, width = pieces[0].shape
+    theirs, at = chunk
+
+    def block(n):
+        core = lax.axis_index("row") % 2
+        half = 1 - core if theirs else core
+        return n * (features // 4 // width) + half * (features // 8 // width) + at // width
 
     def kernel(*refs):
-        core = lax.axis_index("row") % 2
-        n = pl.program_id(0)
         for i in range(4):
 
-            @pl.when(near(lax.axis_index("col"), i) == n)
+            @pl.when(near(lax.axis_index("col"), (3, 1, 2, 0)[i]) == pl.program_id(0))
             def _(i=i):
-                for j, (theirs, at, width) in enumerate(starts):
-                    half = 1 - core if theirs else core
-                    cols = pl.ds(pl.multiple_of(half * (features // 8) + at, 128), width)
-                    refs[-1][:, cols] = refs[i * count + j][...]
-
+                refs[-1][...] = refs[i][...]
+
+    extra = [] if out is None else [out]
     return pl.pallas_call(
         kernel,
         grid=(4,),
-        in_specs=[pl.BlockSpec(a.shape, lambda n: (0, 0)) for a in flat],
-        out_specs=pl.BlockSpec((part, features // 4), lambda n: (0, n)),
+        in_specs=[pl.BlockSpec((part, width), lambda n: (0, 0))] * 4 + [pl.BlockSpec(memory_space=pl.ANY)] * len(extra),
+        out_specs=pl.BlockSpec((part, width), lambda n: (0, block(n))),
         out_shape=jax.ShapeDtypeStruct((part, features), jnp.bfloat16),
-        compiler_params=pltpu.CompilerParams(vmem_limit_bytes=VMEM_LIMIT),
-        cost_estimate=pl.CostEstimate(flops=0, bytes_accessed=4 * part * features, transcendentals=0),
+        input_output_aliases={4: 0} if extra else {},
+        compiler_params=pltpu.CompilerParams(vmem_limit_bytes=VMEM_LIMIT),
+        cost_estimate=pl.CostEstimate(flops=0, bytes_accessed=16 * part * width, transcendentals=0),
         name="place",
-    )(*flat)
+    )(*pieces, *extra)
 
 
 def ring(step):
@@ -352,34 +364,31 @@
 
     left_top = lax.ppermute(top, "col", ring(1))
     right_bottom = lax.ppermute(bottom, "col", ring(3))
+    def send_rest(up, ranks):
+        own = jnp.concatenate(pack(up, ranks, WIDTH, slots - WIDTH))
+        return jnp.concatenate([lax.ppermute(own, "col", ring(k)) for k in (1, 3, 2)], axis=1)
+
+    def no_rest(up, ranks):
+        return jnp.zeros((rows, 3 * (slots - WIDTH)), jnp.bfloat16)
+
+    most = jnp.max(jnp.sum(ranks.reshape(4, -1), axis=1))
+    rest = lax.cond(most > WIDTH, send_rest, no_rest, up, ranks)
+    ups = unpack(None, [(up, 0, 0, 0, rows)], rest, ranks, samples, slots)
+    mine, ups = lax.optimization_barrier((mine, ups))
     piece_far = lax.ppermute(mine, "row", torus(2, True))
     piece_left = lax.ppermute(mine, "row", torus(1, True))
     piece_right = lax.ppermute(mine, "row", torus(3, True))
-
-    most = jnp.max(jnp.sum(ranks.reshape(4, -1), axis=1))
-
-    def send_rest(up, ranks):
-        own = jnp.concatenate(pack(up, ranks, WIDTH, slots - WIDTH))
-        return jnp.concatenate([lax.ppermute(own, "col", ring(k)) for k in (1, 3, 2)], axis=1)
-
-    def no_rest(up, ranks):
-        return jnp.zeros((rows, 3 * (slots - WIDTH)), jnp.bfloat16)
-
-    rest = lax.cond(most > WIDTH, send_rest, no_rest, up, ranks)
-    most = most.reshape(1)
-    scale = slot_scale(ranks, samples).reshape(4, 1, slots)
-    ups = unpack(None, [(up, 0, 0, 0, rows)], rest, most, ranks, scale)
-    mine, piece_left, piece_right, piece_far, left_top, right_bottom, top, bottom, ups = lax.optimization_barrier(
-        (mine, piece_left, piece_right, piece_far, left_top, right_bottom, top, bottom, ups)
-    )
-
-    line = line_up([mine, piece_left, piece_right, piece_far])
+    piece_far, piece_left, piece_right, mine, left_top, right_bottom, top, bottom, ups = lax.optimization_barrier(
+        (piece_far, piece_left, piece_right, mine, left_top, right_bottom, top, bottom, ups)
+    )
+
+    line = line_up([piece_far, piece_left, piece_right, mine])
     line_left = lax.ppermute(line, "row", torus(1, False))
     line_right = lax.ppermute(line, "row", torus(3, False))
     from_left = lax.ppermute(jnp.concatenate([bottom, left_top[:EARLY]]), "col", ring(1))
     from_right = lax.ppermute(jnp.concatenate([top, right_bottom[:EARLY]]), "col", ring(3))
     line_there = lax.ppermute(line, "row", SWAP)
-    ups = unpack(ups, [(left_top, 0, 1, 0, half), (right_bottom, 0, 2, half, half)], rest, most, ranks, scale)
+    ups = unpack(ups, [(left_top, 0, 1, 0, half), (right_bottom, 0, 2, half, half)], rest, ranks, samples, slots)
     line, line_left, line_right, from_left, from_right, line_there, left_top, right_bottom, ups = (
         lax.optimization_barrier(
             (line, line_left, line_right, from_left, from_right, line_there, left_top, right_bottom, ups)
@@ -399,7 +408,7 @@
             (from_left, half, 3, 0, EARLY),
             (from_right, half, 3, half, EARLY),
         ],
-        rest, most, ranks, scale,
+        rest, ranks, samples, slots,
     )
     *line_far, late_left, late_right, left_there, ups = lax.optimization_barrier(
         (*line_far, late_left, late_right, left_there, ups)
@@ -407,23 +416,23 @@
     ups = unpack(
         ups,
         [(late_left, 0, 3, EARLY, half - EARLY), (late_right, 0, 3, half + EARLY, half - EARLY)],
-        rest, most, ranks, scale,
+        rest, ranks, samples, slots,
     )
     lines = [line, line_left, line_right, *line_far]
     other_lines = [line_there, left_there] + [lax.ppermute(a, "row", SWAP) for a in lines[2:]]
 
-    pieces = [[], [], [], []]
+    out, first = None, True
     for theirs, from_lines in ((False, lines), (True, other_lines)):
         for at, width in CHUNKS[theirs]:
-            if len(pieces[0]) == 1:
+            if not first and not theirs:
                 ups, *other_lines[2:] = lax.optimization_barrier((ups, *other_lines[2:]))
+            first = False
             own, to_left, to_right, to_far = merge(ups, from_lines, base, theirs, at, width)
             from_far = lax.ppermute(to_far, "col", ring(2))
             from_left = lax.ppermute(to_right, "col", ring(1))
             from_right = lax.ppermute(to_left, "col", ring(3))
-            for row, piece in zip(pieces, (own, from_left, from_right, from_far)):
-                row.append(piece)
-    return place(pieces, 4 * features)
+            out = place(out, [from_far, from_left, from_right, own], (theirs, at), 4 * features)
+    return out
 
 
 def solution(mesh):

time: 139 us -> 130 us (0.935)
  waiting for transfers between devices: 53.9 us -> 49 us
  other arithmetic: 3.49 us -> 0.88 us
  starting transfers between devices: 39.5 us -> 37.6 us
    ppermute x4, waiting for transfers between devices: 13.9 us -> 6.97 us  [shards(): from_right = lax.ppermute(to_left, 'col', ring(3))]
    ppermute x1, waiting for transfers between devices: 5.92 us -> 0.01 us  [shards(): left_top = lax.ppermute(top, 'col', ring(1))]
    ppermute x1, waiting for transfers between devices: 5.2 us -> 0.13 us  [shards(): piece_right = lax.ppermute(mine, 'row', torus(3, True))]
    ppermute x1, waiting for transfers between devices: 1.49 us -> 5.51 us  [shards(): piece_left = lax.ppermute(mine, 'row', torus(1, True))]
    pallas_call x2 -> x5, Pallas kernels: 2.48 us -> 6.38 us  [the longest x4 6.21 us: place(): pl.pallas_call(kernel, grid=(4,), in_specs=[pl.BlockSpec((part, width), l...]
    ppermute x1, waiting for transfers between devices: 2.67 us -> 6.09 us  [shards(): late_left = lax.ppermute(left_top[EARLY:], 'col', ring(1))]
    ppermute x1, starting transfers between devices: 0.96 us -> 4.11 us  [shards(): line_right = lax.ppermute(line, 'row', torus(3, False))]
    ppermute x1, waiting for transfers between devices: 1.41 us -> 4.53 us  [shards(): piece_far = lax.ppermute(mine, 'row', torus(2, True))]
  transfers between devices with their start and end apart: 31 -> 31, of which waited for: 11 -> 11; matrix products, arithmetic and copies ran while one was open for 4% -> 1% of each run, Pallas kernels for 27% -> 30%
where the time goes in v2:
time: 130 us; the launch traced here: 129 us
  waiting for transfers between devices  49 us (38%)
  Pallas kernels  40 us (31%)
  starting transfers between devices  37.6 us (29%)
    pallas_call x4, Pallas kernels, merge(): pl.pallas_call(kernel, grid=(1,), in_specs=[pl.BlockSpec(memory_space=plt...  19.4 us
    ppermute x1, waiting for transfers between devices, shards(): lax.ppermute(jnp.concatenate([top, right_bottom[:EARLY]]), 'col', ring(3))  18 us
    pallas_call x4, Pallas kernels, unpack(): pl.pallas_call(kernel, grid_spec=pltpu.PrefetchScalarGridSpec(num_scalar_...  9.81 us
    ppermute x4, waiting for transfers between devices, shards(): from_right = lax.ppermute(to_left, 'col', ring(3))  6.97 us
    ppermute x4, starting transfers between devices, shards(): from_far = lax.ppermute(to_far, 'col', ring(2))  6.71 us
    pallas_call x4, Pallas kernels, place(): pl.pallas_call(kernel, grid=(4,), in_specs=[pl.BlockSpec((part, width), l...  6.21 us
    ppermute x1, waiting for transfers between devices, shards(): late_left = lax.ppermute(left_top[EARLY:], 'col', ring(1))  6.09 us
    ppermute x4, starting transfers between devices, shards(): from_left = lax.ppermute(to_right, 'col', ring(1))  5.92 us
  transfers between devices with their start and end apart: 31, of which 11 were waited for; matrix products, arithmetic and copies ran while one was open for 1% of the time, Pallas kernels for 30%

profile of v2, /device:TPU:24, one launch (start us, length us, event | category | flops | bytes accessed | tf_op | source)
XLA Modules:
  0.0 129.3 jit_solution(6545959366571163693)
XLA Ops:
  0.0 0.7 reshape.3
  0.7 0.1 reduce_sum.9
  0.9 0.6 reduce_max.9
  2.2 0.1 conditional.1
  2.2 0.1 broadcast.2
  2.3 0.0 copy-start.2
  2.3 0.0 copy-start.1
  2.3 0.0 copy-start.3
  2.3 0.0 copy-start.4
  2.3 4.2 %pack.3 = (bf16[448,768]{1,0:T(8,128)(2,1)S(1)}, bf16[448,768]{1,0:T(8,128)(2,1)S(1)}) custom-call(s32[64]{0:T(128)} %ranks_ref.9, bf16[896,1024]{1,0:T(8,128)(2,1)} %refs_0_.1), custom_call_target="tpu_custom_call" | custom-call | flops 1409286144 | bytes 3670016 | tf_op jit(solution)/shard_map/pack/pallas_call | solution.py:85
  6.5 0.1 pick.1.refs_3_
  6.6 0.2 collective-permute-start.7
  6.8 1.9 %collective-permute-start.8 = (bf16[448,768]{1,0:T(8,128)(2,1)S(1)}, bf16[448,768]{1,0:T(8,128)(2,1)S(1)}, u32[]{:S(2)}, u32[]{:S(2)}) collective-permute-start(bf16[448,768]{1,0:T(8,128)(2,1)S(1)} %get-tuple-element.80), channel_id=1, source_target_pairs={{0,3},{1,0},{2,1},{3,2},{4,7},{5,4},{6,5},{7,6},{8,11},{9,8},{10,9... | collective-permute-start | bytes 2064392 | tf_op jit(solution)/shard_map/ppermute | solution.py:366
  8.7 1.2 unpack.4.refs_3_
  9.9 3.1 %collective-permute-start.4 = (bf16[2,256,512]{2,1,0:T(8,128)(2,1)S(1)}, bf16[2,256,512]{2,1,0:T(8,128)(2,1)S(1)}, u32[]{:S(2)}, u32[]{:S(2)}) collective-permute-start(bf16[2,256,512]{2,1,0:T(8,128)(2,1)S(1)} %pick.1.refs_3_), channel_id=1, source_target_pairs={{0,64},{4,20},{8,72},{12,28},{16,80},{20,4},{24,88},{28,12},{32,96... | collective-permute-start | bytes 1572872 | tf_op jit(solution)/shard_map/ppermute | solution.py:378
  13.0 0.6 collective-permute-start.5
  13.6 2.6 %collective-permute-start.6 = (bf16[2,256,512]{2,1,0:T(8,128)(2,1)S(1)}, bf16[2,256,512]{2,1,0:T(8,128)(2,1)S(1)}, u32[]{:S(2)}, u32[]{:S(2)}) collective-permute-start(bf16[2,256,512]{2,1,0:T(8,128)(2,1)S(1)} %pick.1.refs_3_), channel_id=1, source_target_pairs={{0,96},{4,28},{8,104},{12,4},{16,112},{20,12},{24,120},{28,20},{32... | collective-permute-start | bytes 1572872 | tf_op jit(solution)/shard_map/ppermute | solution.py:380
  16.3 4.5 %collective-permute-done.4.refs_0_ = bf16[2,256,512]{2,1,0:T(8,128)(2,1)S(1)} collective-permute-done((bf16[2,256,512]{2,1,0:T(8,128)(2,1)S(1)}, bf16[2,256,512]{2,1,0:T(8,128)(2,1)S(1)}, u32[]{:S(2)}, u32[]{:S(2)}) %collective-permute-start.4) | collective-permute-done | bytes 524320 | tf_op jit(solution)/shard_map/ppermute | solution.py:378
  20.8 5.5 %collective-permute-done.5.refs_1_ = bf16[2,256,512]{2,1,0:T(8,128)(2,1)S(1)} collective-permute-done((bf16[2,256,512]{2,1,0:T(8,128)(2,1)S(1)}, bf16[2,256,512]{2,1,0:T(8,128)(2,1)S(1)}, u32[]{:S(2)}, u32[]{:S(2)}) %collective-permute-start.5) | collective-permute-done | bytes 524320 | tf_op jit(solution)/shard_map/ppermute | solution.py:379
  26.3 0.1 collective-permute-done.6.refs_2_
  26.4 0.2 line_up.1.l0
  26.6 4.1 %collective-permute-start.10 = (bf16[2,1024,512]{2,1,0:T(8,128)(2,1)S(1)}, bf16[2,1024,512]{2,1,0:T(8,128)(2,1)S(1)}, u32[]{:S(2)}, u32[]{:S(2)}) collective-permute-start(bf16[2,1024,512]{2,1,0:T(8,128)(2,1)S(1)} %line_up.1.l0), channel_id=1, source_target_pairs={{0,24},{4,100},{8,0},{12,108},{16,8},{20,116},{24,16},{28,124},{32... | collective-permute-start | bytes 6291464 | tf_op jit(solution)/shard_map/ppermute | solution.py:387
  30.8 0.1 pad_maximum_fusion.2
  30.8 0.8 collective-permute-start.12
  31.7 0.1 pad_maximum_fusion.1
  31.7 2.6 %collective-permute-start.11 = (bf16[608,768]{1,0:T(8,128)(2,1)S(1)}, bf16[608,768]{1,0:T(8,128)(2,1)S(1)}, u32[]{:S(2)}, u32[]{:S(2)}) collective-permute-start(bf16[608,768]{1,0:T(8,128)(2,1)S(1)} %pad_maximum_fusion.1), channel_id=1, source_target_pairs={{0,1},{1,2},{2,3},{3,0},{4,5},{5,6},{6,7},{7,4},{8,9},{9,10},{10,1... | collective-permute-start | bytes 2801672 | tf_op jit(solution)/shard_map/ppermute | solution.py:388
  34.3 2.8 %unpack.5.refs_3_ = bf16[8,896,1024]{2,1,0:T(8,128)(2,1)S(1)} custom-call(s32[64]{0:T(128)S(1)} %copy-done.4, s32[64]{0:T(128)S(1)} %copy-done.3, bf16[448,768]{1,0:T(8,128)(2,1)S(1)} %collective-permute-done.7.refs_0_, bf16[448,768]{1,0:T(8,128)(2,1)S(1)} %collective-permute-done.8.refs_1_, ...), custom_call_target="tpu_custom_call", output_to_operand_aliasing={{}: (5, {})} | custom-call | flops 30000001024 | bytes 5505024 | tf_op jit(solution)/shard_map/unpack/pallas_call | solution.py:162
  37.1 18.0 %collective-permute-done.12.refs_1_ = bf16[608,768]{1,0:T(8,128)(2,1)S(1)} collective-permute-done((bf16[608,768]{1,0:T(8,128)(2,1)S(1)}, bf16[608,768]{1,0:T(8,128)(2,1)S(1)}, u32[]{:S(2)}, u32[]{:S(2)}) %collective-permute-start.12) | collective-permute-done | bytes 933920 | tf_op jit(solution)/shard_map/ppermute | solution.py:389
  55.0 0.0 collective-permute-done.11.refs_0_
  55.1 2.9 %collective-permute-done.9.a_ref.l1 = bf16[2,1024,512]{2,1,0:T(8,128)(2,1)S(1)} collective-permute-done((bf16[2,1024,512]{2,1,0:T(8,128)(2,1)S(1)}, bf16[2,1024,512]{2,1,0:T(8,128)(2,1)S(1)}, u32[]{:S(2)}, u32[]{:S(2)}) %collective-permute-start.9) | collective-permute-done | bytes 2097184 | tf_op jit(solution)/shard_map/ppermute | solution.py:386
  58.0 0.2 halves.1
  58.2 0.3 collective-permute-start.14
  58.4 3.2 %collective-permute-start.15 = (bf16[2,512,512]{2,1,0:T(8,128)(2,1)S(1)}, bf16[2,512,512]{2,1,0:T(8,128)(2,1)S(1)}, u32[]{:S(2)}, u32[]{:S(2)}) collective-permute-start(bf16[2,512,512]{2,1,0:T(8,128)(2,1)S(1)} %get-tuple-element.88), channel_id=1, source_target_pairs={{0,24},{4,100},{8,0},{12,108},{16,8},{20,116},{24,16},{28,124},{32... | collective-permute-start | bytes 3145736 | tf_op jit(solution)/shard_map/ppermute | solution.py:399
  61.7 1.5 %collective-permute-start.16 = (bf16[288,768]{1,0:T(8,128)(2,1)S(1)}, bf16[288,768]{1,0:T(8,128)(2,1)S(1)}, u32[]{:S(2)}, u32[]{:S(2)}) collective-permute-start(bf16[288,768]{1,0:T(8,128)(2,1)S(1)} %slice.14), channel_id=1, source_target_pairs={{0,1},{1,2},{2,3},{3,0},{4,5},{5,6},{6,7},{7,4},{8,9},{9,10},{10,1... | collective-permute-start | bytes 1327112 | tf_op jit(solution)/shard_map/ppermute | solution.py:400
  63.2 0.7 collective-permute-start.17
  63.9 3.8 %unpack.6.refs_3_ = bf16[8,896,1024]{2,1,0:T(8,128)(2,1)S(1)} custom-call(s32[64]{0:T(128)S(1)} %copy-done.4, s32[64]{0:T(128)S(1)} %copy-done.3, bf16[608,768]{1,0:T(8,128)(2,1)S(1)} %collective-permute-done.11.refs_0_, bf16[608,768]{1,0:T(8,128)(2,1)S(1)} %collective-permute-done.12.refs_1_, ...), custom_call_target="tpu_custom_call", output_to_operand_aliasing={{}: (5, {})} | custom-call | flops 30000001024 | bytes 5505024 | tf_op jit(solution)/shard_map/unpack/pallas_call | solution.py:162
  67.7 6.1 %collective-permute-done.16.refs_0_ = bf16[288,768]{1,0:T(8,128)(2,1)S(1)} collective-permute-done((bf16[288,768]{1,0:T(8,128)(2,1)S(1)}, bf16[288,768]{1,0:T(8,128)(2,1)S(1)}, u32[]{:S(2)}, u32[]{:S(2)}) %collective-permute-start.16) | collective-permute-done | bytes 442400 | tf_op jit(solution)/shard_map/ppermute | solution.py:400
  73.8 2.5 %collective-permute-done.17.refs_1_ = bf16[288,768]{1,0:T(8,128)(2,1)S(1)} collective-permute-done((bf16[288,768]{1,0:T(8,128)(2,1)S(1)}, bf16[288,768]{1,0:T(8,128)(2,1)S(1)}, u32[]{:S(2)}, u32[]{:S(2)}) %collective-permute-start.17) | collective-permute-done | bytes 442400 | tf_op jit(solution)/shard_map/ppermute | solution.py:401
  76.2 0.1 collective-permute-start.20
  76.3 0.5 collective-permute-start.21
  76.8 2.0 %unpack.7.ups_ref = bf16[8,896,1024]{2,1,0:T(8,128)(2,1)S(1)} custom-call(s32[64]{0:T(128)S(1)} %copy-done.4, s32[64]{0:T(128)S(1)} %copy-done.3, bf16[288,768]{1,0:T(8,128)(2,1)S(1)} %collective-permute-done.16.refs_0_, bf16[288,768]{1,0:T(8,128)(2,1)S(1)} %collective-permute-done.17.refs_1_, ...), custom_call_target="tpu_custom_call", output_to_operand_aliasing={{}: (5, {})} | custom-call | flops 30000001024 | bytes 5505024 | tf_op jit(solution)/shard_map/unpack/pallas_call | solution.py:162
  78.9 4.9 %merge.7 = (bf16[224,512]{1,0:T(8,128)(2,1)S(1)}, bf16[224,512]{1,0:T(8,128)(2,1)S(1)}, bf16[224,512]{1,0:T(8,128)(2,1)S(1)}, bf16[224,512]{1,0:T(8,128)(2,1)S(1)}) custom-call(bf16[8,896,1024]{2,1,0:T(8,128)(2,1)S(1)} %unpack.7.ups_ref, bf16[2,1024,512]{2,1,0:T(8,128)(2,1)S(1)} %line_up.1.l0, bf16[2,1024,512]{2,1,0:T(8,128)(2,1)S(1)} %collective-permute-done.9.a_ref.l1, ...), custom_call_target="tpu_custom_call" | custom-call | flops 3758096384 | bytes 1835008 | tf_op jit(solution)/shard_map/merge/pallas_call | solution.py:285
  83.8 0.2 collective-permute-start.31
  84.0 1.9 %collective-permute-start.32 = (bf16[224,512]{1,0:T(8,128)(2,1)S(1)}, bf16[224,512]{1,0:T(8,128)(2,1)S(1)}, u32[]{:S(2)}, u32[]{:S(2)}) collective-permute-start(bf16[224,512]{1,0:T(8,128)(2,1)S(1)} %get-tuple-element.119), channel_id=1, source_target_pairs={{0,1},{1,2},{2,3},{3,0},{4,5},{5,6},{6,7},{7,4},{8,9},{9,10},{10,1... | collective-permute-start | bytes 688136 | tf_op jit(solution)/shard_map/ppermute | solution.py:432
  85.9 0.1 collective-permute-start.33
  86.0 4.8 %merge.6 = (bf16[224,512]{1,0:T(8,128)(2,1)S(1)}, bf16[224,512]{1,0:T(8,128)(2,1)S(1)}, bf16[224,512]{1,0:T(8,128)(2,1)S(1)}, bf16[224,512]{1,0:T(8,128)(2,1)S(1)}) custom-call(bf16[8,896,1024]{2,1,0:T(8,128)(2,1)S(1)} %unpack.7.ups_ref, bf16[2,1024,512]{2,1,0:T(8,128)(2,1)S(1)} %line_up.1.l0, bf16[2,1024,512]{2,1,0:T(8,128)(2,1)S(1)} %collective-permute-done.9.a_ref.l1, ...), custom_call_target="tpu_custom_call" | custom-call | flops 3758096384 | bytes 1835008 | tf_op jit(solution)/shard_map/merge/pallas_call | solution.py:285
  90.9 3.5 %collective-permute-start.28 = (bf16[224,512]{1,0:T(8,128)(2,1)S(1)}, bf16[224,512]{1,0:T(8,128)(2,1)S(1)}, u32[]{:S(2)}, u32[]{:S(2)}) collective-permute-start(bf16[224,512]{1,0:T(8,128)(2,1)S(1)} %get-tuple-element.114), channel_id=1, source_target_pairs={{0,2},{1,3},{2,0},{3,1},{4,6},{5,7},{6,4},{7,5},{8,10},{9,11},{10,... | collective-permute-start | bytes 688136 | tf_op jit(solution)/shard_map/ppermute | solution.py:431
  94.3 0.6 collective-permute-start.29
  95.0 4.8 %merge.5 = (bf16[224,512]{1,0:T(8,128)(2,1)S(1)}, bf16[224,512]{1,0:T(8,128)(2,1)S(1)}, bf16[224,512]{1,0:T(8,128)(2,1)S(1)}, bf16[224,512]{1,0:T(8,128)(2,1)S(1)}) custom-call(bf16[8,896,1024]{2,1,0:T(8,128)(2,1)S(1)} %unpack.7.ups_ref, bf16[2,1024,512]{2,1,0:T(8,128)(2,1)S(1)} %collective-permute-done.13.l0, ...), custom_call_target="tpu_custom_call" | custom-call | flops 3758096384 | bytes 1835008 | tf_op jit(solution)/shard_map/merge/pallas_call | solution.py:285
  99.8 1.5 %collective-permute-start.30 = (bf16[224,512]{1,0:T(8,128)(2,1)S(1)}, bf16[224,512]{1,0:T(8,128)(2,1)S(1)}, u32[]{:S(2)}, u32[]{:S(2)}) collective-permute-start(bf16[224,512]{1,0:T(8,128)(2,1)S(1)} %get-tuple-element.116), channel_id=1, source_target_pairs={{0,3},{1,0},{2,1},{3,2},{4,7},{5,4},{6,5},{7,6},{8,11},{9,8},{10,9... | collective-permute-start | bytes 688136 | tf_op jit(solution)/shard_map/ppermute | solution.py:433
  101.3 0.7 collective-permute-start.25
  102.0 4.8 %merge.4 = (bf16[224,512]{1,0:T(8,128)(2,1)S(1)}, bf16[224,512]{1,0:T(8,128)(2,1)S(1)}, bf16[224,512]{1,0:T(8,128)(2,1)S(1)}, bf16[224,512]{1,0:T(8,128)(2,1)S(1)}) custom-call(bf16[8,896,1024]{2,1,0:T(8,128)(2,1)S(1)} %unpack.7.ups_ref, bf16[2,1024,512]{2,1,0:T(8,128)(2,1)S(1)} %collective-permute-done.13.l0, ...), custom_call_target="tpu_custom_call" | custom-call | flops 3758096384 | bytes 1835008 | tf_op jit(solution)/shard_map/merge/pallas_call | solution.py:285
  106.9 2.6 %collective-permute-start.26 = (bf16[224,512]{1,0:T(8,128)(2,1)S(1)}, bf16[224,512]{1,0:T(8,128)(2,1)S(1)}, u32[]{:S(2)}, u32[]{:S(2)}) collective-permute-start(bf16[224,512]{1,0:T(8,128)(2,1)S(1)} %get-tuple-element.110), channel_id=1, source_target_pairs={{0,1},{1,2},{2,3},{3,0},{4,5},{5,6},{6,7},{7,4},{8,9},{9,10},{10,1... | collective-permute-start | bytes 688136 | tf_op jit(solution)/shard_map/ppermute | solution.py:432
  109.5 2.3 %collective-permute-start.22 = (bf16[224,512]{1,0:T(8,128)(2,1)S(1)}, bf16[224,512]{1,0:T(8,128)(2,1)S(1)}, u32[]{:S(2)}, u32[]{:S(2)}) collective-permute-start(bf16[224,512]{1,0:T(8,128)(2,1)S(1)} %get-tuple-element.105), channel_id=1, source_target_pairs={{0,2},{1,3},{2,0},{3,1},{4,6},{5,7},{6,4},{7,5},{8,10},{9,11},{10,... | collective-permute-start | bytes 688136 | tf_op jit(solution)/shard_map/ppermute | solution.py:431
  111.8 1.0 collective-permute-done.30.refs_2_
  112.8 0.8 collective-permute-start.23
  113.6 1.2 collective-permute-start.24
  114.8 1.6 %place.4.refs_4_ = bf16[224,8192]{1,0:T(8,128)(2,1)} custom-call(bf16[224,512]{1,0:T(8,128)(2,1)S(1)} %collective-permute-done.31.refs_0_, bf16[224,512]{1,0:T(8,128)(2,1)S(1)} %collective-permute-done.32.refs_1_, bf16[224,512]{1,0:T(8,128)(2,1)S(1)} %collective-permute-done.33.refs_2_, bf16[224,512]{1,0:T(8,128)(2,1)S(1)} %get-tuple-element.121.refs_3_), custom_call_target="tpu_custom_call" | custom-call | bytes 1835008 | tf_op jit(solution)/shard_map/place/pallas_call | solution.py:321
  116.4 1.6 %place.5.refs_4_ = bf16[224,8192]{1,0:T(8,128)(2,1)} custom-call(bf16[224,512]{1,0:T(8,128)(2,1)S(1)} %collective-permute-done.28.refs_0_, bf16[224,512]{1,0:T(8,128)(2,1)S(1)} %collective-permute-done.29.refs_1_, bf16[224,512]{1,0:T(8,128)(2,1)S(1)} %collective-permute-done.30.refs_2_, ...), custom_call_target="tpu_custom_call", output_to_operand_aliasing={{}: (4, {})} | custom-call | bytes 1835008 | tf_op jit(solution)/shard_map/place/pallas_call | solution.py:321
  117.9 2.3 %collective-permute-done.26.refs_1_ = bf16[224,512]{1,0:T(8,128)(2,1)S(1)} collective-permute-done((bf16[224,512]{1,0:T(8,128)(2,1)S(1)}, bf16[224,512]{1,0:T(8,128)(2,1)S(1)}, u32[]{:S(2)}, u32[]{:S(2)}) %collective-permute-start.26) | collective-permute-done | bytes 229408 | tf_op jit(solution)/shard_map/ppermute | solution.py:432
  120.2 3.9 %collective-permute-done.27.refs_2_ = bf16[224,512]{1,0:T(8,128)(2,1)S(1)} collective-permute-done((bf16[224,512]{1,0:T(8,128)(2,1)S(1)}, bf16[224,512]{1,0:T(8,128)(2,1)S(1)}, u32[]{:S(2)}, u32[]{:S(2)}) %collective-permute-start.27) | collective-permute-done | bytes 229408 | tf_op jit(solution)/shard_map/ppermute | solution.py:433
  124.1 1.6 %place.6.refs_4_ = bf16[224,8192]{1,0:T(8,128)(2,1)} custom-call(bf16[224,512]{1,0:T(8,128)(2,1)S(1)} %collective-permute-done.25.refs_0_, bf16[224,512]{1,0:T(8,128)(2,1)S(1)} %collective-permute-done.26.refs_1_, bf16[224,512]{1,0:T(8,128)(2,1)S(1)} %collective-permute-done.27.refs_2_, ...), custom_call_target="tpu_custom_call", output_to_operand_aliasing={{}: (4, {})} | custom-call | bytes 1835008 | tf_op jit(solution)/shard_map/place/pallas_call | solution.py:321
  125.7 2.0 %collective-permute-done.24.refs_2_ = bf16[224,512]{1,0:T(8,128)(2,1)S(1)} collective-permute-done((bf16[224,512]{1,0:T(8,128)(2,1)S(1)}, bf16[224,512]{1,0:T(8,128)(2,1)S(1)}, u32[]{:S(2)}, u32[]{:S(2)}) %collective-permute-start.24) | collective-permute-done | bytes 229408 | tf_op jit(solution)/shard_map/ppermute | solution.py:433
  127.8 1.6 %place.7 = bf16[224,8192]{1,0:T(8,128)(2,1)} custom-call(bf16[224,512]{1,0:T(8,128)(2,1)S(1)} %collective-permute-done.22.refs_0_, bf16[224,512]{1,0:T(8,128)(2,1)S(1)} %collective-permute-done.23.refs_1_, bf16[224,512]{1,0:T(8,128)(2,1)S(1)} %collective-permute-done.24.refs_2_, ...), custom_call_target="tpu_custom_call", output_to_operand_aliasing={{}: (4, {})} | custom-call | bytes 1835008 | tf_op jit(solution)/shard_map/place/pallas_call | solution.py:321
  (35 shorter events, 0.2 us)
Async XLA Ops:
  0.0 6.5 %collective-permute-start.3 = (bf16[128,2048]{1,0:T(8,128)(2,1)}, bf16[128,2048]{1,0:T(8,128)(2,1)S(1)}, u32[]{:S(2)}, u32[]{:S(2)}) collective-permute-start(bf16[128,2048]{1,0:T(8,128)(2,1)} %mine_ref.1), channel_id=1, source_target_pairs={{0,4},{4,0},{8,12},{12,8},{16,20},{20,16},{24,28},{28,24},{32,36},... | collective-permute-start | bytes 1572872 | tf_op jit(solution)/shard_map/ppermute | solution.py:362
  2.3 4.3 %copy-start.2 = (bf16[128,2048]{1,0:T(8,128)(2,1)S(1)}, bf16[128,2048]{1,0:T(8,128)(2,1)}, u32[]{:S(2)}) copy-start(bf16[128,2048]{1,0:T(8,128)(2,1)} %mine_ref.1) | copy-start | bytes 1572868
  2.3 6.4 %copy-start.1 = (bf16[896,1024]{1,0:T(8,128)(2,1)S(1)}, bf16[896,1024]{1,0:T(8,128)(2,1)}, u32[]{:S(2)}) copy-start(bf16[896,1024]{1,0:T(8,128)(2,1)} %refs_0_.1) | copy-start | bytes 5505028
  2.3 6.4 %copy-start.3 = (s32[64]{0:T(128)S(1)}, s32[64]{0:T(128)}, u32[]{:S(2)}) copy-start(s32[64]{0:T(128)} %samples_ref.7) | copy-start | bytes 772
  2.3 6.4 %copy-start.4 = (s32[64]{0:T(128)S(1)}, s32[64]{0:T(128)}, u32[]{:S(2)}) copy-start(s32[64]{0:T(128)} %ranks_ref.9) | copy-start | bytes 772
  6.6 19.8 %collective-permute-start.7 = (bf16[448,768]{1,0:T(8,128)(2,1)S(1)}, bf16[448,768]{1,0:T(8,128)(2,1)S(1)}, u32[]{:S(2)}, u32[]{:S(2)}) collective-permute-start(bf16[448,768]{1,0:T(8,128)(2,1)S(1)} %get-tuple-element.82), channel_id=1, source_target_pairs={{0,1},{1,2},{2,3},{3,0},{4,5},{5,6},{6,7},{7,4},{8,9},{9,10},{10,1... | collective-permute-start | bytes 2064392 | tf_op jit(solution)/shard_map/ppermute | solution.py:365
  6.8 19.6 %collective-permute-start.8 = (bf16[448,768]{1,0:T(8,128)(2,1)S(1)}, bf16[448,768]{1,0:T(8,128)(2,1)S(1)}, u32[]{:S(2)}, u32[]{:S(2)}) collective-permute-start(bf16[448,768]{1,0:T(8,128)(2,1)S(1)} %get-tuple-element.80), channel_id=1, source_target_pairs={{0,3},{1,0},{2,1},{3,2},{4,7},{5,4},{6,5},{7,6},{8,11},{9,8},{10,9... | collective-permute-start | bytes 2064392 | tf_op jit(solution)/shard_map/ppermute | solution.py:366
  9.9 10.9 %collective-permute-start.4 = (bf16[2,256,512]{2,1,0:T(8,128)(2,1)S(1)}, bf16[2,256,512]{2,1,0:T(8,128)(2,1)S(1)}, u32[]{:S(2)}, u32[]{:S(2)}) collective-permute-start(bf16[2,256,512]{2,1,0:T(8,128)(2,1)S(1)} %pick.1.refs_3_), channel_id=1, source_target_pairs={{0,64},{4,20},{8,72},{12,28},{16,80},{20,4},{24,88},{28,12},{32,96... | collective-permute-start | bytes 1572872 | tf_op jit(solution)/shard_map/ppermute | solution.py:378
  13.0 13.3 %collective-permute-start.5 = (bf16[2,256,512]{2,1,0:T(8,128)(2,1)S(1)}, bf16[2,256,512]{2,1,0:T(8,128)(2,1)S(1)}, u32[]{:S(2)}, u32[]{:S(2)}) collective-permute-start(bf16[2,256,512]{2,1,0:T(8,128)(2,1)S(1)} %pick.1.refs_3_), channel_id=1, source_target_pairs={{0,32},{4,12},{8,40},{12,20},{16,48},{20,28},{24,56},{28,4},{32,64... | collective-permute-start | bytes 1572872 | tf_op jit(solution)/shard_map/ppermute | solution.py:379
  13.6 12.8 %collective-permute-start.6 = (bf16[2,256,512]{2,1,0:T(8,128)(2,1)S(1)}, bf16[2,256,512]{2,1,0:T(8,128)(2,1)S(1)}, u32[]{:S(2)}, u32[]{:S(2)}) collective-permute-start(bf16[2,256,512]{2,1,0:T(8,128)(2,1)S(1)} %pick.1.refs_3_), channel_id=1, source_target_pairs={{0,96},{4,28},{8,104},{12,4},{16,112},{20,12},{24,120},{28,20},{32... | collective-permute-start | bytes 1572872 | tf_op jit(solution)/shard_map/ppermute | solution.py:380
  26.6 28.4 %collective-permute-start.10 = (bf16[2,1024,512]{2,1,0:T(8,128)(2,1)S(1)}, bf16[2,1024,512]{2,1,0:T(8,128)(2,1)S(1)}, u32[]{:S(2)}, u32[]{:S(2)}) collective-permute-start(bf16[2,1024,512]{2,1,0:T(8,128)(2,1)S(1)} %line_up.1.l0), channel_id=1, source_target_pairs={{0,24},{4,100},{8,0},{12,108},{16,8},{20,116},{24,16},{28,124},{32... | collective-permute-start | bytes 6291464 | tf_op jit(solution)/shard_map/ppermute | solution.py:387
  30.7 24.3 %collective-permute-start.13 = (bf16[2,1024,512]{2,1,0:T(8,128)(2,1)S(1)}, bf16[2,1024,512]{2,1,0:T(8,128)(2,1)S(1)}, u32[]{:S(2)}, u32[]{:S(2)}) collective-permute-start(bf16[2,1024,512]{2,1,0:T(8,128)(2,1)S(1)} %line_up.1.l0), channel_id=1, source_target_pairs={{0,4},{4,0},{8,12},{12,8},{16,20},{20,16},{24,28},{28,24},{32,36},... | collective-permute-start | bytes 6291464 | tf_op jit(solution)/shard_map/ppermute | solution.py:390
  30.7 27.2 %collective-permute-start.9 = (bf16[2,1024,512]{2,1,0:T(8,128)(2,1)S(1)}, bf16[2,1024,512]{2,1,0:T(8,128)(2,1)S(1)}, u32[]{:S(2)}, u32[]{:S(2)}) collective-permute-start(bf16[2,1024,512]{2,1,0:T(8,128)(2,1)S(1)} %line_up.1.l0), channel_id=1, source_target_pairs={{0,8},{4,36},{8,16},{12,44},{16,24},{20,52},{24,0},{28,60},{32,40}... | collective-permute-start | bytes 6291464 | tf_op jit(solution)/shard_map/ppermute | solution.py:386
  30.8 24.2 %collective-permute-start.12 = (bf16[608,768]{1,0:T(8,128)(2,1)S(1)}, bf16[608,768]{1,0:T(8,128)(2,1)S(1)}, u32[]{:S(2)}, u32[]{:S(2)}) collective-permute-start(bf16[608,768]{1,0:T(8,128)(2,1)S(1)} %pad_maximum_fusion.2), channel_id=1, source_target_pairs={{0,3},{1,0},{2,1},{3,2},{4,7},{5,4},{6,5},{7,6},{8,11},{9,8},{10,9... | collective-permute-start | bytes 2801672 | tf_op jit(solution)/shard_map/ppermute | solution.py:389
  31.7 23.3 %collective-permute-start.11 = (bf16[608,768]{1,0:T(8,128)(2,1)S(1)}, bf16[608,768]{1,0:T(8,128)(2,1)S(1)}, u32[]{:S(2)}, u32[]{:S(2)}) collective-permute-start(bf16[608,768]{1,0:T(8,128)(2,1)S(1)} %pad_maximum_fusion.1), channel_id=1, source_target_pairs={{0,1},{1,2},{2,3},{3,0},{4,5},{5,6},{6,7},{7,4},{8,9},{9,10},{10,1... | collective-permute-start | bytes 2801672 | tf_op jit(solution)/shard_map/ppermute | solution.py:388
  58.0 18.3 %collective-permute-start.18 = (bf16[2,1024,512]{2,1,0:T(8,128)(2,1)S(1)}, bf16[2,1024,512]{2,1,0:T(8,128)(2,1)S(1)}, u32[]{:S(2)}, u32[]{:S(2)}) collective-permute-start(bf16[2,1024,512]{2,1,0:T(8,128)(2,1)S(1)} %collective-permute-done.9.a_ref.l1), channel_id=1, source_target_pairs={{0,4},{4,0},{8,12},{12,8},{16,20},{20,16},{24,28},{28,24},{32,36},... | collective-permute-start | bytes 6291464 | tf_op jit(solution)/shard_map/ppermute | solution.py:402
  58.2 18.1 %collective-permute-start.14 = (bf16[2,512,512]{2,1,0:T(8,128)(2,1)S(1)}, bf16[2,512,512]{2,1,0:T(8,128)(2,1)S(1)}, u32[]{:S(2)}, u32[]{:S(2)}) collective-permute-start(bf16[2,512,512]{2,1,0:T(8,128)(2,1)S(1)} %get-tuple-element.87), channel_id=1, source_target_pairs={{0,8},{4,36},{8,16},{12,44},{16,24},{20,52},{24,0},{28,60},{32,40}... | collective-permute-start | bytes 3145736 | tf_op jit(solution)/shard_map/ppermute | solution.py:399
  58.4 17.8 %collective-permute-start.15 = (bf16[2,512,512]{2,1,0:T(8,128)(2,1)S(1)}, bf16[2,512,512]{2,1,0:T(8,128)(2,1)S(1)}, u32[]{:S(2)}, u32[]{:S(2)}) collective-permute-start(bf16[2,512,512]{2,1,0:T(8,128)(2,1)S(1)} %get-tuple-element.88), channel_id=1, source_target_pairs={{0,24},{4,100},{8,0},{12,108},{16,8},{20,116},{24,16},{28,124},{32... | collective-permute-start | bytes 3145736 | tf_op jit(solution)/shard_map/ppermute | solution.py:399
  61.7 12.1 %collective-permute-start.16 = (bf16[288,768]{1,0:T(8,128)(2,1)S(1)}, bf16[288,768]{1,0:T(8,128)(2,1)S(1)}, u32[]{:S(2)}, u32[]{:S(2)}) collective-permute-start(bf16[288,768]{1,0:T(8,128)(2,1)S(1)} %slice.14), channel_id=1, source_target_pairs={{0,1},{1,2},{2,3},{3,0},{4,5},{5,6},{6,7},{7,4},{8,9},{9,10},{10,1... | collective-permute-start | bytes 1327112 | tf_op jit(solution)/shard_map/ppermute | solution.py:400
  63.2 13.0 %collective-permute-start.17 = (bf16[288,768]{1,0:T(8,128)(2,1)S(1)}, bf16[288,768]{1,0:T(8,128)(2,1)S(1)}, u32[]{:S(2)}, u32[]{:S(2)}) collective-permute-start(bf16[288,768]{1,0:T(8,128)(2,1)S(1)} %slice.15), channel_id=1, source_target_pairs={{0,3},{1,0},{2,1},{3,2},{4,7},{5,4},{6,5},{7,6},{8,11},{9,8},{10,9... | collective-permute-start | bytes 1327112 | tf_op jit(solution)/shard_map/ppermute | solution.py:401
  73.8 12.1 %collective-permute-start.19 = (bf16[2,1024,512]{2,1,0:T(8,128)(2,1)S(1)}, bf16[2,1024,512]{2,1,0:T(8,128)(2,1)S(1)}, u32[]{:S(2)}, u32[]{:S(2)}) collective-permute-start(bf16[2,1024,512]{2,1,0:T(8,128)(2,1)S(1)} %collective-permute-done.10.b_ref.l2), channel_id=1, source_target_pairs={{0,4},{4,0},{8,12},{12,8},{16,20},{20,16},{24,28},{28,24},{32,36},... | collective-permute-start | bytes 6291464 | tf_op jit(solution)/shard_map/ppermute | solution.py:422
  76.2 9.8 %collective-permute-start.20 = (bf16[2,512,512]{2,1,0:T(8,128)(2,1)S(1)}, bf16[2,512,512]{2,1,0:T(8,128)(2,1)S(1)}, u32[]{:S(2)}, u32[]{:S(2)}) collective-permute-start(bf16[2,512,512]{2,1,0:T(8,128)(2,1)S(1)} %collective-permute-done.14.l3), channel_id=1, source_target_pairs={{0,4},{4,0},{8,12},{12,8},{16,20},{20,16},{24,28},{28,24},{32,36},... | collective-permute-start | bytes 3145736 | tf_op jit(solution)/shard_map/ppermute | solution.py:422
  76.3 9.7 %collective-permute-start.21 = (bf16[2,512,512]{2,1,0:T(8,128)(2,1)S(1)}, bf16[2,512,512]{2,1,0:T(8,128)(2,1)S(1)}, u32[]{:S(2)}, u32[]{:S(2)}) collective-permute-start(bf16[2,512,512]{2,1,0:T(8,128)(2,1)S(1)} %collective-permute-done.15.l4), channel_id=1, source_target_pairs={{0,4},{4,0},{8,12},{12,8},{16,20},{20,16},{24,28},{28,24},{32,36},... | collective-permute-start | bytes 3145736 | tf_op jit(solution)/shard_map/ppermute | solution.py:422
  76.8 2.1 %copy-start = (bf16[896,2048]{1,0:T(8,128)(2,1)S(1)}, bf16[896,2048]{1,0:T(8,128)(2,1)}, u32[]{:S(2)}) copy-start(bf16[896,2048]{1,0:T(8,128)(2,1)} %base_ref.7) | copy-start | bytes 11010052
  83.8 16.0 %collective-permute-start.31 = (bf16[224,512]{1,0:T(8,128)(2,1)S(1)}, bf16[224,512]{1,0:T(8,128)(2,1)S(1)}, u32[]{:S(2)}, u32[]{:S(2)}) collective-permute-start(bf16[224,512]{1,0:T(8,128)(2,1)S(1)} %get-tuple-element.118), channel_id=1, source_target_pairs={{0,2},{1,3},{2,0},{3,1},{4,6},{5,7},{6,4},{7,5},{8,10},{9,11},{10,... | collective-permute-start | bytes 688136 | tf_op jit(solution)/shard_map/ppermute | solution.py:431
  84.0 17.3 %collective-permute-start.32 = (bf16[224,512]{1,0:T(8,128)(2,1)S(1)}, bf16[224,512]{1,0:T(8,128)(2,1)S(1)}, u32[]{:S(2)}, u32[]{:S(2)}) collective-permute-start(bf16[224,512]{1,0:T(8,128)(2,1)S(1)} %get-tuple-element.119), channel_id=1, source_target_pairs={{0,1},{1,2},{2,3},{3,0},{4,5},{5,6},{6,7},{7,4},{8,9},{9,10},{10,1... | collective-permute-start | bytes 688136 | tf_op jit(solution)/shard_map/ppermute | solution.py:432
  85.9 21.0 %collective-permute-start.33 = (bf16[224,512]{1,0:T(8,128)(2,1)S(1)}, bf16[224,512]{1,0:T(8,128)(2,1)S(1)}, u32[]{:S(2)}, u32[]{:S(2)}) collective-permute-start(bf16[224,512]{1,0:T(8,128)(2,1)S(1)} %get-tuple-element.120), channel_id=1, source_target_pairs={{0,3},{1,0},{2,1},{3,2},{4,7},{5,4},{6,5},{7,6},{8,11},{9,8},{10,9... | collective-permute-start | bytes 688136 | tf_op jit(solution)/shard_map/ppermute | solution.py:433
  90.9 18.6 %collective-permute-start.28 = (bf16[224,512]{1,0:T(8,128)(2,1)S(1)}, bf16[224,512]{1,0:T(8,128)(2,1)S(1)}, u32[]{:S(2)}, u32[]{:S(2)}) collective-permute-start(bf16[224,512]{1,0:T(8,128)(2,1)S(1)} %get-tuple-element.114), channel_id=1, source_target_pairs={{0,2},{1,3},{2,0},{3,1},{4,6},{5,7},{6,4},{7,5},{8,10},{9,11},{10,... | collective-permute-start | bytes 688136 | tf_op jit(solution)/shard_map/ppermute | solution.py:431
  94.3 15.1 %collective-permute-start.29 = (bf16[224,512]{1,0:T(8,128)(2,1)S(1)}, bf16[224,512]{1,0:T(8,128)(2,1)S(1)}, u32[]{:S(2)}, u32[]{:S(2)}) collective-permute-start(bf16[224,512]{1,0:T(8,128)(2,1)S(1)} %get-tuple-element.115), channel_id=1, source_target_pairs={{0,1},{1,2},{2,3},{3,0},{4,5},{5,6},{6,7},{7,4},{8,9},{9,10},{10,1... | collective-permute-start | bytes 688136 | tf_op jit(solution)/shard_map/ppermute | solution.py:432
  99.8 13.0 %collective-permute-start.30 = (bf16[224,512]{1,0:T(8,128)(2,1)S(1)}, bf16[224,512]{1,0:T(8,128)(2,1)S(1)}, u32[]{:S(2)}, u32[]{:S(2)}) collective-permute-start(bf16[224,512]{1,0:T(8,128)(2,1)S(1)} %get-tuple-element.116), channel_id=1, source_target_pairs={{0,3},{1,0},{2,1},{3,2},{4,7},{5,4},{6,5},{7,6},{8,11},{9,8},{10,9... | collective-permute-start | bytes 688136 | tf_op jit(solution)/shard_map/ppermute | solution.py:433
  101.3 12.3 %collective-permute-start.25 = (bf16[224,512]{1,0:T(8,128)(2,1)S(1)}, bf16[224,512]{1,0:T(8,128)(2,1)S(1)}, u32[]{:S(2)}, u32[]{:S(2)}) collective-permute-start(bf16[224,512]{1,0:T(8,128)(2,1)S(1)} %get-tuple-element.109), channel_id=1, source_target_pairs={{0,2},{1,3},{2,0},{3,1},{4,6},{5,7},{6,4},{7,5},{8,10},{9,11},{10,... | collective-permute-start | bytes 688136 | tf_op jit(solution)/shard_map/ppermute | solution.py:431
  106.9 13.4 %collective-permute-start.26 = (bf16[224,512]{1,0:T(8,128)(2,1)S(1)}, bf16[224,512]{1,0:T(8,128)(2,1)S(1)}, u32[]{:S(2)}, u32[]{:S(2)}) collective-permute-start(bf16[224,512]{1,0:T(8,128)(2,1)S(1)} %get-tuple-element.110), channel_id=1, source_target_pairs={{0,1},{1,2},{2,3},{3,0},{4,5},{5,6},{6,7},{7,4},{8,9},{9,10},{10,1... | collective-permute-start | bytes 688136 | tf_op jit(solution)/shard_map/ppermute | solution.py:432
  109.5 14.7 %collective-permute-start.27 = (bf16[224,512]{1,0:T(8,128)(2,1)S(1)}, bf16[224,512]{1,0:T(8,128)(2,1)S(1)}, u32[]{:S(2)}, u32[]{:S(2)}) collective-permute-start(bf16[224,512]{1,0:T(8,128)(2,1)S(1)} %get-tuple-element.111), channel_id=1, source_target_pairs={{0,3},{1,0},{2,1},{3,2},{4,7},{5,4},{6,5},{7,6},{8,11},{9,8},{10,9... | collective-permute-start | bytes 688136 | tf_op jit(solution)/shard_map/ppermute | solution.py:433
  109.5 16.2 %collective-permute-start.22 = (bf16[224,512]{1,0:T(8,128)(2,1)S(1)}, bf16[224,512]{1,0:T(8,128)(2,1)S(1)}, u32[]{:S(2)}, u32[]{:S(2)}) collective-permute-start(bf16[224,512]{1,0:T(8,128)(2,1)S(1)} %get-tuple-element.105), channel_id=1, source_target_pairs={{0,2},{1,3},{2,0},{3,1},{4,6},{5,7},{6,4},{7,5},{8,10},{9,11},{10,... | collective-permute-start | bytes 688136 | tf_op jit(solution)/shard_map/ppermute | solution.py:431
  112.8 12.9 %collective-permute-start.23 = (bf16[224,512]{1,0:T(8,128)(2,1)S(1)}, bf16[224,512]{1,0:T(8,128)(2,1)S(1)}, u32[]{:S(2)}, u32[]{:S(2)}) collective-permute-start(bf16[224,512]{1,0:T(8,128)(2,1)S(1)} %get-tuple-element.106), channel_id=1, source_target_pairs={{0,1},{1,2},{2,3},{3,0},{4,5},{5,6},{6,7},{7,4},{8,9},{9,10},{10,1... | collective-permute-start | bytes 688136 | tf_op jit(solution)/shard_map/ppermute | solution.py:432
  113.6 14.1 %collective-permute-start.24 = (bf16[224,512]{1,0:T(8,128)(2,1)S(1)}, bf16[224,512]{1,0:T(8,128)(2,1)S(1)}, u32[]{:S(2)}, u32[]{:S(2)}) collective-permute-start(bf16[224,512]{1,0:T(8,128)(2,1)S(1)} %get-tuple-element.107), channel_id=1, source_target_pairs={{0,3},{1,0},{2,1},{3,2},{4,7},{5,4},{6,5},{7,6},{8,11},{9,8},{10,9... | collective-permute-start | bytes 688136 | tf_op jit(solution)/shard_map/ppermute | solution.py:433

commit v3 on v2

--- a/solution.py
+++ b/solution.py
@@ -11,7 +11,7 @@
 CHUNK = 512
 CHUNKS = (((0, 512), (512, 512)), ((0, 512), (512, 512)))
 VMEM_LIMIT = 12 * 2**20
-EARLY = 160
+EARLY = 176
 UNPACK_FLOPS = 30 * 10**9
 MERGE_LIMIT = 22 * 2**20
 
@@ -56,17 +56,31 @@
     return jnp.where(row == place, jnp.float32(1.0), jnp.float32(0.0)).astype(jnp.bfloat16), start
 
 
+def most_live(ranks):
+    def kernel(ranks_ref, out_ref):
+        most = jnp.int32(0)
+        for g in range(4):
+            live = jnp.int32(0)
+            for k in range(ranks.shape[0] // 4):
+                live = live + ranks_ref[g * (ranks.shape[0] // 4) + k]
+            most = jnp.maximum(most, live)
+        out_ref[0] = most
+
+    return pl.pallas_call(
+        kernel,
+        in_specs=[pl.BlockSpec(memory_space=pltpu.SMEM)],
+        out_specs=pl.BlockSpec(memory_space=pltpu.SMEM),
+        out_shape=jax.ShapeDtypeStruct((1,), jnp.int32),
+        name="most_live",
+    )(ranks)
+
+
 def pack(up, ranks, first, width):
     rows, slots = up.shape
     half = rows // 2
     clients = slots // RMAX
 
-    def kernel(ranks_ref, up_ref, top_ref, bottom_ref, up_v, hot, sem):
-        copies = []
-        for j in range(2):
-            span = pl.ds(j * half, half)
-            copies.append(pltpu.make_async_copy(up_ref.at[span], up_v.at[span], sem.at[j]))
-            copies[-1].start()
+    def kernel(ranks_ref, up_ref, top_ref, bottom_ref, hot):
         group = lax.axis_index("col")
         m = lax.broadcasted_iota(jnp.int32, (RMAX, width), 0)
         ahead = lax.broadcasted_iota(jnp.int32, (RMAX, width), 1) - m
@@ -77,9 +91,8 @@
             hot[k * RMAX : (k + 1) * RMAX] = jnp.where(here, jnp.float32(1.0), jnp.float32(0.0)).astype(jnp.bfloat16)
             start = start + rank
         for j, out_ref in enumerate((top_ref, bottom_ref)):
-            copies[j].wait()
             out_ref[...] = jnp.dot(
-                up_v[j * half : (j + 1) * half], hot[...], preferred_element_type=jnp.float32
+                up_ref[j * half : (j + 1) * half], hot[...], preferred_element_type=jnp.float32
             ).astype(jnp.bfloat16)
 
     return pl.pallas_call(
@@ -87,19 +100,15 @@
         grid_spec=pltpu.PrefetchScalarGridSpec(
             num_scalar_prefetch=1,
             grid=(1,),
-            in_specs=[pl.BlockSpec(memory_space=pl.ANY)],
+            in_specs=[pl.BlockSpec(memory_space=pltpu.VMEM)],
             out_specs=[pl.BlockSpec((half, width), lambda i, *_: (0, 0))] * 2,
-            scratch_shapes=[
-                pltpu.VMEM((rows, slots), jnp.bfloat16),
-                pltpu.VMEM((slots, width), jnp.bfloat16),
-                pltpu.SemaphoreType.DMA((2,)),
-            ],
+            scratch_shapes=[pltpu.VMEM((slots, width), jnp.bfloat16)],
         ),
         out_shape=[jax.ShapeDtypeStruct((half, width), jnp.bfloat16)] * 2,
         compiler_params=pltpu.CompilerParams(vmem_limit_bytes=VMEM_LIMIT),
         cost_estimate=pl.CostEstimate(flops=2 * rows * slots * width, bytes_accessed=4 * rows * slots, transcendentals=0),
         name="pack",
-    )(ranks, up)
+    )(ranks, pltpu.with_memory_space_constraint(up, pltpu.VMEM))
 
 
 def unpack(ups, items, rest, ranks, samples, slots):
@@ -371,8 +380,7 @@
     def no_rest(up, ranks):
         return jnp.zeros((rows, 3 * (slots - WIDTH)), jnp.bfloat16)
 
-    most = jnp.max(jnp.sum(ranks.reshape(4, -1), axis=1))
-    rest = lax.cond(most > WIDTH, send_rest, no_rest, up, ranks)
+    rest = lax.cond(most_live(ranks)[0] > WIDTH, send_rest, no_rest, up, ranks)
     ups = unpack(None, [(up, 0, 0, 0, rows)], rest, ranks, samples, slots)
     mine, ups = lax.optimization_barrier((mine, ups))
     piece_far = lax.ppermute(mine, "row", torus(2, True))

time: 130 us -> 129 us (level)
    pallas_call x1, Pallas kernels: 4.2 us -> 2.42 us  [pack(): pl.pallas_call(kernel, grid_spec=pltpu.PrefetchScalarGridSpec(num_scalar_...]
    unnamed x10 -> x12, local copies, waits for them, and re-layouts: 0.03 us -> 1.57 us
  transfers between devices with their start and end apart: 31 -> 31, of which waited for: 11 -> 11; matrix products, arithmetic and copies ran while one was open for 1% -> 0% of each run, Pallas kernels for 30% -> 29%
where the time goes in v3:
time: 129 us; the launch traced here: 128 us
  waiting for transfers between devices  48.4 us (38%)
  Pallas kernels  39.3 us (30%)
  starting transfers between devices  37.4 us (29%)
  local copies, waits for them, and re-layouts  1.76 us (1%)
    pallas_call x4, Pallas kernels, merge(): pl.pallas_call(kernel, grid=(1,), in_specs=[pl.BlockSpec(memory_space=plt...  19.3 us
    ppermute x1, waiting for transfers between devices, shards(): lax.ppermute(jnp.concatenate([top, right_bottom[:EARLY]]), 'col', ring(3))  18.5 us
    pallas_call x4, Pallas kernels, unpack(): pl.pallas_call(kernel, grid_spec=pltpu.PrefetchScalarGridSpec(num_scalar_...  9.76 us
    ppermute x4, waiting for transfers between devices, shards(): from_right = lax.ppermute(to_left, 'col', ring(3))  6.95 us
    ppermute x4, starting transfers between devices, shards(): from_far = lax.ppermute(to_far, 'col', ring(2))  6.71 us
    pallas_call x4, Pallas kernels, place(): pl.pallas_call(kernel, grid=(4,), in_specs=[pl.BlockSpec((part, width), l...  6.21 us
    ppermute x4, starting transfers between devices, shards(): from_left = lax.ppermute(to_right, 'col', ring(1))  5.95 us
    ppermute x1, waiting for transfers between devices, shards(): late_left = lax.ppermute(left_top[EARLY:], 'col', ring(1))  5.54 us
  transfers between devices with their start and end apart: 31, of which 11 were waited for; matrix products, arithmetic and copies ran while one was open for 0% of the time, Pallas kernels for 29%

profile of v3, /device:TPU:24, one launch (start us, length us, event | category | flops | bytes accessed | tf_op | source)
XLA Modules:
  0.0 128.0 jit_solution(2773443686876319807)
XLA Ops:
  0.0 1.2 most_live.1
  1.9 0.1 conditional.1
  1.9 0.1 broadcast.2
  2.0 0.0 copy-start.1
  2.0 1.5 %copy-done.1 = bf16[896,1024]{1,0:T(8,128)(2,1)S(1)} copy-done((bf16[896,1024]{1,0:T(8,128)(2,1)S(1)}, bf16[896,1024]{1,0:T(8,128)(2,1)}, u32[]{:S(2)}) %copy-start.1) | copy-done | bytes 1835032
  3.5 2.4 %pack.3 = (bf16[448,768]{1,0:T(8,128)(2,1)S(1)}, bf16[448,768]{1,0:T(8,128)(2,1)S(1)}) custom-call(s32[64]{0:T(128)} %ranks_ref.11, bf16[896,1024]{1,0:T(8,128)(2,1)S(1)} %copy-done.1), custom_call_target="tpu_custom_call" | custom-call | flops 1409286144 | bytes 3670016 | tf_op jit(solution)/shard_map/pack/pallas_call | solution.py:98
  5.9 0.0 collective-permute-done.3.other_ref
  6.0 0.1 pick.1.refs_3_
  6.0 0.2 collective-permute-start.7
  6.2 1.9 %collective-permute-start.8 = (bf16[448,768]{1,0:T(8,128)(2,1)S(1)}, bf16[448,768]{1,0:T(8,128)(2,1)S(1)}, u32[]{:S(2)}, u32[]{:S(2)}) collective-permute-start(bf16[448,768]{1,0:T(8,128)(2,1)S(1)} %get-tuple-element.80), channel_id=1, source_target_pairs={{0,3},{1,0},{2,1},{3,2},{4,7},{5,4},{6,5},{7,6},{8,11},{9,8},{10,9... | collective-permute-start | bytes 2064392 | tf_op jit(solution)/shard_map/ppermute | solution.py:375
  8.1 1.2 unpack.4.refs_3_
  9.3 3.1 %collective-permute-start.4 = (bf16[2,256,512]{2,1,0:T(8,128)(2,1)S(1)}, bf16[2,256,512]{2,1,0:T(8,128)(2,1)S(1)}, u32[]{:S(2)}, u32[]{:S(2)}) collective-permute-start(bf16[2,256,512]{2,1,0:T(8,128)(2,1)S(1)} %pick.1.refs_3_), channel_id=1, source_target_pairs={{0,64},{4,20},{8,72},{12,28},{16,80},{20,4},{24,88},{28,12},{32,96... | collective-permute-start | bytes 1572872 | tf_op jit(solution)/shard_map/ppermute | solution.py:386
  12.4 0.6 collective-permute-start.5
  13.0 2.6 %collective-permute-start.6 = (bf16[2,256,512]{2,1,0:T(8,128)(2,1)S(1)}, bf16[2,256,512]{2,1,0:T(8,128)(2,1)S(1)}, u32[]{:S(2)}, u32[]{:S(2)}) collective-permute-start(bf16[2,256,512]{2,1,0:T(8,128)(2,1)S(1)} %pick.1.refs_3_), channel_id=1, source_target_pairs={{0,96},{4,28},{8,104},{12,4},{16,112},{20,12},{24,120},{28,20},{32... | collective-permute-start | bytes 1572872 | tf_op jit(solution)/shard_map/ppermute | solution.py:388
  15.7 4.5 %collective-permute-done.4.refs_0_ = bf16[2,256,512]{2,1,0:T(8,128)(2,1)S(1)} collective-permute-done((bf16[2,256,512]{2,1,0:T(8,128)(2,1)S(1)}, bf16[2,256,512]{2,1,0:T(8,128)(2,1)S(1)}, u32[]{:S(2)}, u32[]{:S(2)}) %collective-permute-start.4) | collective-permute-done | bytes 524320 | tf_op jit(solution)/shard_map/ppermute | solution.py:386
  20.2 5.5 %collective-permute-done.5.refs_1_ = bf16[2,256,512]{2,1,0:T(8,128)(2,1)S(1)} collective-permute-done((bf16[2,256,512]{2,1,0:T(8,128)(2,1)S(1)}, bf16[2,256,512]{2,1,0:T(8,128)(2,1)S(1)}, u32[]{:S(2)}, u32[]{:S(2)}) %collective-permute-start.5) | collective-permute-done | bytes 524320 | tf_op jit(solution)/shard_map/ppermute | solution.py:387
  25.7 0.1 collective-permute-done.6.refs_2_
  25.9 0.2 line_up.1.l0
  26.0 4.1 %collective-permute-start.10 = (bf16[2,1024,512]{2,1,0:T(8,128)(2,1)S(1)}, bf16[2,1024,512]{2,1,0:T(8,128)(2,1)S(1)}, u32[]{:S(2)}, u32[]{:S(2)}) collective-permute-start(bf16[2,1024,512]{2,1,0:T(8,128)(2,1)S(1)} %line_up.1.l0), channel_id=1, source_target_pairs={{0,24},{4,100},{8,0},{12,108},{16,8},{20,116},{24,16},{28,124},{32... | collective-permute-start | bytes 6291464 | tf_op jit(solution)/shard_map/ppermute | solution.py:395
  30.1 0.0 collective-permute-start.13
  30.1 0.0 collective-permute-start.9
  30.2 0.1 pad_maximum_fusion.2
  30.2 0.8 collective-permute-start.12
  31.1 0.1 pad_maximum_fusion.1
  31.1 2.6 %collective-permute-start.11 = (bf16[624,768]{1,0:T(8,128)(2,1)S(1)}, bf16[624,768]{1,0:T(8,128)(2,1)S(1)}, u32[]{:S(2)}, u32[]{:S(2)}) collective-permute-start(bf16[624,768]{1,0:T(8,128)(2,1)S(1)} %pad_maximum_fusion.1), channel_id=1, source_target_pairs={{0,1},{1,2},{2,3},{3,0},{4,5},{5,6},{6,7},{7,4},{8,9},{9,10},{10,1... | collective-permute-start | bytes 2875400 | tf_op jit(solution)/shard_map/ppermute | solution.py:396
  33.7 2.8 %unpack.5.refs_3_ = bf16[8,896,1024]{2,1,0:T(8,128)(2,1)S(1)} custom-call(s32[64]{0:T(128)S(1)} %copy-done.6, s32[64]{0:T(128)S(1)} %copy-done.5, bf16[448,768]{1,0:T(8,128)(2,1)S(1)} %collective-permute-done.7.refs_0_, bf16[448,768]{1,0:T(8,128)(2,1)S(1)} %collective-permute-done.8.refs_1_, ...), custom_call_target="tpu_custom_call", output_to_operand_aliasing={{}: (5, {})} | custom-call | flops 30000001024 | bytes 5505024 | tf_op jit(solution)/shard_map/unpack/pallas_call | solution.py:171
  36.5 18.5 %collective-permute-done.12.refs_1_ = bf16[624,768]{1,0:T(8,128)(2,1)S(1)} collective-permute-done((bf16[624,768]{1,0:T(8,128)(2,1)S(1)}, bf16[624,768]{1,0:T(8,128)(2,1)S(1)}, u32[]{:S(2)}, u32[]{:S(2)}) %collective-permute-start.12) | collective-permute-done | bytes 958496 | tf_op jit(solution)/shard_map/ppermute | solution.py:397
  55.0 0.0 collective-permute-done.11.refs_0_
  55.0 2.4 %collective-permute-done.9.a_ref.l1 = bf16[2,1024,512]{2,1,0:T(8,128)(2,1)S(1)} collective-permute-done((bf16[2,1024,512]{2,1,0:T(8,128)(2,1)S(1)}, bf16[2,1024,512]{2,1,0:T(8,128)(2,1)S(1)}, u32[]{:S(2)}, u32[]{:S(2)}) %collective-permute-start.9) | collective-permute-done | bytes 2097184 | tf_op jit(solution)/shard_map/ppermute | solution.py:394
  57.4 0.2 halves.1
  57.6 0.1 collective-permute-start.14
  57.6 3.2 %collective-permute-start.15 = (bf16[2,512,512]{2,1,0:T(8,128)(2,1)S(1)}, bf16[2,512,512]{2,1,0:T(8,128)(2,1)S(1)}, u32[]{:S(2)}, u32[]{:S(2)}) collective-permute-start(bf16[2,512,512]{2,1,0:T(8,128)(2,1)S(1)} %get-tuple-element.88), channel_id=1, source_target_pairs={{0,24},{4,100},{8,0},{12,108},{16,8},{20,116},{24,16},{28,124},{32... | collective-permute-start | bytes 3145736 | tf_op jit(solution)/shard_map/ppermute | solution.py:407
  60.9 1.7 %collective-permute-start.16 = (bf16[272,768]{1,0:T(8,128)(2,1)S(1)}, bf16[272,768]{1,0:T(8,128)(2,1)S(1)}, u32[]{:S(2)}, u32[]{:S(2)}) collective-permute-start(bf16[272,768]{1,0:T(8,128)(2,1)S(1)} %slice.14), channel_id=1, source_target_pairs={{0,1},{1,2},{2,3},{3,0},{4,5},{5,6},{6,7},{7,4},{8,9},{9,10},{10,1... | collective-permute-start | bytes 1253384 | tf_op jit(solution)/shard_map/ppermute | solution.py:408
  62.6 0.5 collective-permute-start.17
  63.1 3.8 %unpack.6.refs_3_ = bf16[8,896,1024]{2,1,0:T(8,128)(2,1)S(1)} custom-call(s32[64]{0:T(128)S(1)} %copy-done.6, s32[64]{0:T(128)S(1)} %copy-done.5, bf16[624,768]{1,0:T(8,128)(2,1)S(1)} %collective-permute-done.11.refs_0_, bf16[624,768]{1,0:T(8,128)(2,1)S(1)} %collective-permute-done.12.refs_1_, ...), custom_call_target="tpu_custom_call", output_to_operand_aliasing={{}: (5, {})} | custom-call | flops 30000001024 | bytes 5505024 | tf_op jit(solution)/shard_map/unpack/pallas_call | solution.py:171
  66.9 5.5 %collective-permute-done.16.refs_0_ = bf16[272,768]{1,0:T(8,128)(2,1)S(1)} collective-permute-done((bf16[272,768]{1,0:T(8,128)(2,1)S(1)}, bf16[272,768]{1,0:T(8,128)(2,1)S(1)}, u32[]{:S(2)}, u32[]{:S(2)}) %collective-permute-start.16) | collective-permute-done | bytes 417824 | tf_op jit(solution)/shard_map/ppermute | solution.py:408
  72.5 2.5 %collective-permute-done.17.refs_1_ = bf16[272,768]{1,0:T(8,128)(2,1)S(1)} collective-permute-done((bf16[272,768]{1,0:T(8,128)(2,1)S(1)}, bf16[272,768]{1,0:T(8,128)(2,1)S(1)}, u32[]{:S(2)}, u32[]{:S(2)}) %collective-permute-start.17) | collective-permute-done | bytes 417824 | tf_op jit(solution)/shard_map/ppermute | solution.py:409
  74.9 0.1 collective-permute-start.20
  75.0 0.5 collective-permute-start.21
  75.5 2.0 %unpack.7.ups_ref = bf16[8,896,1024]{2,1,0:T(8,128)(2,1)S(1)} custom-call(s32[64]{0:T(128)S(1)} %copy-done.6, s32[64]{0:T(128)S(1)} %copy-done.5, bf16[272,768]{1,0:T(8,128)(2,1)S(1)} %collective-permute-done.16.refs_0_, bf16[272,768]{1,0:T(8,128)(2,1)S(1)} %collective-permute-done.17.refs_1_, ...), custom_call_target="tpu_custom_call", output_to_operand_aliasing={{}: (5, {})} | custom-call | flops 30000001024 | bytes 5505024 | tf_op jit(solution)/shard_map/unpack/pallas_call | solution.py:171
  77.5 0.1 copy-done
  77.6 4.8 %merge.7 = (bf16[224,512]{1,0:T(8,128)(2,1)S(1)}, bf16[224,512]{1,0:T(8,128)(2,1)S(1)}, bf16[224,512]{1,0:T(8,128)(2,1)S(1)}, bf16[224,512]{1,0:T(8,128)(2,1)S(1)}) custom-call(bf16[8,896,1024]{2,1,0:T(8,128)(2,1)S(1)} %unpack.7.ups_ref, bf16[2,1024,512]{2,1,0:T(8,128)(2,1)S(1)} %line_up.1.l0, bf16[2,1024,512]{2,1,0:T(8,128)(2,1)S(1)} %collective-permute-done.9.a_ref.l1, ...), custom_call_target="tpu_custom_call" | custom-call | flops 3758096384 | bytes 1835008 | tf_op jit(solution)/shard_map/merge/pallas_call | solution.py:294
  82.4 0.2 collective-permute-start.31
  82.7 1.9 %collective-permute-start.32 = (bf16[224,512]{1,0:T(8,128)(2,1)S(1)}, bf16[224,512]{1,0:T(8,128)(2,1)S(1)}, u32[]{:S(2)}, u32[]{:S(2)}) collective-permute-start(bf16[224,512]{1,0:T(8,128)(2,1)S(1)} %get-tuple-element.119), channel_id=1, source_target_pairs={{0,1},{1,2},{2,3},{3,0},{4,5},{5,6},{6,7},{7,4},{8,9},{9,10},{10,1... | collective-permute-start | bytes 688136 | tf_op jit(solution)/shard_map/ppermute | solution.py:440
  84.6 0.1 collective-permute-start.33
  84.7 4.8 %merge.6 = (bf16[224,512]{1,0:T(8,128)(2,1)S(1)}, bf16[224,512]{1,0:T(8,128)(2,1)S(1)}, bf16[224,512]{1,0:T(8,128)(2,1)S(1)}, bf16[224,512]{1,0:T(8,128)(2,1)S(1)}) custom-call(bf16[8,896,1024]{2,1,0:T(8,128)(2,1)S(1)} %unpack.7.ups_ref, bf16[2,1024,512]{2,1,0:T(8,128)(2,1)S(1)} %line_up.1.l0, bf16[2,1024,512]{2,1,0:T(8,128)(2,1)S(1)} %collective-permute-done.9.a_ref.l1, ...), custom_call_target="tpu_custom_call" | custom-call | flops 3758096384 | bytes 1835008 | tf_op jit(solution)/shard_map/merge/pallas_call | solution.py:294
  89.5 3.4 %collective-permute-start.28 = (bf16[224,512]{1,0:T(8,128)(2,1)S(1)}, bf16[224,512]{1,0:T(8,128)(2,1)S(1)}, u32[]{:S(2)}, u32[]{:S(2)}) collective-permute-start(bf16[224,512]{1,0:T(8,128)(2,1)S(1)} %get-tuple-element.114), channel_id=1, source_target_pairs={{0,2},{1,3},{2,0},{3,1},{4,6},{5,7},{6,4},{7,5},{8,10},{9,11},{10,... | collective-permute-start | bytes 688136 | tf_op jit(solution)/shard_map/ppermute | solution.py:439
  93.0 0.6 collective-permute-start.29
  93.6 4.8 %merge.5 = (bf16[224,512]{1,0:T(8,128)(2,1)S(1)}, bf16[224,512]{1,0:T(8,128)(2,1)S(1)}, bf16[224,512]{1,0:T(8,128)(2,1)S(1)}, bf16[224,512]{1,0:T(8,128)(2,1)S(1)}) custom-call(bf16[8,896,1024]{2,1,0:T(8,128)(2,1)S(1)} %unpack.7.ups_ref, bf16[2,1024,512]{2,1,0:T(8,128)(2,1)S(1)} %collective-permute-done.13.l0, ...), custom_call_target="tpu_custom_call" | custom-call | flops 3758096384 | bytes 1835008 | tf_op jit(solution)/shard_map/merge/pallas_call | solution.py:294
  98.4 1.5 %collective-permute-start.30 = (bf16[224,512]{1,0:T(8,128)(2,1)S(1)}, bf16[224,512]{1,0:T(8,128)(2,1)S(1)}, u32[]{:S(2)}, u32[]{:S(2)}) collective-permute-start(bf16[224,512]{1,0:T(8,128)(2,1)S(1)} %get-tuple-element.116), channel_id=1, source_target_pairs={{0,3},{1,0},{2,1},{3,2},{4,7},{5,4},{6,5},{7,6},{8,11},{9,8},{10,9... | collective-permute-start | bytes 688136 | tf_op jit(solution)/shard_map/ppermute | solution.py:441
  99.9 0.8 collective-permute-start.25
  100.7 4.8 %merge.4 = (bf16[224,512]{1,0:T(8,128)(2,1)S(1)}, bf16[224,512]{1,0:T(8,128)(2,1)S(1)}, bf16[224,512]{1,0:T(8,128)(2,1)S(1)}, bf16[224,512]{1,0:T(8,128)(2,1)S(1)}) custom-call(bf16[8,896,1024]{2,1,0:T(8,128)(2,1)S(1)} %unpack.7.ups_ref, bf16[2,1024,512]{2,1,0:T(8,128)(2,1)S(1)} %collective-permute-done.13.l0, ...), custom_call_target="tpu_custom_call" | custom-call | flops 3758096384 | bytes 1835008 | tf_op jit(solution)/shard_map/merge/pallas_call | solution.py:294
  105.5 2.6 %collective-permute-start.26 = (bf16[224,512]{1,0:T(8,128)(2,1)S(1)}, bf16[224,512]{1,0:T(8,128)(2,1)S(1)}, u32[]{:S(2)}, u32[]{:S(2)}) collective-permute-start(bf16[224,512]{1,0:T(8,128)(2,1)S(1)} %get-tuple-element.110), channel_id=1, source_target_pairs={{0,1},{1,2},{2,3},{3,0},{4,5},{5,6},{6,7},{7,4},{8,9},{9,10},{10,1... | collective-permute-start | bytes 688136 | tf_op jit(solution)/shard_map/ppermute | solution.py:440
  108.2 2.3 %collective-permute-start.22 = (bf16[224,512]{1,0:T(8,128)(2,1)S(1)}, bf16[224,512]{1,0:T(8,128)(2,1)S(1)}, u32[]{:S(2)}, u32[]{:S(2)}) collective-permute-start(bf16[224,512]{1,0:T(8,128)(2,1)S(1)} %get-tuple-element.105), channel_id=1, source_target_pairs={{0,2},{1,3},{2,0},{3,1},{4,6},{5,7},{6,4},{7,5},{8,10},{9,11},{10,... | collective-permute-start | bytes 688136 | tf_op jit(solution)/shard_map/ppermute | solution.py:439
  110.4 1.0 collective-permute-done.30.refs_2_
  111.4 0.8 collective-permute-start.23
  112.2 1.2 collective-permute-start.24
  113.5 1.6 %place.4.refs_4_ = bf16[224,8192]{1,0:T(8,128)(2,1)} custom-call(bf16[224,512]{1,0:T(8,128)(2,1)S(1)} %collective-permute-done.31.refs_0_, bf16[224,512]{1,0:T(8,128)(2,1)S(1)} %collective-permute-done.32.refs_1_, bf16[224,512]{1,0:T(8,128)(2,1)S(1)} %collective-permute-done.33.refs_2_, bf16[224,512]{1,0:T(8,128)(2,1)S(1)} %get-tuple-element.121.refs_3_), custom_call_target="tpu_custom_call" | custom-call | bytes 1835008 | tf_op jit(solution)/shard_map/place/pallas_call | solution.py:330
  115.0 1.6 %place.5.refs_4_ = bf16[224,8192]{1,0:T(8,128)(2,1)} custom-call(bf16[224,512]{1,0:T(8,128)(2,1)S(1)} %collective-permute-done.28.refs_0_, bf16[224,512]{1,0:T(8,128)(2,1)S(1)} %collective-permute-done.29.refs_1_, bf16[224,512]{1,0:T(8,128)(2,1)S(1)} %collective-permute-done.30.refs_2_, ...), custom_call_target="tpu_custom_call", output_to_operand_aliasing={{}: (4, {})} | custom-call | bytes 1835008 | tf_op jit(solution)/shard_map/place/pallas_call | solution.py:330
  116.6 2.3 %collective-permute-done.26.refs_1_ = bf16[224,512]{1,0:T(8,128)(2,1)S(1)} collective-permute-done((bf16[224,512]{1,0:T(8,128)(2,1)S(1)}, bf16[224,512]{1,0:T(8,128)(2,1)S(1)}, u32[]{:S(2)}, u32[]{:S(2)}) %collective-permute-start.26) | collective-permute-done | bytes 229408 | tf_op jit(solution)/shard_map/ppermute | solution.py:440
  118.9 3.9 %collective-permute-done.27.refs_2_ = bf16[224,512]{1,0:T(8,128)(2,1)S(1)} collective-permute-done((bf16[224,512]{1,0:T(8,128)(2,1)S(1)}, bf16[224,512]{1,0:T(8,128)(2,1)S(1)}, u32[]{:S(2)}, u32[]{:S(2)}) %collective-permute-start.27) | collective-permute-done | bytes 229408 | tf_op jit(solution)/shard_map/ppermute | solution.py:441
  122.8 1.6 %place.6.refs_4_ = bf16[224,8192]{1,0:T(8,128)(2,1)} custom-call(bf16[224,512]{1,0:T(8,128)(2,1)S(1)} %collective-permute-done.25.refs_0_, bf16[224,512]{1,0:T(8,128)(2,1)S(1)} %collective-permute-done.26.refs_1_, bf16[224,512]{1,0:T(8,128)(2,1)S(1)} %collective-permute-done.27.refs_2_, ...), custom_call_target="tpu_custom_call", output_to_operand_aliasing={{}: (4, {})} | custom-call | bytes 1835008 | tf_op jit(solution)/shard_map/place/pallas_call | solution.py:330
  124.4 2.0 %collective-permute-done.24.refs_2_ = bf16[224,512]{1,0:T(8,128)(2,1)S(1)} collective-permute-done((bf16[224,512]{1,0:T(8,128)(2,1)S(1)}, bf16[224,512]{1,0:T(8,128)(2,1)S(1)}, u32[]{:S(2)}, u32[]{:S(2)}) %collective-permute-start.24) | collective-permute-done | bytes 229408 | tf_op jit(solution)/shard_map/ppermute | solution.py:441
  126.4 1.6 %place.7 = bf16[224,8192]{1,0:T(8,128)(2,1)} custom-call(bf16[224,512]{1,0:T(8,128)(2,1)S(1)} %collective-permute-done.22.refs_0_, bf16[224,512]{1,0:T(8,128)(2,1)S(1)} %collective-permute-done.23.refs_1_, bf16[224,512]{1,0:T(8,128)(2,1)S(1)} %collective-permute-done.24.refs_2_, ...), custom_call_target="tpu_custom_call", output_to_operand_aliasing={{}: (4, {})} | custom-call | bytes 1835008 | tf_op jit(solution)/shard_map/place/pallas_call | solution.py:330
  (35 shorter events, 0.2 us)
Async XLA Ops:
  0.0 5.9 %collective-permute-start.3 = (bf16[128,2048]{1,0:T(8,128)(2,1)}, bf16[128,2048]{1,0:T(8,128)(2,1)S(1)}, u32[]{:S(2)}, u32[]{:S(2)}) collective-permute-start(bf16[128,2048]{1,0:T(8,128)(2,1)} %mine_ref.1), channel_id=1, source_target_pairs={{0,4},{4,0},{8,12},{12,8},{16,20},{20,16},{24,28},{28,24},{32,36},... | collective-permute-start | bytes 1572872 | tf_op jit(solution)/shard_map/ppermute | solution.py:371
  2.0 1.5 %copy-start.1 = (bf16[896,1024]{1,0:T(8,128)(2,1)S(1)}, bf16[896,1024]{1,0:T(8,128)(2,1)}, u32[]{:S(2)}) copy-start(bf16[896,1024]{1,0:T(8,128)(2,1)} %refs_0_.1) | copy-start | bytes 5505028
  3.5 2.4 %copy-start.4 = (bf16[128,2048]{1,0:T(8,128)(2,1)S(1)}, bf16[128,2048]{1,0:T(8,128)(2,1)}, u32[]{:S(2)}) copy-start(bf16[128,2048]{1,0:T(8,128)(2,1)} %mine_ref.1) | copy-start | bytes 1572868
  3.5 4.6 %copy-start.2 = (bf16[896,1024]{1,0:T(8,128)(2,1)S(1)}, bf16[896,1024]{1,0:T(8,128)(2,1)}, u32[]{:S(2)}) copy-start(bf16[896,1024]{1,0:T(8,128)(2,1)} %refs_0_.1) | copy-start | bytes 5505028
  3.5 4.6 %copy-start.5 = (s32[64]{0:T(128)S(1)}, s32[64]{0:T(128)}, u32[]{:S(2)}) copy-start(s32[64]{0:T(128)} %samples_ref.7) | copy-start | bytes 772
  3.5 4.6 %copy-start.6 = (s32[64]{0:T(128)S(1)}, s32[64]{0:T(128)}, u32[]{:S(2)}) copy-start(s32[64]{0:T(128)} %ranks_ref.11) | copy-start | bytes 772
  6.0 19.8 %collective-permute-start.7 = (bf16[448,768]{1,0:T(8,128)(2,1)S(1)}, bf16[448,768]{1,0:T(8,128)(2,1)S(1)}, u32[]{:S(2)}, u32[]{:S(2)}) collective-permute-start(bf16[448,768]{1,0:T(8,128)(2,1)S(1)} %get-tuple-element.82), channel_id=1, source_target_pairs={{0,1},{1,2},{2,3},{3,0},{4,5},{5,6},{6,7},{7,4},{8,9},{9,10},{10,1... | collective-permute-start | bytes 2064392 | tf_op jit(solution)/shard_map/ppermute | solution.py:374
  6.2 19.6 %collective-permute-start.8 = (bf16[448,768]{1,0:T(8,128)(2,1)S(1)}, bf16[448,768]{1,0:T(8,128)(2,1)S(1)}, u32[]{:S(2)}, u32[]{:S(2)}) collective-permute-start(bf16[448,768]{1,0:T(8,128)(2,1)S(1)} %get-tuple-element.80), channel_id=1, source_target_pairs={{0,3},{1,0},{2,1},{3,2},{4,7},{5,4},{6,5},{7,6},{8,11},{9,8},{10,9... | collective-permute-start | bytes 2064392 | tf_op jit(solution)/shard_map/ppermute | solution.py:375
  9.3 10.9 %collective-permute-start.4 = (bf16[2,256,512]{2,1,0:T(8,128)(2,1)S(1)}, bf16[2,256,512]{2,1,0:T(8,128)(2,1)S(1)}, u32[]{:S(2)}, u32[]{:S(2)}) collective-permute-start(bf16[2,256,512]{2,1,0:T(8,128)(2,1)S(1)} %pick.1.refs_3_), channel_id=1, source_target_pairs={{0,64},{4,20},{8,72},{12,28},{16,80},{20,4},{24,88},{28,12},{32,96... | collective-permute-start | bytes 1572872 | tf_op jit(solution)/shard_map/ppermute | solution.py:386
  12.4 13.3 %collective-permute-start.5 = (bf16[2,256,512]{2,1,0:T(8,128)(2,1)S(1)}, bf16[2,256,512]{2,1,0:T(8,128)(2,1)S(1)}, u32[]{:S(2)}, u32[]{:S(2)}) collective-permute-start(bf16[2,256,512]{2,1,0:T(8,128)(2,1)S(1)} %pick.1.refs_3_), channel_id=1, source_target_pairs={{0,32},{4,12},{8,40},{12,20},{16,48},{20,28},{24,56},{28,4},{32,64... | collective-permute-start | bytes 1572872 | tf_op jit(solution)/shard_map/ppermute | solution.py:387
  13.0 12.8 %collective-permute-start.6 = (bf16[2,256,512]{2,1,0:T(8,128)(2,1)S(1)}, bf16[2,256,512]{2,1,0:T(8,128)(2,1)S(1)}, u32[]{:S(2)}, u32[]{:S(2)}) collective-permute-start(bf16[2,256,512]{2,1,0:T(8,128)(2,1)S(1)} %pick.1.refs_3_), channel_id=1, source_target_pairs={{0,96},{4,28},{8,104},{12,4},{16,112},{20,12},{24,120},{28,20},{32... | collective-permute-start | bytes 1572872 | tf_op jit(solution)/shard_map/ppermute | solution.py:388
  26.0 29.0 %collective-permute-start.10 = (bf16[2,1024,512]{2,1,0:T(8,128)(2,1)S(1)}, bf16[2,1024,512]{2,1,0:T(8,128)(2,1)S(1)}, u32[]{:S(2)}, u32[]{:S(2)}) collective-permute-start(bf16[2,1024,512]{2,1,0:T(8,128)(2,1)S(1)} %line_up.1.l0), channel_id=1, source_target_pairs={{0,24},{4,100},{8,0},{12,108},{16,8},{20,116},{24,16},{28,124},{32... | collective-permute-start | bytes 6291464 | tf_op jit(solution)/shard_map/ppermute | solution.py:395
  30.1 24.9 %collective-permute-start.13 = (bf16[2,1024,512]{2,1,0:T(8,128)(2,1)S(1)}, bf16[2,1024,512]{2,1,0:T(8,128)(2,1)S(1)}, u32[]{:S(2)}, u32[]{:S(2)}) collective-permute-start(bf16[2,1024,512]{2,1,0:T(8,128)(2,1)S(1)} %line_up.1.l0), channel_id=1, source_target_pairs={{0,4},{4,0},{8,12},{12,8},{16,20},{20,16},{24,28},{28,24},{32,36},... | collective-permute-start | bytes 6291464 | tf_op jit(solution)/shard_map/ppermute | solution.py:398
  30.1 27.2 %collective-permute-start.9 = (bf16[2,1024,512]{2,1,0:T(8,128)(2,1)S(1)}, bf16[2,1024,512]{2,1,0:T(8,128)(2,1)S(1)}, u32[]{:S(2)}, u32[]{:S(2)}) collective-permute-start(bf16[2,1024,512]{2,1,0:T(8,128)(2,1)S(1)} %line_up.1.l0), channel_id=1, source_target_pairs={{0,8},{4,36},{8,16},{12,44},{16,24},{20,52},{24,0},{28,60},{32,40}... | collective-permute-start | bytes 6291464 | tf_op jit(solution)/shard_map/ppermute | solution.py:394
  30.2 24.7 %collective-permute-start.12 = (bf16[624,768]{1,0:T(8,128)(2,1)S(1)}, bf16[624,768]{1,0:T(8,128)(2,1)S(1)}, u32[]{:S(2)}, u32[]{:S(2)}) collective-permute-start(bf16[624,768]{1,0:T(8,128)(2,1)S(1)} %pad_maximum_fusion.2), channel_id=1, source_target_pairs={{0,3},{1,0},{2,1},{3,2},{4,7},{5,4},{6,5},{7,6},{8,11},{9,8},{10,9... | collective-permute-start | bytes 2875400 | tf_op jit(solution)/shard_map/ppermute | solution.py:397
  31.1 23.8 %collective-permute-start.11 = (bf16[624,768]{1,0:T(8,128)(2,1)S(1)}, bf16[624,768]{1,0:T(8,128)(2,1)S(1)}, u32[]{:S(2)}, u32[]{:S(2)}) collective-permute-start(bf16[624,768]{1,0:T(8,128)(2,1)S(1)} %pad_maximum_fusion.1), channel_id=1, source_target_pairs={{0,1},{1,2},{2,3},{3,0},{4,5},{5,6},{6,7},{7,4},{8,9},{9,10},{10,1... | collective-permute-start | bytes 2875400 | tf_op jit(solution)/shard_map/ppermute | solution.py:396
  57.4 17.6 %collective-permute-start.18 = (bf16[2,1024,512]{2,1,0:T(8,128)(2,1)S(1)}, bf16[2,1024,512]{2,1,0:T(8,128)(2,1)S(1)}, u32[]{:S(2)}, u32[]{:S(2)}) collective-permute-start(bf16[2,1024,512]{2,1,0:T(8,128)(2,1)S(1)} %collective-permute-done.9.a_ref.l1), channel_id=1, source_target_pairs={{0,4},{4,0},{8,12},{12,8},{16,20},{20,16},{24,28},{28,24},{32,36},... | collective-permute-start | bytes 6291464 | tf_op jit(solution)/shard_map/ppermute | solution.py:410
  57.6 17.4 %collective-permute-start.14 = (bf16[2,512,512]{2,1,0:T(8,128)(2,1)S(1)}, bf16[2,512,512]{2,1,0:T(8,128)(2,1)S(1)}, u32[]{:S(2)}, u32[]{:S(2)}) collective-permute-start(bf16[2,512,512]{2,1,0:T(8,128)(2,1)S(1)} %get-tuple-element.87), channel_id=1, source_target_pairs={{0,8},{4,36},{8,16},{12,44},{16,24},{20,52},{24,0},{28,60},{32,40}... | collective-permute-start | bytes 3145736 | tf_op jit(solution)/shard_map/ppermute | solution.py:407
  57.6 17.3 %collective-permute-start.15 = (bf16[2,512,512]{2,1,0:T(8,128)(2,1)S(1)}, bf16[2,512,512]{2,1,0:T(8,128)(2,1)S(1)}, u32[]{:S(2)}, u32[]{:S(2)}) collective-permute-start(bf16[2,512,512]{2,1,0:T(8,128)(2,1)S(1)} %get-tuple-element.88), channel_id=1, source_target_pairs={{0,24},{4,100},{8,0},{12,108},{16,8},{20,116},{24,16},{28,124},{32... | collective-permute-start | bytes 3145736 | tf_op jit(solution)/shard_map/ppermute | solution.py:407
  60.9 11.6 %collective-permute-start.16 = (bf16[272,768]{1,0:T(8,128)(2,1)S(1)}, bf16[272,768]{1,0:T(8,128)(2,1)S(1)}, u32[]{:S(2)}, u32[]{:S(2)}) collective-permute-start(bf16[272,768]{1,0:T(8,128)(2,1)S(1)} %slice.14), channel_id=1, source_target_pairs={{0,1},{1,2},{2,3},{3,0},{4,5},{5,6},{6,7},{7,4},{8,9},{9,10},{10,1... | collective-permute-start | bytes 1253384 | tf_op jit(solution)/shard_map/ppermute | solution.py:408
  62.6 12.3 %collective-permute-start.17 = (bf16[272,768]{1,0:T(8,128)(2,1)S(1)}, bf16[272,768]{1,0:T(8,128)(2,1)S(1)}, u32[]{:S(2)}, u32[]{:S(2)}) collective-permute-start(bf16[272,768]{1,0:T(8,128)(2,1)S(1)} %slice.15), channel_id=1, source_target_pairs={{0,3},{1,0},{2,1},{3,2},{4,7},{5,4},{6,5},{7,6},{8,11},{9,8},{10,9... | collective-permute-start | bytes 1253384 | tf_op jit(solution)/shard_map/ppermute | solution.py:409
  72.5 12.1 %collective-permute-start.19 = (bf16[2,1024,512]{2,1,0:T(8,128)(2,1)S(1)}, bf16[2,1024,512]{2,1,0:T(8,128)(2,1)S(1)}, u32[]{:S(2)}, u32[]{:S(2)}) collective-permute-start(bf16[2,1024,512]{2,1,0:T(8,128)(2,1)S(1)} %collective-permute-done.10.b_ref.l2), channel_id=1, source_target_pairs={{0,4},{4,0},{8,12},{12,8},{16,20},{20,16},{24,28},{28,24},{32,36},... | collective-permute-start | bytes 6291464 | tf_op jit(solution)/shard_map/ppermute | solution.py:430
  74.9 9.7 %collective-permute-start.20 = (bf16[2,512,512]{2,1,0:T(8,128)(2,1)S(1)}, bf16[2,512,512]{2,1,0:T(8,128)(2,1)S(1)}, u32[]{:S(2)}, u32[]{:S(2)}) collective-permute-start(bf16[2,512,512]{2,1,0:T(8,128)(2,1)S(1)} %collective-permute-done.14.l3), channel_id=1, source_target_pairs={{0,4},{4,0},{8,12},{12,8},{16,20},{20,16},{24,28},{28,24},{32,36},... | collective-permute-start | bytes 3145736 | tf_op jit(solution)/shard_map/ppermute | solution.py:430
  75.0 9.7 %collective-permute-start.21 = (bf16[2,512,512]{2,1,0:T(8,128)(2,1)S(1)}, bf16[2,512,512]{2,1,0:T(8,128)(2,1)S(1)}, u32[]{:S(2)}, u32[]{:S(2)}) collective-permute-start(bf16[2,512,512]{2,1,0:T(8,128)(2,1)S(1)} %collective-permute-done.15.l4), channel_id=1, source_target_pairs={{0,4},{4,0},{8,12},{12,8},{16,20},{20,16},{24,28},{28,24},{32,36},... | collective-permute-start | bytes 3145736 | tf_op jit(solution)/shard_map/ppermute | solution.py:430
  75.5 2.0 %copy-start = (bf16[896,2048]{1,0:T(8,128)(2,1)S(1)}, bf16[896,2048]{1,0:T(8,128)(2,1)}, u32[]{:S(2)}) copy-start(bf16[896,2048]{1,0:T(8,128)(2,1)} %base_ref.7) | copy-start | bytes 11010052
  82.4 16.0 %collective-permute-start.31 = (bf16[224,512]{1,0:T(8,128)(2,1)S(1)}, bf16[224,512]{1,0:T(8,128)(2,1)S(1)}, u32[]{:S(2)}, u32[]{:S(2)}) collective-permute-start(bf16[224,512]{1,0:T(8,128)(2,1)S(1)} %get-tuple-element.118), channel_id=1, source_target_pairs={{0,2},{1,3},{2,0},{3,1},{4,6},{5,7},{6,4},{7,5},{8,10},{9,11},{10,... | collective-permute-start | bytes 688136 | tf_op jit(solution)/shard_map/ppermute | solution.py:439
  82.7 17.3 %collective-permute-start.32 = (bf16[224,512]{1,0:T(8,128)(2,1)S(1)}, bf16[224,512]{1,0:T(8,128)(2,1)S(1)}, u32[]{:S(2)}, u32[]{:S(2)}) collective-permute-start(bf16[224,512]{1,0:T(8,128)(2,1)S(1)} %get-tuple-element.119), channel_id=1, source_target_pairs={{0,1},{1,2},{2,3},{3,0},{4,5},{5,6},{6,7},{7,4},{8,9},{9,10},{10,1... | collective-permute-start | bytes 688136 | tf_op jit(solution)/shard_map/ppermute | solution.py:440
  84.6 21.0 %collective-permute-start.33 = (bf16[224,512]{1,0:T(8,128)(2,1)S(1)}, bf16[224,512]{1,0:T(8,128)(2,1)S(1)}, u32[]{:S(2)}, u32[]{:S(2)}) collective-permute-start(bf16[224,512]{1,0:T(8,128)(2,1)S(1)} %get-tuple-element.120), channel_id=1, source_target_pairs={{0,3},{1,0},{2,1},{3,2},{4,7},{5,4},{6,5},{7,6},{8,11},{9,8},{10,9... | collective-permute-start | bytes 688136 | tf_op jit(solution)/shard_map/ppermute | solution.py:441
  89.5 18.6 %collective-permute-start.28 = (bf16[224,512]{1,0:T(8,128)(2,1)S(1)}, bf16[224,512]{1,0:T(8,128)(2,1)S(1)}, u32[]{:S(2)}, u32[]{:S(2)}) collective-permute-start(bf16[224,512]{1,0:T(8,128)(2,1)S(1)} %get-tuple-element.114), channel_id=1, source_target_pairs={{0,2},{1,3},{2,0},{3,1},{4,6},{5,7},{6,4},{7,5},{8,10},{9,11},{10,... | collective-permute-start | bytes 688136 | tf_op jit(solution)/shard_map/ppermute | solution.py:439
  93.0 15.2 %collective-permute-start.29 = (bf16[224,512]{1,0:T(8,128)(2,1)S(1)}, bf16[224,512]{1,0:T(8,128)(2,1)S(1)}, u32[]{:S(2)}, u32[]{:S(2)}) collective-permute-start(bf16[224,512]{1,0:T(8,128)(2,1)S(1)} %get-tuple-element.115), channel_id=1, source_target_pairs={{0,1},{1,2},{2,3},{3,0},{4,5},{5,6},{6,7},{7,4},{8,9},{9,10},{10,1... | collective-permute-start | bytes 688136 | tf_op jit(solution)/shard_map/ppermute | solution.py:440
  98.4 13.0 %collective-permute-start.30 = (bf16[224,512]{1,0:T(8,128)(2,1)S(1)}, bf16[224,512]{1,0:T(8,128)(2,1)S(1)}, u32[]{:S(2)}, u32[]{:S(2)}) collective-permute-start(bf16[224,512]{1,0:T(8,128)(2,1)S(1)} %get-tuple-element.116), channel_id=1, source_target_pairs={{0,3},{1,0},{2,1},{3,2},{4,7},{5,4},{6,5},{7,6},{8,11},{9,8},{10,9... | collective-permute-start | bytes 688136 | tf_op jit(solution)/shard_map/ppermute | solution.py:441
  99.9 12.3 %collective-permute-start.25 = (bf16[224,512]{1,0:T(8,128)(2,1)S(1)}, bf16[224,512]{1,0:T(8,128)(2,1)S(1)}, u32[]{:S(2)}, u32[]{:S(2)}) collective-permute-start(bf16[224,512]{1,0:T(8,128)(2,1)S(1)} %get-tuple-element.109), channel_id=1, source_target_pairs={{0,2},{1,3},{2,0},{3,1},{4,6},{5,7},{6,4},{7,5},{8,10},{9,11},{10,... | collective-permute-start | bytes 688136 | tf_op jit(solution)/shard_map/ppermute | solution.py:439
  105.5 13.4 %collective-permute-start.26 = (bf16[224,512]{1,0:T(8,128)(2,1)S(1)}, bf16[224,512]{1,0:T(8,128)(2,1)S(1)}, u32[]{:S(2)}, u32[]{:S(2)}) collective-permute-start(bf16[224,512]{1,0:T(8,128)(2,1)S(1)} %get-tuple-element.110), channel_id=1, source_target_pairs={{0,1},{1,2},{2,3},{3,0},{4,5},{5,6},{6,7},{7,4},{8,9},{9,10},{10,1... | collective-permute-start | bytes 688136 | tf_op jit(solution)/shard_map/ppermute | solution.py:440
  108.2 14.7 %collective-permute-start.27 = (bf16[224,512]{1,0:T(8,128)(2,1)S(1)}, bf16[224,512]{1,0:T(8,128)(2,1)S(1)}, u32[]{:S(2)}, u32[]{:S(2)}) collective-permute-start(bf16[224,512]{1,0:T(8,128)(2,1)S(1)} %get-tuple-element.111), channel_id=1, source_target_pairs={{0,3},{1,0},{2,1},{3,2},{4,7},{5,4},{6,5},{7,6},{8,11},{9,8},{10,9... | collective-permute-start | bytes 688136 | tf_op jit(solution)/shard_map/ppermute | solution.py:441
  108.2 16.2 %collective-permute-start.22 = (bf16[224,512]{1,0:T(8,128)(2,1)S(1)}, bf16[224,512]{1,0:T(8,128)(2,1)S(1)}, u32[]{:S(2)}, u32[]{:S(2)}) collective-permute-start(bf16[224,512]{1,0:T(8,128)(2,1)S(1)} %get-tuple-element.105), channel_id=1, source_target_pairs={{0,2},{1,3},{2,0},{3,1},{4,6},{5,7},{6,4},{7,5},{8,10},{9,11},{10,... | collective-permute-start | bytes 688136 | tf_op jit(solution)/shard_map/ppermute | solution.py:439
  111.4 13.0 %collective-permute-start.23 = (bf16[224,512]{1,0:T(8,128)(2,1)S(1)}, bf16[224,512]{1,0:T(8,128)(2,1)S(1)}, u32[]{:S(2)}, u32[]{:S(2)}) collective-permute-start(bf16[224,512]{1,0:T(8,128)(2,1)S(1)} %get-tuple-element.106), channel_id=1, source_target_pairs={{0,1},{1,2},{2,3},{3,0},{4,5},{5,6},{6,7},{7,4},{8,9},{9,10},{10,1... | collective-permute-start | bytes 688136 | tf_op jit(solution)/shard_map/ppermute | solution.py:440
  112.2 14.1 %collective-permute-start.24 = (bf16[224,512]{1,0:T(8,128)(2,1)S(1)}, bf16[224,512]{1,0:T(8,128)(2,1)S(1)}, u32[]{:S(2)}, u32[]{:S(2)}) collective-permute-start(bf16[224,512]{1,0:T(8,128)(2,1)S(1)} %get-tuple-element.107), channel_id=1, source_target_pairs={{0,3},{1,0},{2,1},{3,2},{4,7},{5,4},{6,5},{7,6},{8,11},{9,8},{10,9... | collective-permute-start | bytes 688136 | tf_op jit(solution)/shard_map/ppermute | solution.py:441

commit v4 on v3

--- a/solution.py
+++ b/solution.py
@@ -314,30 +314,32 @@
     part, width = pieces[0].shape
     theirs, at = chunk
 
-    def block(n):
+    def kernel(*refs):
+        out_ref, sem = refs[-2:]
         core = lax.axis_index("row") % 2
         half = 1 - core if theirs else core
-        return n * (features // 4 // width) + half * (features // 8 // width) + at // width
-
-    def kernel(*refs):
+        copies = []
         for i in range(4):
-
-            @pl.when(near(lax.axis_index("col"), (3, 1, 2, 0)[i]) == pl.program_id(0))
-            def _(i=i):
-                refs[-1][...] = refs[i][...]
+            owner = near(lax.axis_index("col"), (3, 1, 2, 0)[i])
+            start = owner * (features // 4) + half * (features // 8) + at
+            cols = pl.ds(pl.multiple_of(start, width), width)
+            copies.append(pltpu.make_async_copy(refs[i], out_ref.at[:, cols], sem.at[i]))
+            copies[-1].start()
+        for copy in copies:
+            copy.wait()
 
     extra = [] if out is None else [out]
     return pl.pallas_call(
         kernel,
-        grid=(4,),
-        in_specs=[pl.BlockSpec((part, width), lambda n: (0, 0))] * 4 + [pl.BlockSpec(memory_space=pl.ANY)] * len(extra),
-        out_specs=pl.BlockSpec((part, width), lambda n: (0, block(n))),
+        in_specs=[pl.BlockSpec(memory_space=pltpu.VMEM)] * 4 + [pl.BlockSpec(memory_space=pl.ANY)] * len(extra),
+        out_specs=pl.BlockSpec(memory_space=pl.ANY),
         out_shape=jax.ShapeDtypeStruct((part, features), jnp.bfloat16),
+        scratch_shapes=[pltpu.SemaphoreType.DMA((4,))],
         input_output_aliases={4: 0} if extra else {},
         compiler_params=pltpu.CompilerParams(vmem_limit_bytes=VMEM_LIMIT),
         cost_estimate=pl.CostEstimate(flops=0, bytes_accessed=16 * part * width, transcendentals=0),
         name="place",
-    )(*pieces, *extra)
+    )(*[pltpu.with_memory_space_constraint(a, pltpu.VMEM) for a in pieces], *extra)
 
 
 def ring(step):

time: 129 us -> 128 us (level)
  Pallas kernels: 39.3 us -> 36.9 us
  waiting for transfers between devices: 48.4 us -> 50.2 us
    pallas_call x4, Pallas kernels: 6.21 us -> 3.81 us  [place(): pl.pallas_call(kernel, in_specs=[pl.BlockSpec(memory_space=pltpu.VMEM)] *...]
    ppermute x4, waiting for transfers between devices: 2.35 us -> 3.82 us  [shards(): from_left = lax.ppermute(to_right, 'col', ring(1))]
  transfers between devices with their start and end apart: 31 -> 31, of which waited for: 11 -> 12; matrix products, arithmetic and copies ran while one was open for 0% -> 0% of each run, Pallas kernels for 29% -> 28%
where the time goes in v4:
time: 128 us
  waiting for transfers between devices  50.2 us (39%)
  starting transfers between devices  37.4 us (29%)
  Pallas kernels  36.9 us (29%)
  local copies, waits for them, and re-layouts  1.76 us (1%)
    pallas_call x4, Pallas kernels, merge(): pl.pallas_call(kernel, grid=(1,), in_specs=[pl.BlockSpec(memory_space=plt...  19.3 us
    ppermute x1, waiting for transfers between devices, shards(): lax.ppermute(jnp.concatenate([top, right_bottom[:EARLY]]), 'col', ring(3))  18.5 us
    pallas_call x4, Pallas kernels, unpack(): pl.pallas_call(kernel, grid_spec=pltpu.PrefetchScalarGridSpec(num_scalar_...  9.76 us
    ppermute x4, waiting for transfers between devices, shards(): from_right = lax.ppermute(to_left, 'col', ring(3))  7.24 us
    ppermute x4, starting transfers between devices, shards(): from_far = lax.ppermute(to_far, 'col', ring(2))  6.71 us
    ppermute x4, starting transfers between devices, shards(): from_left = lax.ppermute(to_right, 'col', ring(1))  5.95 us
    ppermute x1, waiting for transfers between devices, shards(): late_left = lax.ppermute(left_top[EARLY:], 'col', ring(1))  5.54 us
    ppermute x1, waiting for transfers between devices, shards(): piece_left = lax.ppermute(mine, 'row', torus(1, True))  5.51 us
  transfers between devices with their start and end apart: 31, of which 12 were waited for; matrix products, arithmetic and copies ran while one was open for 0% of the time, Pallas kernels for 28%

profile of v4, /device:TPU:24, one launch (start us, length us, event | category | flops | bytes accessed | tf_op | source)
XLA Modules:
  0.0 127.5 jit_solution(10146710831469509756)
XLA Ops:
  0.0 0.0 collective-permute-start.3
  0.0 1.2 most_live.1
  1.9 0.1 conditional.1
  1.9 0.1 broadcast.2
  2.0 0.0 copy-start.1
  2.0 1.5 %copy-done.1 = bf16[896,1024]{1,0:T(8,128)(2,1)S(1)} copy-done((bf16[896,1024]{1,0:T(8,128)(2,1)S(1)}, bf16[896,1024]{1,0:T(8,128)(2,1)}, u32[]{:S(2)}) %copy-start.1) | copy-done | bytes 1835032
  3.5 2.4 %pack.3 = (bf16[448,768]{1,0:T(8,128)(2,1)S(1)}, bf16[448,768]{1,0:T(8,128)(2,1)S(1)}) custom-call(s32[64]{0:T(128)} %ranks_ref.11, bf16[896,1024]{1,0:T(8,128)(2,1)S(1)} %copy-done.1), custom_call_target="tpu_custom_call" | custom-call | flops 1409286144 | bytes 3670016 | tf_op jit(solution)/shard_map/pack/pallas_call | solution.py:98
  5.9 0.0 collective-permute-done.3.other_ref
  6.0 0.1 pick.1.refs_3_
  6.0 0.2 collective-permute-start.7
  6.2 1.9 %collective-permute-start.8 = (bf16[448,768]{1,0:T(8,128)(2,1)S(1)}, bf16[448,768]{1,0:T(8,128)(2,1)S(1)}, u32[]{:S(2)}, u32[]{:S(2)}) collective-permute-start(bf16[448,768]{1,0:T(8,128)(2,1)S(1)} %get-tuple-element.80), channel_id=1, source_target_pairs={{0,3},{1,0},{2,1},{3,2},{4,7},{5,4},{6,5},{7,6},{8,11},{9,8},{10,9... | collective-permute-start | bytes 2064392 | tf_op jit(solution)/shard_map/ppermute | solution.py:377
  8.1 1.2 unpack.4.refs_3_
  9.3 3.1 %collective-permute-start.4 = (bf16[2,256,512]{2,1,0:T(8,128)(2,1)S(1)}, bf16[2,256,512]{2,1,0:T(8,128)(2,1)S(1)}, u32[]{:S(2)}, u32[]{:S(2)}) collective-permute-start(bf16[2,256,512]{2,1,0:T(8,128)(2,1)S(1)} %pick.1.refs_3_), channel_id=1, source_target_pairs={{0,64},{4,20},{8,72},{12,28},{16,80},{20,4},{24,88},{28,12},{32,96... | collective-permute-start | bytes 1572872 | tf_op jit(solution)/shard_map/ppermute | solution.py:388
  12.4 0.6 collective-permute-start.5
  13.0 2.6 %collective-permute-start.6 = (bf16[2,256,512]{2,1,0:T(8,128)(2,1)S(1)}, bf16[2,256,512]{2,1,0:T(8,128)(2,1)S(1)}, u32[]{:S(2)}, u32[]{:S(2)}) collective-permute-start(bf16[2,256,512]{2,1,0:T(8,128)(2,1)S(1)} %pick.1.refs_3_), channel_id=1, source_target_pairs={{0,96},{4,28},{8,104},{12,4},{16,112},{20,12},{24,120},{28,20},{32... | collective-permute-start | bytes 1572872 | tf_op jit(solution)/shard_map/ppermute | solution.py:390
  15.7 4.5 %collective-permute-done.4.refs_0_ = bf16[2,256,512]{2,1,0:T(8,128)(2,1)S(1)} collective-permute-done((bf16[2,256,512]{2,1,0:T(8,128)(2,1)S(1)}, bf16[2,256,512]{2,1,0:T(8,128)(2,1)S(1)}, u32[]{:S(2)}, u32[]{:S(2)}) %collective-permute-start.4) | collective-permute-done | bytes 524320 | tf_op jit(solution)/shard_map/ppermute | solution.py:388
  20.2 5.5 %collective-permute-done.5.refs_1_ = bf16[2,256,512]{2,1,0:T(8,128)(2,1)S(1)} collective-permute-done((bf16[2,256,512]{2,1,0:T(8,128)(2,1)S(1)}, bf16[2,256,512]{2,1,0:T(8,128)(2,1)S(1)}, u32[]{:S(2)}, u32[]{:S(2)}) %collective-permute-start.5) | collective-permute-done | bytes 524320 | tf_op jit(solution)/shard_map/ppermute | solution.py:389
  25.7 0.1 collective-permute-done.6.refs_2_
  25.9 0.2 line_up.1.l0
  26.0 4.1 %collective-permute-start.10 = (bf16[2,1024,512]{2,1,0:T(8,128)(2,1)S(1)}, bf16[2,1024,512]{2,1,0:T(8,128)(2,1)S(1)}, u32[]{:S(2)}, u32[]{:S(2)}) collective-permute-start(bf16[2,1024,512]{2,1,0:T(8,128)(2,1)S(1)} %line_up.1.l0), channel_id=1, source_target_pairs={{0,24},{4,100},{8,0},{12,108},{16,8},{20,116},{24,16},{28,124},{32... | collective-permute-start | bytes 6291464 | tf_op jit(solution)/shard_map/ppermute | solution.py:397
  30.2 0.1 pad_maximum_fusion.2
  30.2 0.8 collective-permute-start.12
  31.1 0.1 pad_maximum_fusion.1
  31.1 2.6 %collective-permute-start.11 = (bf16[624,768]{1,0:T(8,128)(2,1)S(1)}, bf16[624,768]{1,0:T(8,128)(2,1)S(1)}, u32[]{:S(2)}, u32[]{:S(2)}) collective-permute-start(bf16[624,768]{1,0:T(8,128)(2,1)S(1)} %pad_maximum_fusion.1), channel_id=1, source_target_pairs={{0,1},{1,2},{2,3},{3,0},{4,5},{5,6},{6,7},{7,4},{8,9},{9,10},{10,1... | collective-permute-start | bytes 2875400 | tf_op jit(solution)/shard_map/ppermute | solution.py:398
  33.7 2.8 %unpack.5.refs_3_ = bf16[8,896,1024]{2,1,0:T(8,128)(2,1)S(1)} custom-call(s32[64]{0:T(128)S(1)} %copy-done.6, s32[64]{0:T(128)S(1)} %copy-done.5, bf16[448,768]{1,0:T(8,128)(2,1)S(1)} %collective-permute-done.7.refs_0_, bf16[448,768]{1,0:T(8,128)(2,1)S(1)} %collective-permute-done.8.refs_1_, ...), custom_call_target="tpu_custom_call", output_to_operand_aliasing={{}: (5, {})} | custom-call | flops 30000001024 | bytes 5505024 | tf_op jit(solution)/shard_map/unpack/pallas_call | solution.py:171
  36.5 18.5 %collective-permute-done.12.refs_1_ = bf16[624,768]{1,0:T(8,128)(2,1)S(1)} collective-permute-done((bf16[624,768]{1,0:T(8,128)(2,1)S(1)}, bf16[624,768]{1,0:T(8,128)(2,1)S(1)}, u32[]{:S(2)}, u32[]{:S(2)}) %collective-permute-start.12) | collective-permute-done | bytes 958496 | tf_op jit(solution)/shard_map/ppermute | solution.py:399
  55.0 0.0 collective-permute-done.11.refs_0_
  55.0 2.4 %collective-permute-done.9.a_ref.l1 = bf16[2,1024,512]{2,1,0:T(8,128)(2,1)S(1)} collective-permute-done((bf16[2,1024,512]{2,1,0:T(8,128)(2,1)S(1)}, bf16[2,1024,512]{2,1,0:T(8,128)(2,1)S(1)}, u32[]{:S(2)}, u32[]{:S(2)}) %collective-permute-start.9) | collective-permute-done | bytes 2097184 | tf_op jit(solution)/shard_map/ppermute | solution.py:396
  57.4 0.2 halves.1
  57.6 0.1 collective-permute-start.14
  57.6 3.2 %collective-permute-start.15 = (bf16[2,512,512]{2,1,0:T(8,128)(2,1)S(1)}, bf16[2,512,512]{2,1,0:T(8,128)(2,1)S(1)}, u32[]{:S(2)}, u32[]{:S(2)}) collective-permute-start(bf16[2,512,512]{2,1,0:T(8,128)(2,1)S(1)} %get-tuple-element.88), channel_id=1, source_target_pairs={{0,24},{4,100},{8,0},{12,108},{16,8},{20,116},{24,16},{28,124},{32... | collective-permute-start | bytes 3145736 | tf_op jit(solution)/shard_map/ppermute | solution.py:409
  60.9 1.7 %collective-permute-start.16 = (bf16[272,768]{1,0:T(8,128)(2,1)S(1)}, bf16[272,768]{1,0:T(8,128)(2,1)S(1)}, u32[]{:S(2)}, u32[]{:S(2)}) collective-permute-start(bf16[272,768]{1,0:T(8,128)(2,1)S(1)} %slice.14), channel_id=1, source_target_pairs={{0,1},{1,2},{2,3},{3,0},{4,5},{5,6},{6,7},{7,4},{8,9},{9,10},{10,1... | collective-permute-start | bytes 1253384 | tf_op jit(solution)/shard_map/ppermute | solution.py:410
  62.6 0.5 collective-permute-start.17
  63.1 3.8 %unpack.6.refs_3_ = bf16[8,896,1024]{2,1,0:T(8,128)(2,1)S(1)} custom-call(s32[64]{0:T(128)S(1)} %copy-done.6, s32[64]{0:T(128)S(1)} %copy-done.5, bf16[624,768]{1,0:T(8,128)(2,1)S(1)} %collective-permute-done.11.refs_0_, bf16[624,768]{1,0:T(8,128)(2,1)S(1)} %collective-permute-done.12.refs_1_, ...), custom_call_target="tpu_custom_call", output_to_operand_aliasing={{}: (5, {})} | custom-call | flops 30000001024 | bytes 5505024 | tf_op jit(solution)/shard_map/unpack/pallas_call | solution.py:171
  66.9 5.5 %collective-permute-done.16.refs_0_ = bf16[272,768]{1,0:T(8,128)(2,1)S(1)} collective-permute-done((bf16[272,768]{1,0:T(8,128)(2,1)S(1)}, bf16[272,768]{1,0:T(8,128)(2,1)S(1)}, u32[]{:S(2)}, u32[]{:S(2)}) %collective-permute-start.16) | collective-permute-done | bytes 417824 | tf_op jit(solution)/shard_map/ppermute | solution.py:410
  72.5 2.5 %collective-permute-done.17.refs_1_ = bf16[272,768]{1,0:T(8,128)(2,1)S(1)} collective-permute-done((bf16[272,768]{1,0:T(8,128)(2,1)S(1)}, bf16[272,768]{1,0:T(8,128)(2,1)S(1)}, u32[]{:S(2)}, u32[]{:S(2)}) %collective-permute-start.17) | collective-permute-done | bytes 417824 | tf_op jit(solution)/shard_map/ppermute | solution.py:411
  74.9 0.1 collective-permute-start.20
  75.0 0.5 collective-permute-start.21
  75.5 2.0 %unpack.7.ups_ref = bf16[8,896,1024]{2,1,0:T(8,128)(2,1)S(1)} custom-call(s32[64]{0:T(128)S(1)} %copy-done.6, s32[64]{0:T(128)S(1)} %copy-done.5, bf16[272,768]{1,0:T(8,128)(2,1)S(1)} %collective-permute-done.16.refs_0_, bf16[272,768]{1,0:T(8,128)(2,1)S(1)} %collective-permute-done.17.refs_1_, ...), custom_call_target="tpu_custom_call", output_to_operand_aliasing={{}: (5, {})} | custom-call | flops 30000001024 | bytes 5505024 | tf_op jit(solution)/shard_map/unpack/pallas_call | solution.py:171
  77.5 0.1 copy-done
  77.6 4.8 %merge.7 = (bf16[224,512]{1,0:T(8,128)(2,1)S(1)}, bf16[224,512]{1,0:T(8,128)(2,1)S(1)}, bf16[224,512]{1,0:T(8,128)(2,1)S(1)}, bf16[224,512]{1,0:T(8,128)(2,1)S(1)}) custom-call(bf16[8,896,1024]{2,1,0:T(8,128)(2,1)S(1)} %unpack.7.ups_ref, bf16[2,1024,512]{2,1,0:T(8,128)(2,1)S(1)} %line_up.1.l0, bf16[2,1024,512]{2,1,0:T(8,128)(2,1)S(1)} %collective-permute-done.9.a_ref.l1, ...), custom_call_target="tpu_custom_call" | custom-call | flops 3758096384 | bytes 1835008 | tf_op jit(solution)/shard_map/merge/pallas_call | solution.py:294
  82.4 0.2 collective-permute-start.31
  82.7 1.9 %collective-permute-start.32 = (bf16[224,512]{1,0:T(8,128)(2,1)S(1)}, bf16[224,512]{1,0:T(8,128)(2,1)S(1)}, u32[]{:S(2)}, u32[]{:S(2)}) collective-permute-start(bf16[224,512]{1,0:T(8,128)(2,1)S(1)} %get-tuple-element.119), channel_id=1, source_target_pairs={{0,1},{1,2},{2,3},{3,0},{4,5},{5,6},{6,7},{7,4},{8,9},{9,10},{10,1... | collective-permute-start | bytes 688136 | tf_op jit(solution)/shard_map/ppermute | solution.py:442
  84.6 0.1 collective-permute-start.33
  84.7 4.8 %merge.6 = (bf16[224,512]{1,0:T(8,128)(2,1)S(1)}, bf16[224,512]{1,0:T(8,128)(2,1)S(1)}, bf16[224,512]{1,0:T(8,128)(2,1)S(1)}, bf16[224,512]{1,0:T(8,128)(2,1)S(1)}) custom-call(bf16[8,896,1024]{2,1,0:T(8,128)(2,1)S(1)} %unpack.7.ups_ref, bf16[2,1024,512]{2,1,0:T(8,128)(2,1)S(1)} %line_up.1.l0, bf16[2,1024,512]{2,1,0:T(8,128)(2,1)S(1)} %collective-permute-done.9.a_ref.l1, ...), custom_call_target="tpu_custom_call" | custom-call | flops 3758096384 | bytes 1835008 | tf_op jit(solution)/shard_map/merge/pallas_call | solution.py:294
  89.5 3.4 %collective-permute-start.28 = (bf16[224,512]{1,0:T(8,128)(2,1)S(1)}, bf16[224,512]{1,0:T(8,128)(2,1)S(1)}, u32[]{:S(2)}, u32[]{:S(2)}) collective-permute-start(bf16[224,512]{1,0:T(8,128)(2,1)S(1)} %get-tuple-element.114), channel_id=1, source_target_pairs={{0,2},{1,3},{2,0},{3,1},{4,6},{5,7},{6,4},{7,5},{8,10},{9,11},{10,... | collective-permute-start | bytes 688136 | tf_op jit(solution)/shard_map/ppermute | solution.py:441
  93.0 0.6 collective-permute-start.29
  93.6 4.8 %merge.5 = (bf16[224,512]{1,0:T(8,128)(2,1)S(1)}, bf16[224,512]{1,0:T(8,128)(2,1)S(1)}, bf16[224,512]{1,0:T(8,128)(2,1)S(1)}, bf16[224,512]{1,0:T(8,128)(2,1)S(1)}) custom-call(bf16[8,896,1024]{2,1,0:T(8,128)(2,1)S(1)} %unpack.7.ups_ref, bf16[2,1024,512]{2,1,0:T(8,128)(2,1)S(1)} %collective-permute-done.13.l0, ...), custom_call_target="tpu_custom_call" | custom-call | flops 3758096384 | bytes 1835008 | tf_op jit(solution)/shard_map/merge/pallas_call | solution.py:294
  98.4 1.5 %collective-permute-start.30 = (bf16[224,512]{1,0:T(8,128)(2,1)S(1)}, bf16[224,512]{1,0:T(8,128)(2,1)S(1)}, u32[]{:S(2)}, u32[]{:S(2)}) collective-permute-start(bf16[224,512]{1,0:T(8,128)(2,1)S(1)} %get-tuple-element.116), channel_id=1, source_target_pairs={{0,3},{1,0},{2,1},{3,2},{4,7},{5,4},{6,5},{7,6},{8,11},{9,8},{10,9... | collective-permute-start | bytes 688136 | tf_op jit(solution)/shard_map/ppermute | solution.py:443
  99.9 0.8 collective-permute-start.25
  100.7 4.8 %merge.4 = (bf16[224,512]{1,0:T(8,128)(2,1)S(1)}, bf16[224,512]{1,0:T(8,128)(2,1)S(1)}, bf16[224,512]{1,0:T(8,128)(2,1)S(1)}, bf16[224,512]{1,0:T(8,128)(2,1)S(1)}) custom-call(bf16[8,896,1024]{2,1,0:T(8,128)(2,1)S(1)} %unpack.7.ups_ref, bf16[2,1024,512]{2,1,0:T(8,128)(2,1)S(1)} %collective-permute-done.13.l0, ...), custom_call_target="tpu_custom_call" | custom-call | flops 3758096384 | bytes 1835008 | tf_op jit(solution)/shard_map/merge/pallas_call | solution.py:294
  105.5 2.6 %collective-permute-start.26 = (bf16[224,512]{1,0:T(8,128)(2,1)S(1)}, bf16[224,512]{1,0:T(8,128)(2,1)S(1)}, u32[]{:S(2)}, u32[]{:S(2)}) collective-permute-start(bf16[224,512]{1,0:T(8,128)(2,1)S(1)} %get-tuple-element.110), channel_id=1, source_target_pairs={{0,1},{1,2},{2,3},{3,0},{4,5},{5,6},{6,7},{7,4},{8,9},{9,10},{10,1... | collective-permute-start | bytes 688136 | tf_op jit(solution)/shard_map/ppermute | solution.py:442
  108.2 2.3 %collective-permute-start.22 = (bf16[224,512]{1,0:T(8,128)(2,1)S(1)}, bf16[224,512]{1,0:T(8,128)(2,1)S(1)}, u32[]{:S(2)}, u32[]{:S(2)}) collective-permute-start(bf16[224,512]{1,0:T(8,128)(2,1)S(1)} %get-tuple-element.105), channel_id=1, source_target_pairs={{0,2},{1,3},{2,0},{3,1},{4,6},{5,7},{6,4},{7,5},{8,10},{9,11},{10,... | collective-permute-start | bytes 688136 | tf_op jit(solution)/shard_map/ppermute | solution.py:441
  110.4 1.0 collective-permute-done.30.refs_2_
  111.4 0.8 collective-permute-start.23
  112.2 1.2 collective-permute-start.24
  113.5 0.9 place.4.refs_4_
  114.4 1.0 place.5.refs_4_
  115.4 3.5 %collective-permute-done.26.refs_1_ = bf16[224,512]{1,0:T(8,128)(2,1)S(1)} collective-permute-done((bf16[224,512]{1,0:T(8,128)(2,1)S(1)}, bf16[224,512]{1,0:T(8,128)(2,1)S(1)}, u32[]{:S(2)}, u32[]{:S(2)}) %collective-permute-start.26) | collective-permute-done | bytes 229408 | tf_op jit(solution)/shard_map/ppermute | solution.py:442
  118.9 3.9 %collective-permute-done.27.refs_2_ = bf16[224,512]{1,0:T(8,128)(2,1)S(1)} collective-permute-done((bf16[224,512]{1,0:T(8,128)(2,1)S(1)}, bf16[224,512]{1,0:T(8,128)(2,1)S(1)}, u32[]{:S(2)}, u32[]{:S(2)}) %collective-permute-start.27) | collective-permute-done | bytes 229408 | tf_op jit(solution)/shard_map/ppermute | solution.py:443
  122.8 0.9 place.6.refs_4_
  123.8 0.3 collective-permute-done.23.refs_1_
  124.1 2.3 %collective-permute-done.24.refs_2_ = bf16[224,512]{1,0:T(8,128)(2,1)S(1)} collective-permute-done((bf16[224,512]{1,0:T(8,128)(2,1)S(1)}, bf16[224,512]{1,0:T(8,128)(2,1)S(1)}, u32[]{:S(2)}, u32[]{:S(2)}) %collective-permute-start.24) | collective-permute-done | bytes 229408 | tf_op jit(solution)/shard_map/ppermute | solution.py:443
  126.4 0.9 place.7
  (35 shorter events, 0.2 us)
Async XLA Ops:
  0.0 5.9 %collective-permute-start.3 = (bf16[128,2048]{1,0:T(8,128)(2,1)}, bf16[128,2048]{1,0:T(8,128)(2,1)S(1)}, u32[]{:S(2)}, u32[]{:S(2)}) collective-permute-start(bf16[128,2048]{1,0:T(8,128)(2,1)} %mine_ref.1), channel_id=1, source_target_pairs={{0,4},{4,0},{8,12},{12,8},{16,20},{20,16},{24,28},{28,24},{32,36},... | collective-permute-start | bytes 1572872 | tf_op jit(solution)/shard_map/ppermute | solution.py:373
  2.0 1.5 %copy-start.1 = (bf16[896,1024]{1,0:T(8,128)(2,1)S(1)}, bf16[896,1024]{1,0:T(8,128)(2,1)}, u32[]{:S(2)}) copy-start(bf16[896,1024]{1,0:T(8,128)(2,1)} %refs_0_.1) | copy-start | bytes 5505028
  3.5 2.4 %copy-start.4 = (bf16[128,2048]{1,0:T(8,128)(2,1)S(1)}, bf16[128,2048]{1,0:T(8,128)(2,1)}, u32[]{:S(2)}) copy-start(bf16[128,2048]{1,0:T(8,128)(2,1)} %mine_ref.1) | copy-start | bytes 1572868
  3.5 4.6 %copy-start.2 = (bf16[896,1024]{1,0:T(8,128)(2,1)S(1)}, bf16[896,1024]{1,0:T(8,128)(2,1)}, u32[]{:S(2)}) copy-start(bf16[896,1024]{1,0:T(8,128)(2,1)} %refs_0_.1) | copy-start | bytes 5505028
  3.5 4.6 %copy-start.5 = (s32[64]{0:T(128)S(1)}, s32[64]{0:T(128)}, u32[]{:S(2)}) copy-start(s32[64]{0:T(128)} %samples_ref.7) | copy-start | bytes 772
  3.5 4.6 %copy-start.6 = (s32[64]{0:T(128)S(1)}, s32[64]{0:T(128)}, u32[]{:S(2)}) copy-start(s32[64]{0:T(128)} %ranks_ref.11) | copy-start | bytes 772
  6.0 19.8 %collective-permute-start.7 = (bf16[448,768]{1,0:T(8,128)(2,1)S(1)}, bf16[448,768]{1,0:T(8,128)(2,1)S(1)}, u32[]{:S(2)}, u32[]{:S(2)}) collective-permute-start(bf16[448,768]{1,0:T(8,128)(2,1)S(1)} %get-tuple-element.82), channel_id=1, source_target_pairs={{0,1},{1,2},{2,3},{3,0},{4,5},{5,6},{6,7},{7,4},{8,9},{9,10},{10,1... | collective-permute-start | bytes 2064392 | tf_op jit(solution)/shard_map/ppermute | solution.py:376
  6.2 19.6 %collective-permute-start.8 = (bf16[448,768]{1,0:T(8,128)(2,1)S(1)}, bf16[448,768]{1,0:T(8,128)(2,1)S(1)}, u32[]{:S(2)}, u32[]{:S(2)}) collective-permute-start(bf16[448,768]{1,0:T(8,128)(2,1)S(1)} %get-tuple-element.80), channel_id=1, source_target_pairs={{0,3},{1,0},{2,1},{3,2},{4,7},{5,4},{6,5},{7,6},{8,11},{9,8},{10,9... | collective-permute-start | bytes 2064392 | tf_op jit(solution)/shard_map/ppermute | solution.py:377
  9.3 10.9 %collective-permute-start.4 = (bf16[2,256,512]{2,1,0:T(8,128)(2,1)S(1)}, bf16[2,256,512]{2,1,0:T(8,128)(2,1)S(1)}, u32[]{:S(2)}, u32[]{:S(2)}) collective-permute-start(bf16[2,256,512]{2,1,0:T(8,128)(2,1)S(1)} %pick.1.refs_3_), channel_id=1, source_target_pairs={{0,64},{4,20},{8,72},{12,28},{16,80},{20,4},{24,88},{28,12},{32,96... | collective-permute-start | bytes 1572872 | tf_op jit(solution)/shard_map/ppermute | solution.py:388
  12.4 13.3 %collective-permute-start.5 = (bf16[2,256,512]{2,1,0:T(8,128)(2,1)S(1)}, bf16[2,256,512]{2,1,0:T(8,128)(2,1)S(1)}, u32[]{:S(2)}, u32[]{:S(2)}) collective-permute-start(bf16[2,256,512]{2,1,0:T(8,128)(2,1)S(1)} %pick.1.refs_3_), channel_id=1, source_target_pairs={{0,32},{4,12},{8,40},{12,20},{16,48},{20,28},{24,56},{28,4},{32,64... | collective-permute-start | bytes 1572872 | tf_op jit(solution)/shard_map/ppermute | solution.py:389
  13.0 12.8 %collective-permute-start.6 = (bf16[2,256,512]{2,1,0:T(8,128)(2,1)S(1)}, bf16[2,256,512]{2,1,0:T(8,128)(2,1)S(1)}, u32[]{:S(2)}, u32[]{:S(2)}) collective-permute-start(bf16[2,256,512]{2,1,0:T(8,128)(2,1)S(1)} %pick.1.refs_3_), channel_id=1, source_target_pairs={{0,96},{4,28},{8,104},{12,4},{16,112},{20,12},{24,120},{28,20},{32... | collective-permute-start | bytes 1572872 | tf_op jit(solution)/shard_map/ppermute | solution.py:390
  26.0 29.0 %collective-permute-start.10 = (bf16[2,1024,512]{2,1,0:T(8,128)(2,1)S(1)}, bf16[2,1024,512]{2,1,0:T(8,128)(2,1)S(1)}, u32[]{:S(2)}, u32[]{:S(2)}) collective-permute-start(bf16[2,1024,512]{2,1,0:T(8,128)(2,1)S(1)} %line_up.1.l0), channel_id=1, source_target_pairs={{0,24},{4,100},{8,0},{12,108},{16,8},{20,116},{24,16},{28,124},{32... | collective-permute-start | bytes 6291464 | tf_op jit(solution)/shard_map/ppermute | solution.py:397
  30.1 24.9 %collective-permute-start.13 = (bf16[2,1024,512]{2,1,0:T(8,128)(2,1)S(1)}, bf16[2,1024,512]{2,1,0:T(8,128)(2,1)S(1)}, u32[]{:S(2)}, u32[]{:S(2)}) collective-permute-start(bf16[2,1024,512]{2,1,0:T(8,128)(2,1)S(1)} %line_up.1.l0), channel_id=1, source_target_pairs={{0,4},{4,0},{8,12},{12,8},{16,20},{20,16},{24,28},{28,24},{32,36},... | collective-permute-start | bytes 6291464 | tf_op jit(solution)/shard_map/ppermute | solution.py:400
  30.1 27.2 %collective-permute-start.9 = (bf16[2,1024,512]{2,1,0:T(8,128)(2,1)S(1)}, bf16[2,1024,512]{2,1,0:T(8,128)(2,1)S(1)}, u32[]{:S(2)}, u32[]{:S(2)}) collective-permute-start(bf16[2,1024,512]{2,1,0:T(8,128)(2,1)S(1)} %line_up.1.l0), channel_id=1, source_target_pairs={{0,8},{4,36},{8,16},{12,44},{16,24},{20,52},{24,0},{28,60},{32,40}... | collective-permute-start | bytes 6291464 | tf_op jit(solution)/shard_map/ppermute | solution.py:396
  30.2 24.7 %collective-permute-start.12 = (bf16[624,768]{1,0:T(8,128)(2,1)S(1)}, bf16[624,768]{1,0:T(8,128)(2,1)S(1)}, u32[]{:S(2)}, u32[]{:S(2)}) collective-permute-start(bf16[624,768]{1,0:T(8,128)(2,1)S(1)} %pad_maximum_fusion.2), channel_id=1, source_target_pairs={{0,3},{1,0},{2,1},{3,2},{4,7},{5,4},{6,5},{7,6},{8,11},{9,8},{10,9... | collective-permute-start | bytes 2875400 | tf_op jit(solution)/shard_map/ppermute | solution.py:399
  31.1 23.8 %collective-permute-start.11 = (bf16[624,768]{1,0:T(8,128)(2,1)S(1)}, bf16[624,768]{1,0:T(8,128)(2,1)S(1)}, u32[]{:S(2)}, u32[]{:S(2)}) collective-permute-start(bf16[624,768]{1,0:T(8,128)(2,1)S(1)} %pad_maximum_fusion.1), channel_id=1, source_target_pairs={{0,1},{1,2},{2,3},{3,0},{4,5},{5,6},{6,7},{7,4},{8,9},{9,10},{10,1... | collective-permute-start | bytes 2875400 | tf_op jit(solution)/shard_map/ppermute | solution.py:398
  57.4 17.6 %collective-permute-start.18 = (bf16[2,1024,512]{2,1,0:T(8,128)(2,1)S(1)}, bf16[2,1024,512]{2,1,0:T(8,128)(2,1)S(1)}, u32[]{:S(2)}, u32[]{:S(2)}) collective-permute-start(bf16[2,1024,512]{2,1,0:T(8,128)(2,1)S(1)} %collective-permute-done.9.a_ref.l1), channel_id=1, source_target_pairs={{0,4},{4,0},{8,12},{12,8},{16,20},{20,16},{24,28},{28,24},{32,36},... | collective-permute-start | bytes 6291464 | tf_op jit(solution)/shard_map/ppermute | solution.py:412
  57.6 17.4 %collective-permute-start.14 = (bf16[2,512,512]{2,1,0:T(8,128)(2,1)S(1)}, bf16[2,512,512]{2,1,0:T(8,128)(2,1)S(1)}, u32[]{:S(2)}, u32[]{:S(2)}) collective-permute-start(bf16[2,512,512]{2,1,0:T(8,128)(2,1)S(1)} %get-tuple-element.87), channel_id=1, source_target_pairs={{0,8},{4,36},{8,16},{12,44},{16,24},{20,52},{24,0},{28,60},{32,40}... | collective-permute-start | bytes 3145736 | tf_op jit(solution)/shard_map/ppermute | solution.py:409
  57.6 17.3 %collective-permute-start.15 = (bf16[2,512,512]{2,1,0:T(8,128)(2,1)S(1)}, bf16[2,512,512]{2,1,0:T(8,128)(2,1)S(1)}, u32[]{:S(2)}, u32[]{:S(2)}) collective-permute-start(bf16[2,512,512]{2,1,0:T(8,128)(2,1)S(1)} %get-tuple-element.88), channel_id=1, source_target_pairs={{0,24},{4,100},{8,0},{12,108},{16,8},{20,116},{24,16},{28,124},{32... | collective-permute-start | bytes 3145736 | tf_op jit(solution)/shard_map/ppermute | solution.py:409
  60.9 11.6 %collective-permute-start.16 = (bf16[272,768]{1,0:T(8,128)(2,1)S(1)}, bf16[272,768]{1,0:T(8,128)(2,1)S(1)}, u32[]{:S(2)}, u32[]{:S(2)}) collective-permute-start(bf16[272,768]{1,0:T(8,128)(2,1)S(1)} %slice.14), channel_id=1, source_target_pairs={{0,1},{1,2},{2,3},{3,0},{4,5},{5,6},{6,7},{7,4},{8,9},{9,10},{10,1... | collective-permute-start | bytes 1253384 | tf_op jit(solution)/shard_map/ppermute | solution.py:410
  62.6 12.3 %collective-permute-start.17 = (bf16[272,768]{1,0:T(8,128)(2,1)S(1)}, bf16[272,768]{1,0:T(8,128)(2,1)S(1)}, u32[]{:S(2)}, u32[]{:S(2)}) collective-permute-start(bf16[272,768]{1,0:T(8,128)(2,1)S(1)} %slice.15), channel_id=1, source_target_pairs={{0,3},{1,0},{2,1},{3,2},{4,7},{5,4},{6,5},{7,6},{8,11},{9,8},{10,9... | collective-permute-start | bytes 1253384 | tf_op jit(solution)/shard_map/ppermute | solution.py:411
  72.5 12.1 %collective-permute-start.19 = (bf16[2,1024,512]{2,1,0:T(8,128)(2,1)S(1)}, bf16[2,1024,512]{2,1,0:T(8,128)(2,1)S(1)}, u32[]{:S(2)}, u32[]{:S(2)}) collective-permute-start(bf16[2,1024,512]{2,1,0:T(8,128)(2,1)S(1)} %collective-permute-done.10.b_ref.l2), channel_id=1, source_target_pairs={{0,4},{4,0},{8,12},{12,8},{16,20},{20,16},{24,28},{28,24},{32,36},... | collective-permute-start | bytes 6291464 | tf_op jit(solution)/shard_map/ppermute | solution.py:432
  74.9 9.7 %collective-permute-start.20 = (bf16[2,512,512]{2,1,0:T(8,128)(2,1)S(1)}, bf16[2,512,512]{2,1,0:T(8,128)(2,1)S(1)}, u32[]{:S(2)}, u32[]{:S(2)}) collective-permute-start(bf16[2,512,512]{2,1,0:T(8,128)(2,1)S(1)} %collective-permute-done.14.l3), channel_id=1, source_target_pairs={{0,4},{4,0},{8,12},{12,8},{16,20},{20,16},{24,28},{28,24},{32,36},... | collective-permute-start | bytes 3145736 | tf_op jit(solution)/shard_map/ppermute | solution.py:432
  75.0 9.7 %collective-permute-start.21 = (bf16[2,512,512]{2,1,0:T(8,128)(2,1)S(1)}, bf16[2,512,512]{2,1,0:T(8,128)(2,1)S(1)}, u32[]{:S(2)}, u32[]{:S(2)}) collective-permute-start(bf16[2,512,512]{2,1,0:T(8,128)(2,1)S(1)} %collective-permute-done.15.l4), channel_id=1, source_target_pairs={{0,4},{4,0},{8,12},{12,8},{16,20},{20,16},{24,28},{28,24},{32,36},... | collective-permute-start | bytes 3145736 | tf_op jit(solution)/shard_map/ppermute | solution.py:432
  75.5 2.0 %copy-start = (bf16[896,2048]{1,0:T(8,128)(2,1)S(1)}, bf16[896,2048]{1,0:T(8,128)(2,1)}, u32[]{:S(2)}) copy-start(bf16[896,2048]{1,0:T(8,128)(2,1)} %base_ref.7) | copy-start | bytes 11010052
  82.4 16.0 %collective-permute-start.31 = (bf16[224,512]{1,0:T(8,128)(2,1)S(1)}, bf16[224,512]{1,0:T(8,128)(2,1)S(1)}, u32[]{:S(2)}, u32[]{:S(2)}) collective-permute-start(bf16[224,512]{1,0:T(8,128)(2,1)S(1)} %get-tuple-element.118), channel_id=1, source_target_pairs={{0,2},{1,3},{2,0},{3,1},{4,6},{5,7},{6,4},{7,5},{8,10},{9,11},{10,... | collective-permute-start | bytes 688136 | tf_op jit(solution)/shard_map/ppermute | solution.py:441
  82.7 17.3 %collective-permute-start.32 = (bf16[224,512]{1,0:T(8,128)(2,1)S(1)}, bf16[224,512]{1,0:T(8,128)(2,1)S(1)}, u32[]{:S(2)}, u32[]{:S(2)}) collective-permute-start(bf16[224,512]{1,0:T(8,128)(2,1)S(1)} %get-tuple-element.119), channel_id=1, source_target_pairs={{0,1},{1,2},{2,3},{3,0},{4,5},{5,6},{6,7},{7,4},{8,9},{9,10},{10,1... | collective-permute-start | bytes 688136 | tf_op jit(solution)/shard_map/ppermute | solution.py:442
  84.6 21.0 %collective-permute-start.33 = (bf16[224,512]{1,0:T(8,128)(2,1)S(1)}, bf16[224,512]{1,0:T(8,128)(2,1)S(1)}, u32[]{:S(2)}, u32[]{:S(2)}) collective-permute-start(bf16[224,512]{1,0:T(8,128)(2,1)S(1)} %get-tuple-element.120), channel_id=1, source_target_pairs={{0,3},{1,0},{2,1},{3,2},{4,7},{5,4},{6,5},{7,6},{8,11},{9,8},{10,9... | collective-permute-start | bytes 688136 | tf_op jit(solution)/shard_map/ppermute | solution.py:443
  89.5 18.6 %collective-permute-start.28 = (bf16[224,512]{1,0:T(8,128)(2,1)S(1)}, bf16[224,512]{1,0:T(8,128)(2,1)S(1)}, u32[]{:S(2)}, u32[]{:S(2)}) collective-permute-start(bf16[224,512]{1,0:T(8,128)(2,1)S(1)} %get-tuple-element.114), channel_id=1, source_target_pairs={{0,2},{1,3},{2,0},{3,1},{4,6},{5,7},{6,4},{7,5},{8,10},{9,11},{10,... | collective-permute-start | bytes 688136 | tf_op jit(solution)/shard_map/ppermute | solution.py:441
  93.0 15.2 %collective-permute-start.29 = (bf16[224,512]{1,0:T(8,128)(2,1)S(1)}, bf16[224,512]{1,0:T(8,128)(2,1)S(1)}, u32[]{:S(2)}, u32[]{:S(2)}) collective-permute-start(bf16[224,512]{1,0:T(8,128)(2,1)S(1)} %get-tuple-element.115), channel_id=1, source_target_pairs={{0,1},{1,2},{2,3},{3,0},{4,5},{5,6},{6,7},{7,4},{8,9},{9,10},{10,1... | collective-permute-start | bytes 688136 | tf_op jit(solution)/shard_map/ppermute | solution.py:442
  98.4 13.0 %collective-permute-start.30 = (bf16[224,512]{1,0:T(8,128)(2,1)S(1)}, bf16[224,512]{1,0:T(8,128)(2,1)S(1)}, u32[]{:S(2)}, u32[]{:S(2)}) collective-permute-start(bf16[224,512]{1,0:T(8,128)(2,1)S(1)} %get-tuple-element.116), channel_id=1, source_target_pairs={{0,3},{1,0},{2,1},{3,2},{4,7},{5,4},{6,5},{7,6},{8,11},{9,8},{10,9... | collective-permute-start | bytes 688136 | tf_op jit(solution)/shard_map/ppermute | solution.py:443
  99.9 12.3 %collective-permute-start.25 = (bf16[224,512]{1,0:T(8,128)(2,1)S(1)}, bf16[224,512]{1,0:T(8,128)(2,1)S(1)}, u32[]{:S(2)}, u32[]{:S(2)}) collective-permute-start(bf16[224,512]{1,0:T(8,128)(2,1)S(1)} %get-tuple-element.109), channel_id=1, source_target_pairs={{0,2},{1,3},{2,0},{3,1},{4,6},{5,7},{6,4},{7,5},{8,10},{9,11},{10,... | collective-permute-start | bytes 688136 | tf_op jit(solution)/shard_map/ppermute | solution.py:441
  105.5 13.4 %collective-permute-start.26 = (bf16[224,512]{1,0:T(8,128)(2,1)S(1)}, bf16[224,512]{1,0:T(8,128)(2,1)S(1)}, u32[]{:S(2)}, u32[]{:S(2)}) collective-permute-start(bf16[224,512]{1,0:T(8,128)(2,1)S(1)} %get-tuple-element.110), channel_id=1, source_target_pairs={{0,1},{1,2},{2,3},{3,0},{4,5},{5,6},{6,7},{7,4},{8,9},{9,10},{10,1... | collective-permute-start | bytes 688136 | tf_op jit(solution)/shard_map/ppermute | solution.py:442
  108.2 14.7 %collective-permute-start.27 = (bf16[224,512]{1,0:T(8,128)(2,1)S(1)}, bf16[224,512]{1,0:T(8,128)(2,1)S(1)}, u32[]{:S(2)}, u32[]{:S(2)}) collective-permute-start(bf16[224,512]{1,0:T(8,128)(2,1)S(1)} %get-tuple-element.111), channel_id=1, source_target_pairs={{0,3},{1,0},{2,1},{3,2},{4,7},{5,4},{6,5},{7,6},{8,11},{9,8},{10,9... | collective-permute-start | bytes 688136 | tf_op jit(solution)/shard_map/ppermute | solution.py:443
  108.2 15.6 %collective-permute-start.22 = (bf16[224,512]{1,0:T(8,128)(2,1)S(1)}, bf16[224,512]{1,0:T(8,128)(2,1)S(1)}, u32[]{:S(2)}, u32[]{:S(2)}) collective-permute-start(bf16[224,512]{1,0:T(8,128)(2,1)S(1)} %get-tuple-element.105), channel_id=1, source_target_pairs={{0,2},{1,3},{2,0},{3,1},{4,6},{5,7},{6,4},{7,5},{8,10},{9,11},{10,... | collective-permute-start | bytes 688136 | tf_op jit(solution)/shard_map/ppermute | solution.py:441
  111.4 12.7 %collective-permute-start.23 = (bf16[224,512]{1,0:T(8,128)(2,1)S(1)}, bf16[224,512]{1,0:T(8,128)(2,1)S(1)}, u32[]{:S(2)}, u32[]{:S(2)}) collective-permute-start(bf16[224,512]{1,0:T(8,128)(2,1)S(1)} %get-tuple-element.106), channel_id=1, source_target_pairs={{0,1},{1,2},{2,3},{3,0},{4,5},{5,6},{6,7},{7,4},{8,9},{9,10},{10,1... | collective-permute-start | bytes 688136 | tf_op jit(solution)/shard_map/ppermute | solution.py:442
  112.2 14.1 %collective-permute-start.24 = (bf16[224,512]{1,0:T(8,128)(2,1)S(1)}, bf16[224,512]{1,0:T(8,128)(2,1)S(1)}, u32[]{:S(2)}, u32[]{:S(2)}) collective-permute-start(bf16[224,512]{1,0:T(8,128)(2,1)S(1)} %get-tuple-element.107), channel_id=1, source_target_pairs={{0,3},{1,0},{2,1},{3,2},{4,7},{5,4},{6,5},{7,6},{8,11},{9,8},{10,9... | collective-permute-start | bytes 688136 | tf_op jit(solution)/shard_map/ppermute | solution.py:443
